TPU v7x, 128 devices: a whole 4x4x4 slice. The times are simulated.
128 devices in a mesh: comp: 2 (over z_hi), gx: 32 (over y, x, z_lo), gy: 2 (over core).
Axes of the slice: x: 4, y: 4, z: 4 (z_hi: 2, z_lo: 2; z = z_hi * 2 + z_lo), core: 2. Of those that a mesh axis runs over, the one named last changes fastest.
Arguments:
- layered_heat_profile: float32 [2, 8, 8192, 256], P('comp', None, 'gx', 'gy'), may hold values from -6 to 6
- prior_marine_heat: float32 [8192, 256], P('gx', 'gy'), may hold values from -6 to 6
- transfer_factor_table: float32 [8, 8192, 256], P(None, 'gx', 'gy'), may hold values from 0.1 to 1
- depth_fraction_matrix: float32 [8, 8], replicated, may hold values from -2 to 2
- adjacent_cell_table: int32 [6, 8192, 256], P(None, 'gx', 'gy'), may hold values from 0 to 33539, as said below
- destination_water_peer: int32 [16384, 2], P(('gx', 'gy')), may hold values from 0 to 63, all different within a row; in each aligned block of 256 rows (0 to 255, 256 to 511, ...) at most 18 rows name the same one
- destination_water_line: int32 [16384, 2], P(('gx', 'gy')), may hold values from 0 to 255
- interpolation_matrix_blocks: bfloat16 [16384, 2, 128, 128], P(('gx', 'gy')), may hold values from -0.5 to 0.5
Outputs:
- state_out: float32 [2, 8, 8192, 256], P('comp', None, 'gx', 'gy')
- boundary_coupled_pair: float32 [2, 8192, 256], P('comp', 'gx', 'gy')
Inputs may be any that keep to these rules, and one draw needn't show every extreme that they name: `destination_water_peer`: each row names 2 different ocean ranks; among the rows of one device no rank is named by more than 18 routes, and exactly 18 for some rank. `adjacent_cell_table`: each entry indexes a device's block of 256 x 128 cells extended by one cell on every side, flattened row by row; a cell's entries are its six hexagonal neighbours in offset rows, except land neighbours, which are the cell's own index.
All inputs are finite; a program needn't handle non-finite values.
Results may differ from a plain program's by a relative error of at most 0.0054.
Values may be sent and summed in bfloat16 or wider, within the bound.
No kernel may reach another device: no remote copies, remote signals or barrier semaphores. Data moves between devices by JAX's collectives and lax.ppermute only.
A program may use at most 320 MiB of HBM per device.

v0:
```python
import jax
import jax.numpy as jnp
import numpy as np
from jax import lax
from jax.sharding import PartitionSpec as P

ATMOS_DIFFUSION = 0.01
MIXING = 0.2
OCEAN_DIFFUSION = 0.12


def shortened(shard):
    return jax.tree.map(lambda a: a.astype(jnp.bfloat16) if a.dtype == jnp.float32 else a, shard)


def from_behind(block, axis, distance):
    devices = range(lax.axis_size(axis))
    route = [(i - distance, i) for i in devices if i - distance in devices]
    return lax.ppermute(block, axis, route)


def extended_2(shard, sides, width):
    for axis, dim in sides:
        size, length = (lax.axis_size(axis), shard.shape[dim])
        up = [(i, (i + 1) % size) for i in range(size)]
        down = [(j, i) for i, j in up]
        last = lax.slice_in_dim(shard, length - width, length, axis=dim)
        leading = lax.slice_in_dim(shard, 0, width, axis=dim)
        before = lax.ppermute(last, axis, up)
        after = lax.ppermute(leading, axis, down)
        shard = jnp.concatenate([before, shard, after], axis=dim)
    return shard


def second_table():
    gll_nodes = np.array([-1.0, -1.0 / np.sqrt(5.0), 1.0 / np.sqrt(5.0), 1.0])
    poly_order = 3
    legendre = (5.0 * gll_nodes**3 - 3.0 * gll_nodes) / 2.0
    derivative = np.zeros((4, 4))
    for row_index in range(4):
        for col_index in range(4):
            if row_index != col_index:
                derivative[row_index, col_index] = legendre[row_index] / (
                    legendre[col_index] * (gll_nodes[row_index] - gll_nodes[col_index])
                )
    derivative[0, 0] = -poly_order * (poly_order + 1) / 4.0
    derivative[3, 3] = poly_order * (poly_order + 1) / 4.0
    return derivative @ derivative


def vertical(field):
    padded = jnp.concatenate([field[:1], field, field[-1:]], axis=0)
    return padded[2:] + padded[:-2] - 2.0 * field


def atmos_local(field):
    levels, extent_x, extent_y = field.shape
    matrix_x = jnp.asarray(np.kron(np.eye(extent_x // 4), second_table()), jnp.float32)
    matrix_y = jnp.asarray(np.kron(np.eye(extent_y // 4), second_table()), jnp.float32)
    along_x = jnp.einsum("ij,ljy->liy", matrix_x, field, precision=lax.Precision.HIGHEST)
    along_y = jnp.einsum("lxj,ij->lxi", field, matrix_y, precision=lax.Precision.HIGHEST)
    return field + ATMOS_DIFFUSION * (along_x + along_y) + MIXING * vertical(field)


def assemble(extended):
    extent_x = extended.shape[1] - 2
    extent_y = extended.shape[2] - 2
    phase_x = (jnp.arange(extent_x) % 4)[None, :, None]
    centre = extended[:, 1:-1, :]
    half_x = jnp.where(
        phase_x == 3,
        0.5 * (centre + extended[:, 2:, :]),
        jnp.where(phase_x == 0, 0.5 * (centre + extended[:, :-2, :]), centre),
    )
    phase_y = (jnp.arange(extent_y) % 4)[None, None, :]
    middle = half_x[:, :, 1:-1]
    return jnp.where(
        phase_y == 3,
        0.5 * (middle + half_x[:, :, 2:]),
        jnp.where(phase_y == 0, 0.5 * (middle + half_x[:, :, :-2]), middle),
    )


def local(
    layered_heat_profile,
    prior_marine_heat,
    transfer_factor_table,
    depth_fraction_matrix,
    adjacent_cell_table,
    destination_water_peer,
    destination_water_line,
    interpolation_matrix_blocks,
):
    is_atmosphere_side = lax.axis_index("comp") == 0
    rank_count = lax.axis_size("gx") * lax.axis_size("gy")
    owned_grid_block = layered_heat_profile[0]
    levels, row_count, col_count = owned_grid_block.shape
    channels = transfer_factor_table.shape[0]
    fanout = destination_water_peer.shape[1]
    item_count = row_count * fanout
    capacity = 2 * fanout * row_count // rank_count + 2
    slot_count = rank_count * capacity

    def send_flux():
        boundary_transport_quantity = (
            transfer_factor_table * (owned_grid_block[0] - prior_marine_heat)[None]
        ).astype(jnp.bfloat16)
        partials = jnp.einsum(
            "fbp,bkpq->bkfq",
            boundary_transport_quantity,
            interpolation_matrix_blocks,
            preferred_element_type=jnp.float32,
        ).astype(jnp.bfloat16)
        peer_ranks = destination_water_peer.reshape(-1)
        owner_hits = (peer_ranks[:, None] == jnp.arange(rank_count)[None, :]).astype(jnp.int32)
        before = jnp.cumsum(owner_hits, axis=0) - owner_hits
        slot_index = jnp.sum(before * owner_hits, axis=1)
        position = peer_ranks * capacity + slot_index
        place_int = (position[:, None] == jnp.arange(slot_count)[None, :]).astype(jnp.int32)
        placement_map = place_int.astype(jnp.bfloat16)
        packed = jnp.einsum(
            "is,iz->sz",
            placement_map,
            partials.reshape(item_count, channels * col_count),
            preferred_element_type=jnp.float32,
        ).astype(jnp.bfloat16)
        labels = (
            jnp.einsum("is,i->s", place_int, destination_water_line.reshape(-1) - row_count)
            + row_count
        )
        return (
            packed.reshape(rank_count, capacity, channels, col_count),
            labels.reshape(rank_count, capacity),
            placement_map,
        )

    def no_flux():
        return (
            jnp.zeros((rank_count, capacity, channels, col_count), jnp.bfloat16),
            jnp.full((rank_count, capacity), row_count, jnp.int32),
            jnp.zeros((item_count, slot_count), jnp.bfloat16),
        )

    packed, labels, placement_map = lax.cond(is_atmosphere_side, send_flux, no_flux)
    sectioned = (
        lax.all_to_all(packed, ("gx", "gy"), split_axis=0, concat_axis=0, tiled=True),
        lax.all_to_all(labels, ("gx", "gy"), split_axis=0, concat_axis=0, tiled=True),
    )
    received, received_ids = from_behind((sectioned[0], shortened(sectioned[1])), "comp", 1)
    matches = (received_ids.reshape(-1)[:, None] == jnp.arange(row_count)[None, :]).astype(
        jnp.bfloat16
    )

    def ocean_flux():
        return jnp.einsum(
            "sr,sfq->frq",
            matches,
            received.reshape(slot_count, channels, col_count),
            preferred_element_type=jnp.float32,
        )

    boundary_driving_term = lax.cond(
        is_atmosphere_side,
        lambda: jnp.zeros((channels, row_count, col_count), jnp.float32),
        ocean_flux,
    )

    def ocean_step(extended):
        centre = extended[:, 1:-1, 1:-1]
        flat = extended.reshape(levels, -1)
        near_values = jnp.take(flat, adjacent_cell_table.reshape(-1), axis=1).reshape(
            levels, adjacent_cell_table.shape[0], row_count, col_count
        )
        spread = jnp.sum(near_values - centre[:, None], axis=1)
        forcing_push = jnp.einsum(
            "lf,fxy->lxy",
            depth_fraction_matrix,
            boundary_driving_term,
            precision=lax.Precision.HIGHEST,
        )
        return centre + OCEAN_DIFFUSION * spread + MIXING * vertical(centre) + forcing_push

    current = owned_grid_block
    for substep in range(2):
        prepared = lax.cond(is_atmosphere_side, atmos_local, lambda grid: grid, current)
        extended = extended_2(prepared, (("gx", 1), ("gy", 2)), 1)
        if substep == 0:
            current = lax.cond(is_atmosphere_side, assemble, ocean_step, extended)
        else:
            current = lax.cond(
                is_atmosphere_side, assemble, lambda grid: grid[:, 1:-1, 1:-1], extended
            )

    def ocean_send():
        surface_top = current[0].astype(jnp.bfloat16)
        picked = jnp.dot(matches, surface_top, preferred_element_type=jnp.float32).astype(
            jnp.bfloat16
        )
        return picked.reshape(rank_count, capacity, col_count)

    outgoing = lax.cond(
        is_atmosphere_side,
        lambda: jnp.zeros((rank_count, capacity, col_count), jnp.bfloat16),
        ocean_send,
    )
    crossed = from_behind(outgoing, "comp", -1)
    arrived = lax.all_to_all(crossed, ("gx", "gy"), split_axis=0, concat_axis=0, tiled=True)

    def atmosphere_sea_temp():
        values = jnp.dot(
            placement_map,
            arrived.reshape(slot_count, col_count),
            preferred_element_type=jnp.float32,
        ).astype(jnp.bfloat16)
        return jnp.einsum(
            "bkpq,bkq->bp",
            interpolation_matrix_blocks,
            values.reshape(row_count, fanout, col_count),
            preferred_element_type=jnp.float32,
        )

    boundary_coupled_pair = lax.cond(
        is_atmosphere_side, atmosphere_sea_temp, lambda: boundary_driving_term[0]
    )
    return (current[None], boundary_coupled_pair[None])


def solution(mesh):
    return jax.shard_map(
        local,
        mesh=mesh,
        in_specs=(
            P("comp", None, "gx", "gy"),
            P("gx", "gy"),
            P(None, "gx", "gy"),
            P(),
            P(None, "gx", "gy"),
            P(("gx", "gy"), None),
            P(("gx", "gy"), None),
            P(("gx", "gy"), None, None, None),
        ),
        out_specs=(P("comp", None, "gx", "gy"), P("comp", "gx", "gy")),
        check_vma=False,
    )
```

profile of v0, /device:TPU:1, one launch (start us, length us, event | category | flops | bytes accessed | tf_op | source)
XLA Modules:
  0.0 962.6 jit_solution(9188093261082276390)
XLA Ops:
  0.6 18.9 %conditional.9 = (bf16[64,18,8,128]{3,2,1,0:T(8,128)(2,1)S(1)}, s32[64,18]{1,0:T(8,128)}, bf16[512,1152]{1,0:T(8,128)(2,1)}) conditional(s32[]{:T(128)} %convert_element_type.48, () %tuple.71, (s32[256,2]{0,1:T(2,128)}, f32[8,256,128]{2,1,0:T(8,128)}, f32[256,128]{1,0:T(8,128)}, f32[8,256,128]{2,1,0:T(8,128)}, bf16[256,2,128,128]{3,2,1,0:T(8,128)(2,1)}, ...), branch_computations={%region_2.3_spmd, %region_3.7_spmd} | conditional | flops 1352404096 | bytes 35209076 | solution.py:144
  5.8 8.2 convolution_convert_fusion.3
  14.0 2.7 fusion.44
  19.5 42.4 %all_to_all.22 = bf16[64,18,8,128]{3,2,1,0:T(8,128)(2,1)} all-to-all(bf16[64,18,8,128]{3,2,1,0:T(8,128)(2,1)S(1)} %get-tuple-element.111), channel_id=1, replica_groups=mesh['comp'=2,'gx'=32,'gy'=2] {'gx','gy'}, dimensions={0} | all-to-all | bytes 4718592 | tf_op jit(solution)/shard_map/all_to_all | solution.py:146
  61.9 2.7 collective-permute-start.4
  64.6 4.8 all-to-all-start.1
  69.5 4.6 conditional.8
  77.2 4.6 collective-permute-start.1
  81.9 45.3 %all-to-all-done.1 = s32[64,1,18]{2,1,0:T(1,128)S(1)} async-done(((s32[64,1,18]{2,1,0:T(1,128)}), s32[64,1,18]{2,1,0:T(1,128)S(1)}, u32[]{:S(2)}, u32[]{:S(2)}) %all-to-all-start.1) | async-done | bytes 4640 | tf_op jit(solution)/shard_map/all_to_all | solution.py:147
  128.5 8.0 collective-permute-done
  143.7 6.0 conditional.11
  145.1 2.5 copy.105
  149.8 4.1 conditional.12
  156.2 4.3 collective-permute-start.7
  160.6 18.1 %collective-permute-done.6 = f32[8,1,128]{1,0,2:T(8,128)S(1)} collective-permute-done((f32[8,1,128]{1,0,2:T(8,128)S(1)}, f32[8,1,128]{1,0,2:T(8,128)S(1)}, u32[]{:S(2)}, u32[]{:S(2)}) %collective-permute-start.6) | collective-permute-done | bytes 4128 | tf_op jit(solution)/shard_map/ppermute | solution.py:29
  183.7 14.0 %conditional.13 = (f32[8,256,128]{2,1,0:T(8,128)}) conditional(s32[]{:T(128)} %convert_element_type.48, (f32[8,256,128]{1,2,0:T(8,128)S(1)}) %tuple.132, f32[8,258,130]{1,0,2:T(8,128)S(1)} %pad_maximum_fusion.7), branch_computations={%region_14.15_spmd, %region_15.16_spmd} | conditional | flops 3173376 | bytes 21235208 | solution.py:190
  187.8 2.8 copy.110
  190.6 2.8 copy.111
  193.3 2.8 select_select_fusion
  199.2 734.3 %collective-permute-done.10 = bf16[64,18,128]{2,1,0:T(8,128)(2,1)} collective-permute-done((bf16[64,18,128]{2,1,0:T(8,128)(2,1)S(1)}, bf16[64,18,128]{2,1,0:T(8,128)(2,1)}, u32[]{:S(2)}, u32[]{:S(2)}) %collective-permute-start.10) | collective-permute-done | bytes 294944 | tf_op jit(solution)/shard_map/ppermute | solution.py:19
  933.5 5.0 all-to-all-start.2
  938.6 10.8 %all-to-all-done.2 = bf16[64,18,128]{2,1,0:T(8,128)(2,1)S(1)} async-done(((bf16[64,18,128]{2,1,0:T(8,128)(2,1)}), bf16[64,18,128]{2,1,0:T(8,128)(2,1)S(1)}, u32[]{:S(2)}, u32[]{:S(2)}) %all-to-all-start.2) | async-done | bytes 294944 | tf_op jit(solution)/shard_map/all_to_all | solution.py:207
  949.4 12.3 %conditional.15 = (f32[1,256,128]{2,1,0:T(8,128)S(1)}) conditional(s32[]{:T(128)} %convert_element_type.48, (f32[8,256,128]{1,2,0:T(8,128)S(1)}) %tuple.133, (bf16[64,18,128]{2,1,0:T(8,128)(2,1)S(1)}, bf16[512,1152]{1,0:T(8,128)(2,1)}, bf16[256,2,128,128]{3,2,1,0:T(8,128)(2,1)}) %tuple.79), branch_computations={%region_18.19_spmd, %region_19.20_spmd} | conditional | flops 167837696 | bytes 19234824 | solution.py:222
  951.5 10.2 %fusion.36 = f32[256,1,128,1]{2,1,3,0:T(1,128)S(1)} fusion(bf16[256,2,128,128]{3,2,1,0:T(8,128)(2,1)} %get-tuple-element.105, bf16[256,2,128,1]{2,1,0,3:T(2,128)(2,1)S(1)} %bitcast.100), kind=kOutput, calls=%fused_computation.64 | convolution fusion | flops 16777216 | bytes 17039360 | tf_op jit(solution)/shard_map/cond/branch_1_fun/bkpq,bkq->bp/dot_general | solution.py:215
  (102 shorter events, 47.7 us)
Async XLA Ops:
  0.7 4.2 copy-start.14
  0.7 5.1 copy-start.11
  19.5 50.0 %copy-start = (f32[1,8,256,128]{3,2,1,0:T(8,128)S(1)}, f32[1,8,256,128]{3,2,1,0:T(8,128)}, u32[]{:S(2)}) copy-start(f32[1,8,256,128]{3,2,1,0:T(8,128)} %param.26) | copy-start | bytes 3145732
  19.5 50.0 %copy-start.16 = (f32[128,128]{1,0:T(8,128)S(1)}, f32[128,128]{1,0:T(8,128)}, u32[]{:S(2)}) copy-start(f32[128,128]{1,0:T(8,128)} %constant.129.clone) | copy-start | bytes 196612
  61.9 80.0 %collective-permute-start.4 = (bf16[64,18,8,128]{3,2,1,0:T(8,128)(2,1)}, bf16[64,18,8,128]{3,2,1,0:T(8,128)(2,1)}, u32[]{:S(2)}, u32[]{:S(2)}) collective-permute-start(bf16[64,18,8,128]{3,2,1,0:T(8,128)(2,1)} %all_to_all.22), channel_id=1, source_target_pairs={{0,64},{1,65},{2,66},{3,67},{4,68},{5,69},{6,70},{7,71},{8,72},{9,... | collective-permute-start | bytes 7077896 | tf_op jit(solution)/shard_map/ppermute | solution.py:19
  64.6 62.5 %all-to-all-start.1 = ((s32[64,1,18]{2,1,0:T(1,128)}), s32[64,1,18]{2,1,0:T(1,128)S(1)}, u32[]{:S(2)}, u32[]{:S(2)}) async-start(s32[64,1,18]{2,1,0:T(1,128)} %bitcast.26), calls=%async_computation.1 | async-start | bytes 65536 | tf_op jit(solution)/shard_map/all_to_all | solution.py:147
  75.9 60.6 %collective-permute-start = (f32[8,1,128]{1,0,2:T(8,128)}, f32[8,1,128]{1,0,2:T(8,128)S(1)}, u32[]{:S(2)}, u32[]{:S(2)}) collective-permute-start(f32[8,1,128]{1,0,2:T(8,128)} %get-tuple-element.208), channel_id=1, source_target_pairs={{0,2},{2,4},{4,6},{6,8},{8,10},{10,12},{12,14},{14,16},{16,18},{18... | collective-permute-start | bytes 12296 | tf_op jit(solution)/shard_map/ppermute | solution.py:29
  77.2 60.3 %collective-permute-start.1 = (f32[8,1,128]{1,0,2:T(8,128)}, f32[8,1,128]{1,0,2:T(8,128)S(1)}, u32[]{:S(2)}, u32[]{:S(2)}) collective-permute-start(f32[8,1,128]{1,0,2:T(8,128)} %get-tuple-element.209), channel_id=1, source_target_pairs={{2,0},{4,2},{6,4},{8,6},{10,8},{12,10},{14,12},{16,14},{18,16},{20... | collective-permute-start | bytes 12296 | tf_op jit(solution)/shard_map/ppermute | solution.py:30
  127.2 11.9 %collective-permute-start.5 = (s32[64,18]{1,0:T(8,128)S(1)}, s32[64,18]{1,0:T(8,128)S(1)}, u32[]{:S(2)}, u32[]{:S(2)}) collective-permute-start(s32[64,18]{1,0:T(8,128)S(1)} %bitcast.102), channel_id=1, source_target_pairs={{0,64},{1,65},{2,66},{3,67},{4,68},{5,69},{6,70},{7,71},{8,72},{9,... | collective-permute-start | bytes 13832 | tf_op jit(solution)/shard_map/ppermute | solution.py:19
  137.6 2.2 collective-permute-start.2
  139.0 1.2 collective-permute-start.3
  139.4 2.5 copy-start.7
  141.9 1.8 copy-start.1
  141.9 1.8 copy-start.18
  143.7 6.0 copy-start.12
  154.9 28.2 %copy-start.4 = (f32[8,256,128]{1,2,0:T(8,128)S(1)}, f32[8,256,128]{1,2,0:T(8,128)}, u32[]{:S(2)}) copy-start(f32[8,256,128]{1,2,0:T(8,128)} %copy-done.3) | copy-start | bytes 3145732
  154.9 23.8 %collective-permute-start.6 = (f32[8,1,128]{1,0,2:T(8,128)S(1)}, f32[8,1,128]{1,0,2:T(8,128)S(1)}, u32[]{:S(2)}, u32[]{:S(2)}) collective-permute-start(f32[8,1,128]{1,0,2:T(8,128)S(1)} %get-tuple-element.206), channel_id=1, source_target_pairs={{0,2},{2,4},{4,6},{6,8},{8,10},{10,12},{12,14},{14,16},{16,18},{18... | collective-permute-start | bytes 12296 | tf_op jit(solution)/shard_map/ppermute | solution.py:29
  156.2 24.3 %collective-permute-start.7 = (f32[8,1,128]{1,0,2:T(8,128)S(1)}, f32[8,1,128]{1,0,2:T(8,128)S(1)}, u32[]{:S(2)}, u32[]{:S(2)}) collective-permute-start(f32[8,1,128]{1,0,2:T(8,128)S(1)} %get-tuple-element.207), channel_id=1, source_target_pairs={{2,0},{4,2},{6,4},{8,6},{10,8},{12,10},{14,12},{16,14},{18,16},{20... | collective-permute-start | bytes 12296 | tf_op jit(solution)/shard_map/ppermute | solution.py:30
  180.6 2.1 collective-permute-start.8
  181.9 1.2 collective-permute-start.9
  183.7 14.0 %copy-start.8 = (bf16[1152,256]{1,0:T(8,128)(2,1)S(1)}, bf16[1152,256]{1,0:T(8,128)(2,1)}, u32[]{:S(2)}) copy-start(bf16[1152,256]{1,0:T(8,128)(2,1)} %copy-done.7) | copy-start | bytes 1769476
  197.7 751.7 %copy-start.5 = (f32[8,256,128]{1,2,0:T(8,128)S(1)}, f32[8,256,128]{1,2,0:T(8,128)}, u32[]{:S(2)}) copy-start(f32[8,256,128]{1,2,0:T(8,128)} %get-tuple-element.217) | copy-start | bytes 3145732
  197.8 735.7 %collective-permute-start.10 = (bf16[64,18,128]{2,1,0:T(8,128)(2,1)S(1)}, bf16[64,18,128]{2,1,0:T(8,128)(2,1)}, u32[]{:S(2)}, u32[]{:S(2)}) collective-permute-start(bf16[64,18,128]{2,1,0:T(8,128)(2,1)S(1)} %get-tuple-element.221), channel_id=1, source_target_pairs={{64,0},{65,1},{66,2},{67,3},{68,4},{69,5},{70,6},{71,7},{72,8},{73... | collective-permute-start | bytes 884744 | tf_op jit(solution)/shard_map/ppermute | solution.py:19
  933.5 15.9 %all-to-all-start.2 = ((bf16[64,18,128]{2,1,0:T(8,128)(2,1)}), bf16[64,18,128]{2,1,0:T(8,128)(2,1)S(1)}, u32[]{:S(2)}, u32[]{:S(2)}) async-start(bf16[64,18,128]{2,1,0:T(8,128)(2,1)} %collective-permute-done.10), calls=%async_computation.2 | async-start | bytes 786432 | tf_op jit(solution)/shard_map/all_to_all | solution.py:207
  (6 other events, 5.9 us)
where the time goes:
time: 970 us; the launch traced here: 963 us
  waiting for transfers between devices  821 us (85%)
  blocking collectives  42.4 us (4%)
  starting transfers between devices  29.9 us (3%)
  matrix products  29.3 us (3%)
  local copies, waits for them, and re-layouts  23.2 us (2%)
  other arithmetic  12.9 us (1%)
    ppermute x3, waiting for transfers between devices, from_behind(): return lax.ppermute(block, axis, route)  734 us
    all_to_all x1, waiting for transfers between devices, local(): lax.all_to_all(labels, ('gx', 'gy'), split_axis=0, concat_axis=0, tiled=T...  45.3 us
    all_to_all x1, blocking collectives, local(): lax.all_to_all(packed, ('gx', 'gy'), split_axis=0, concat_axis=0, tiled=T...  42.4 us
    ppermute x4, waiting for transfers between devices, extended_2(): before = lax.ppermute(last, axis, up)  27.2 us
  transfers between devices with their start and end apart: 13, of which 11 were waited for; matrix products, arithmetic and copies ran while one was open for 1% of the time, Pallas kernels for 0%

commit v1 on v0

v1 whole, which is shorter than its diff:
```python
import functools

import jax
import jax.numpy as jnp
import numpy as np
from jax import lax
from jax.experimental import pallas as pl
from jax.experimental.pallas import tpu as pltpu
from jax.sharding import PartitionSpec as P

ATMOS_DIFFUSION = 0.01
MIXING = 0.2
OCEAN_DIFFUSION = 0.12

RANKS = 64
CAP = 18
LEV = 8
NF = 8
ROWS = 256
COLS = 128
K = 2
OCEAN_SLOTS = 19
ATMOS_SLOTS = 24

VMEM = pl.BlockSpec(memory_space=pltpu.VMEM)
SMEM = pl.BlockSpec(memory_space=pltpu.SMEM)
F32 = jnp.float32
BF16 = jnp.bfloat16


def second_table():
    gll_nodes = np.array([-1.0, -1.0 / np.sqrt(5.0), 1.0 / np.sqrt(5.0), 1.0])
    poly_order = 3
    legendre = (5.0 * gll_nodes**3 - 3.0 * gll_nodes) / 2.0
    derivative = np.zeros((4, 4))
    for row_index in range(4):
        for col_index in range(4):
            if row_index != col_index:
                derivative[row_index, col_index] = legendre[row_index] / (
                    legendre[col_index] * (gll_nodes[row_index] - gll_nodes[col_index])
                )
    derivative[0, 0] = -poly_order * (poly_order + 1) / 4.0
    derivative[3, 3] = poly_order * (poly_order + 1) / 4.0
    return derivative @ derivative


SECOND = second_table()


def call(body, out_shape, specs, **params):
    return pl.pallas_call(
        body,
        out_shape=out_shape,
        in_specs=specs,
        out_specs=jax.tree.map(lambda _: VMEM, out_shape),
        compiler_params=pltpu.CompilerParams(vmem_limit_bytes=params.pop("vmem", 24 << 20)),
        **params,
    )


def positions_body(peer_ref, line_ref, pos_ref, label_ref):
    count = ROWS * K
    peer = jnp.concatenate([peer_ref[k : k + 1, :] for k in range(K)], axis=1)
    line = jnp.concatenate([line_ref[k : k + 1, :] for k in range(K)], axis=1)
    hits = lax.broadcasted_iota(jnp.int32, (RANKS, count), 0) == peer
    hits_f = jnp.where(hits, 1.0, 0.0)
    earlier = lax.broadcasted_iota(jnp.int32, (count, count), 0) < lax.broadcasted_iota(
        jnp.int32, (count, count), 1
    )
    before = jnp.dot(
        hits_f.astype(BF16),
        jnp.where(earlier, 1.0, 0.0).astype(BF16),
        preferred_element_type=F32,
    )
    slot = jnp.sum(hits_f * before, axis=0, keepdims=True).astype(jnp.int32)
    for width, at in ((OCEAN_SLOTS, 0), (ATMOS_SLOTS, K)):
        position = peer * width + slot
        for k in range(K):
            pos_ref[at + k : at + k + 1, :] = position[:, k * ROWS : (k + 1) * ROWS]
    slot_hits = lax.broadcasted_iota(jnp.int32, (COLS, count), 0) == slot
    shifted = jnp.where(hits, (line + 1).astype(F32), 0.0).astype(BF16)
    label_ref[...] = (
        lax.dot_general(
            shifted,
            jnp.where(slot_hits, 1.0, 0.0).astype(BF16),
            (((1,), (1,)), ((), ())),
            preferred_element_type=F32,
        )
        - 1.0
    )


def positions(peer, line):
    return call(
        positions_body,
        (
            jax.ShapeDtypeStruct((2 * K, ROWS), jnp.int32),
            jax.ShapeDtypeStruct((RANKS, COLS), F32),
        ),
        [VMEM, VMEM],
    )(peer.T, line.T)


def ocean_flux_body(per, pos_ref, label_ref, air_ref, prior_ref, factor_ref, w_ref, out_ref, rows):
    step = pl.program_id(0)

    @pl.when(step == 0)
    def _():
        out_ref[...] = jnp.zeros_like(out_ref)
        for d in range(RANKS):
            out_ref[d * OCEAN_SLOTS + CAP] = jnp.broadcast_to(
                label_ref[d : d + 1, :], (NF, COLS)
            ).astype(BF16)

    difference = air_ref[...] - prior_ref[...]
    for f in range(NF):
        rows[pl.ds(f, per, stride=NF), :] = factor_ref[f] * difference
    for b in range(per):
        flux = rows[b * NF : (b + 1) * NF, :].astype(BF16)
        for k in range(K):
            part = jnp.dot(flux, w_ref[b, k], preferred_element_type=F32)
            out_ref[pos_ref[k, step * per + b]] = part.astype(BF16)


def flux_specs(per):
    return [
        SMEM,
        pl.BlockSpec((RANKS, COLS), lambda i: (0, 0)),
        pl.BlockSpec((per, COLS), lambda i: (i, 0)),
        pl.BlockSpec((per, COLS), lambda i: (i, 0)),
        pl.BlockSpec((NF, per, COLS), lambda i: (0, i, 0)),
        pl.BlockSpec((per, K, COLS, COLS), lambda i: (i, 0, 0, 0)),
    ]


def ocean_flux(pos, labels, air, prior, factors, weights, per=16):
    return pl.pallas_call(
        functools.partial(ocean_flux_body, per),
        out_shape=jax.ShapeDtypeStruct((RANKS * OCEAN_SLOTS, NF, COLS), BF16),
        grid=(ROWS // per,),
        in_specs=flux_specs(per),
        out_specs=pl.BlockSpec((RANKS * OCEAN_SLOTS, NF, COLS), lambda i: (0, 0, 0)),
        scratch_shapes=[pltpu.VMEM((per * NF, COLS), F32)],
        compiler_params=pltpu.CompilerParams(vmem_limit_bytes=32 << 20),
    )(pos, labels, air, prior, factors, weights)


def atmos_flux_body(
    per, pos_ref, label_ref, air_ref, prior_ref, factor_ref, w_ref, share_ref, out_ref, packed, rows
):
    step = pl.program_id(0)

    @pl.when(step == 0)
    def _():
        packed[...] = jnp.zeros_like(packed)
        for d in range(RANKS):
            packed[d * ATMOS_SLOTS + CAP : d * ATMOS_SLOTS + CAP + 1, :] = label_ref[d : d + 1, :]

    mixed = share_ref[0, 0] * factor_ref[0]
    for f in range(1, NF):
        mixed += share_ref[0, f] * factor_ref[f]
    flux = mixed * (air_ref[...] - prior_ref[...])
    high = flux.astype(BF16).astype(F32)
    rows[...] = jnp.zeros_like(rows)
    rows[pl.ds(0, per, stride=8), :] = high
    rows[pl.ds(1, per, stride=8), :] = flux - high
    for b in range(per):
        pair = rows[b * 8 : (b + 1) * 8, :].astype(BF16)
        for k in range(K):
            part = jnp.dot(pair, w_ref[b, k], preferred_element_type=F32)
            packed[pl.ds(pos_ref[K + k, step * per + b], 1), :] = part[0:1, :] + part[1:2, :]

    @pl.when(step == pl.num_programs(0) - 1)
    def _():
        out_ref[...] = packed[...].astype(BF16).reshape(RANKS, ATMOS_SLOTS, COLS)


def atmos_flux(pos, labels, air, prior, factors, weights, share, per=16):
    return pl.pallas_call(
        functools.partial(atmos_flux_body, per),
        out_shape=jax.ShapeDtypeStruct((RANKS, ATMOS_SLOTS, COLS), BF16),
        grid=(ROWS // per,),
        in_specs=flux_specs(per) + [SMEM],
        out_specs=pl.BlockSpec((RANKS, ATMOS_SLOTS, COLS), lambda i: (0, 0, 0)),
        scratch_shapes=[
            pltpu.VMEM((RANKS * ATMOS_SLOTS, COLS), F32),
            pltpu.VMEM((per * 8, COLS), F32),
        ],
        compiler_params=pltpu.CompilerParams(vmem_limit_bytes=32 << 20),
    )(pos, labels, air, prior, factors, weights, share)


def iotas():
    return (
        lax.broadcasted_iota(jnp.int32, (ROWS, COLS), 0),
        lax.broadcasted_iota(jnp.int32, (ROWS, COLS), 1),
    )


def side_lanes(lane, level):
    return (lane == 2 * level) | (lane == (2 * level - 1) % COLS)


def packed_sides(fields, lane):
    packed = jnp.zeros((ROWS, COLS), F32)
    for l, field in enumerate(fields):
        turned = field if l == 0 else pltpu.roll(field, 2 * l, 1)
        packed = jnp.where(side_lanes(lane, l), turned, packed)
    return packed


def unpacked_sides(packed, level):
    return packed if level == 0 else pltpu.roll(packed, COLS - 2 * level, 1)


def row_above(field, before, row):
    return jnp.where(row == 0, before, pltpu.roll(field, 1, 0))


def row_below(field, after, row):
    return jnp.where(row == ROWS - 1, after, pltpu.roll(field, ROWS - 1, 0))


def column_left(field, sides, lane):
    return pltpu.roll(jnp.where(lane == COLS - 1, sides, field), 1, 1)


def column_right(field, sides, lane):
    return pltpu.roll(jnp.where(lane == 0, sides, field), COLS - 1, 1)


def second_along(field, axis, index, extent):
    phase = index % 4
    total = None
    for shift in range(-3, 4):
        factor = jnp.zeros(index.shape, F32)
        for p in range(4):
            if 0 <= p + shift < 4:
                factor = jnp.where(phase == p, F32(SECOND[p, p + shift]), factor)
        moved = field if shift == 0 else pltpu.roll(field, (-shift) % extent, axis)
        total = factor * moved if total is None else total + factor * moved
    return total


def atmos_local(levels, row, lane):
    out = []
    for l, field in enumerate(levels):
        below, above = levels[max(l - 1, 0)], levels[min(l + 1, LEV - 1)]
        along = second_along(field, 0, row, ROWS) + second_along(field, 1, lane, COLS)
        out.append(field + ATMOS_DIFFUSION * along + MIXING * (above + below - 2.0 * field))
    return out


def assembled_rows(field, before, after, row):
    phase = row % 4
    return jnp.where(
        phase == 3,
        0.5 * (field + row_below(field, after, row)),
        jnp.where(phase == 0, 0.5 * (field + row_above(field, before, row)), field),
    )


def assembled_columns(field, sides, lane):
    phase = lane % 4
    return jnp.where(
        phase == 3,
        0.5 * (field + column_right(field, sides, lane)),
        jnp.where(phase == 0, 0.5 * (field + column_left(field, sides, lane)), field),
    )


def assembled(levels_ref, sides_ref, before_ref, after_ref, sides_row, row, lane):
    end = sides_row
    sides = assembled_rows(
        sides_ref[...], before_ref[end : end + 1, :], after_ref[end : end + 1, :], row
    )
    out = []
    for l in range(LEV):
        half = assembled_rows(
            levels_ref[l], before_ref[l : l + 1, :], after_ref[l : l + 1, :], row
        )
        out.append(assembled_columns(half, unpacked_sides(sides, l), lane))
    return out


def neighbour_counts(table_ref, row, lane):
    own = (row + 1) * (COLS + 2) + lane + 1
    counts = {}
    for dr in (-1, 0, 1):
        for dc in (-1, 0, 1):
            if dr or dc:
                target = own + (dr * (COLS + 2) + dc)
                count = jnp.zeros((ROWS, COLS), F32)
                for e in range(table_ref.shape[0]):
                    count += jnp.where(table_ref[e] == target, 1.0, 0.0)
                counts[dr, dc] = count
    return counts


def neighbour_spread(field, sides, before, after, sides_before, sides_after, counts, row, lane):
    total = jnp.zeros((ROWS, COLS), F32)
    for dr in (-1, 0, 1):
        if dr == 0:
            line, ends = field, sides
        elif dr == -1:
            line, ends = row_above(field, before, row), row_above(sides, sides_before, row)
        else:
            line, ends = row_below(field, after, row), row_below(sides, sides_after, row)
        total += counts[dr, -1] * (column_left(line, ends, lane) - field)
        total += counts[dr, 1] * (column_right(line, ends, lane) - field)
        if dr:
            total += counts[dr, 0] * (line - field)
    return total


def atmos_first_body(u_ref, sea_ref, out_ref, sides_ref):
    row, lane = iotas()
    moved = atmos_local([u_ref[l] for l in range(LEV)], row, lane)
    for l in range(LEV):
        out_ref[l] = moved[l]
    sides_ref[...] = packed_sides(moved + [sea_ref[0].astype(F32)], lane)


def atmos_second_body(
    u_ref, sides_ref, before_ref, after_ref, sea_ref, table_ref, out_ref, packed_ref, base_ref
):
    row, lane = iotas()
    level_list = assembled(u_ref, sides_ref, before_ref, after_ref, LEV + 1, row, lane)
    moved = atmos_local(level_list, row, lane)
    for l in range(LEV):
        out_ref[l] = moved[l]
    packed_ref[...] = packed_sides(moved, lane)
    top, under = sea_ref[0].astype(F32), sea_ref[1].astype(F32)
    sides = unpacked_sides(sides_ref[...], LEV)
    ends = [unpacked_sides(r[LEV + 1 : LEV + 2, :], LEV) for r in (before_ref, after_ref)]
    spread = neighbour_spread(
        top,
        sides,
        before_ref[LEV : LEV + 1, :],
        after_ref[LEV : LEV + 1, :],
        ends[0],
        ends[1],
        neighbour_counts(table_ref, row, lane),
        row,
        lane,
    )
    base_ref[...] = top + OCEAN_DIFFUSION * spread + MIXING * (under - top)


def atmos_third_body(u_ref, sides_ref, before_ref, after_ref, out_ref):
    row, lane = iotas()
    final = assembled(u_ref, sides_ref, before_ref, after_ref, LEV, row, lane)
    for l in range(LEV):
        out_ref[l] = final[l]


def ocean_sides_body(o_ref, sides_ref):
    _, lane = iotas()
    sides_ref[...] = packed_sides([o_ref[l] for l in range(LEV)], lane)


def ocean_base_body(o_ref, sides_ref, before_ref, after_ref, table_ref, out_ref, counts_ref):
    row, lane = iotas()
    order = [(dr, dc) for dr in (-1, 0, 1) for dc in (-1, 0, 1) if dr or dc]
    found = neighbour_counts(table_ref, row, lane)
    for n, key in enumerate(order):
        counts_ref[n] = found[key]
    for l in range(LEV):
        field = o_ref[l]
        sides = unpacked_sides(sides_ref[...], l)
        ends = [unpacked_sides(r[LEV : LEV + 1, :], l) for r in (before_ref, after_ref)]
        spread = neighbour_spread(
            field,
            sides,
            before_ref[l : l + 1, :],
            after_ref[l : l + 1, :],
            ends[0],
            ends[1],
            {key: counts_ref[n] for n, key in enumerate(order)},
            row,
            lane,
        )
        below, above = o_ref[max(l - 1, 0)], o_ref[min(l + 1, LEV - 1)]
        out_ref[l] = field + OCEAN_DIFFUSION * spread + MIXING * (above + below - 2.0 * field)


def exchanged(levels, sides):
    size = lax.axis_size("gx")
    up = [(i, (i + 1) % size) for i in range(size)]
    down = [(j, i) for i, j in up]
    sides = lax.ppermute(sides, "gy", [(0, 1), (1, 0)])
    last = jnp.concatenate([v[:, ROWS - 1, :] for v in levels] + [sides[ROWS - 1 :, :]], axis=0)
    first = jnp.concatenate([v[:, 0, :] for v in levels] + [sides[:1, :]], axis=0)
    return sides, lax.ppermute(last, "gx", up), lax.ppermute(first, "gx", down)


def row_hits(labels):
    width = ATMOS_SLOTS
    shape = (RANKS, width, COLS)
    diagonal = lax.broadcasted_iota(jnp.int32, shape, 1) == lax.broadcasted_iota(jnp.int32, shape, 2)
    spread = jnp.where(diagonal, labels[:, None, :], 0.0)
    column = jnp.sum(spread, axis=2, keepdims=True).reshape(RANKS * width, 1)
    slot = lax.broadcasted_iota(jnp.int32, (RANKS, width, 1), 1).reshape(RANKS * width, 1)
    column = jnp.where(slot < CAP, column, -1.0).astype(jnp.int32)
    rows = lax.broadcasted_iota(jnp.int32, (RANKS * width, ROWS), 1)
    return jnp.where(column == rows, 1.0, 0.0).astype(BF16)


def top_body(arrived_ref, base_ref, out_ref):
    arrived = arrived_ref[...].astype(F32)
    hits = row_hits(arrived[:, CAP, :])
    values = arrived.reshape(RANKS * ATMOS_SLOTS, COLS).astype(BF16)
    pushed = lax.dot_general(hits, values, (((0,), (0,)), ((), ())), preferred_element_type=F32)
    top = (base_ref[...] + pushed).astype(BF16)
    picked = jnp.dot(hits, top, preferred_element_type=F32)
    out_ref[...] = picked.astype(BF16).reshape(RANKS, ATMOS_SLOTS, COLS)


def sums_body(arrived_ref, base_ref, share_ref, out_ref, first_ref, wide, hits):
    f = pl.program_id(0)
    slots = RANKS * OCEAN_SLOTS

    @pl.when(f == 0)
    def _():
        wide[...] = arrived_ref[...].astype(F32).reshape(slots * NF, COLS)
        width = OCEAN_SLOTS * NF
        labels = wide[pl.ds(CAP * NF, RANKS, stride=width), :]
        hits[...] = row_hits(labels)
        out_ref[...] = base_ref[...]

    parts = []
    for d in range(RANKS):
        begin = d * OCEAN_SLOTS * NF + f
        parts.append(wide[pl.ds(begin, 16, stride=NF), :])
        parts.append(wide[pl.ds(begin + 16 * NF, 3, stride=NF), :])
        parts.append(jnp.zeros((5, COLS), F32))
    values = jnp.concatenate(parts, axis=0).astype(BF16)
    forcing = lax.dot_general(
        hits[...], values, (((0,), (0,)), ((), ())), preferred_element_type=F32
    )
    for l in range(LEV):
        out_ref[l] += share_ref[l, f] * forcing

    @pl.when(f == 0)
    def _():
        first_ref[...] = forcing


def ocean_sums(arrived, base, share):
    whole = lambda shape: pl.BlockSpec(shape, lambda f: (0,) * len(shape))
    slots = RANKS * OCEAN_SLOTS
    return pl.pallas_call(
        sums_body,
        out_shape=(
            jax.ShapeDtypeStruct((LEV, ROWS, COLS), F32),
            jax.ShapeDtypeStruct((ROWS, COLS), F32),
        ),
        grid=(NF,),
        in_specs=[whole((slots, NF, COLS)), whole((LEV, ROWS, COLS)), SMEM],
        out_specs=(whole((LEV, ROWS, COLS)), whole((ROWS, COLS))),
        scratch_shapes=[
            pltpu.VMEM((slots * NF, COLS), F32),
            pltpu.VMEM((RANKS * ATMOS_SLOTS, ROWS), BF16),
        ],
        compiler_params=pltpu.CompilerParams(vmem_limit_bytes=40 << 20),
    )(arrived, base, share)


def remap_body(per, pos_ref, arrived_ref, w_ref, out_ref, wide):
    step = pl.program_id(0)

    @pl.when(step == 0)
    def _():
        wide[...] = arrived_ref[...].astype(F32).reshape(RANKS * ATMOS_SLOTS, COLS)

    for b in range(per):
        total = None
        for k in range(K):
            value = wide[pl.ds(pos_ref[K + k, step * per + b], 1), :].astype(BF16)
            part = lax.dot_general(
                value, w_ref[b, k], (((1,), (1,)), ((), ())), preferred_element_type=F32
            )
            total = part if total is None else total + part
        out_ref[b : b + 1, :] = total


def remap(pos, arrived, weights, per=16):
    return pl.pallas_call(
        functools.partial(remap_body, per),
        out_shape=jax.ShapeDtypeStruct((ROWS, COLS), F32),
        grid=(ROWS // per,),
        in_specs=[
            SMEM,
            pl.BlockSpec((RANKS, ATMOS_SLOTS, COLS), lambda i: (0, 0, 0)),
            pl.BlockSpec((per, K, COLS, COLS), lambda i: (i, 0, 0, 0)),
        ],
        out_specs=pl.BlockSpec((per, COLS), lambda i: (i, 0)),
        scratch_shapes=[pltpu.VMEM((RANKS * ATMOS_SLOTS, COLS), F32)],
        compiler_params=pltpu.CompilerParams(vmem_limit_bytes=32 << 20),
    )(pos, arrived, weights)


def to_peers(payload):
    return lax.all_to_all(payload, ("gx", "gy"), split_axis=0, concat_axis=0, tiled=True)


def local(
    layered_heat_profile,
    prior_marine_heat,
    transfer_factor_table,
    depth_fraction_matrix,
    adjacent_cell_table,
    destination_water_peer,
    destination_water_line,
    interpolation_matrix_blocks,
):
    is_atmosphere_side = lax.axis_index("comp") == 0
    own = layered_heat_profile[0]
    block = jax.ShapeDtypeStruct((LEV, ROWS, COLS), F32)
    plane = jax.ShapeDtypeStruct((ROWS, COLS), F32)

    air = lax.ppermute(own[0], "comp", [(0, 1)])
    sea = lax.ppermute(own[:2].astype(BF16), "comp", [(1, 0)])
    pos, labels = positions(destination_water_peer, destination_water_line)

    def early_flux():
        return atmos_flux(
            pos,
            labels,
            own[0],
            prior_marine_heat,
            transfer_factor_table,
            interpolation_matrix_blocks,
            depth_fraction_matrix,
        )

    packed = lax.cond(
        is_atmosphere_side,
        early_flux,
        lambda: jnp.zeros((RANKS, ATMOS_SLOTS, COLS), BF16),
    )

    def atmosphere():
        arrived = to_peers(packed)
        moved, sides = call(atmos_first_body, (block, plane), [VMEM, VMEM])(own, sea)
        halo = exchanged([moved, sea[:1].astype(F32)], sides)
        moved, sides, base = call(atmos_second_body, (block, plane, plane), [VMEM] * 6)(
            moved, *halo, sea, adjacent_cell_table
        )
        picked = call(
            top_body, jax.ShapeDtypeStruct((RANKS, ATMOS_SLOTS, COLS), BF16), [VMEM, VMEM]
        )(arrived, base)
        returned = to_peers(picked)
        halo = exchanged([moved], sides)
        final = call(atmos_third_body, block, [VMEM] * 4)(moved, *halo)
        return final, remap(pos, returned, interpolation_matrix_blocks)

    def ocean():
        payload = ocean_flux(
            pos,
            labels,
            air,
            prior_marine_heat,
            transfer_factor_table,
            interpolation_matrix_blocks,
        )
        arrived = to_peers(payload.reshape(RANKS, OCEAN_SLOTS * NF, COLS))
        sides = call(ocean_sides_body, plane, [VMEM])(own)
        halo = exchanged([own], sides)
        base = call(
            ocean_base_body,
            block,
            [VMEM] * 5,
            scratch_shapes=[pltpu.VMEM((8, ROWS, COLS), F32)],
        )(own, *halo, adjacent_cell_table)
        return ocean_sums(
            arrived.reshape(RANKS * OCEAN_SLOTS, NF, COLS), base, depth_fraction_matrix
        )

    state, plane_out = lax.cond(is_atmosphere_side, atmosphere, ocean)
    return state[None], plane_out[None]


def solution(mesh):
    return jax.shard_map(
        local,
        mesh=mesh,
        in_specs=(
            P("comp", None, "gx", "gy"),
            P("gx", "gy"),
            P(None, "gx", "gy"),
            P(),
            P(None, "gx", "gy"),
            P(("gx", "gy"), None),
            P(("gx", "gy"), None),
            P(("gx", "gy"), None, None, None),
        ),
        out_specs=(P("comp", None, "gx", "gy"), P("comp", "gx", "gy")),
        check_vma=False,
    )
```

time: 970 us -> 96.8 us (0.10)
  waiting for transfers between devices: 821 us -> 7.16 us
  Pallas kernels: 0 us -> 43.8 us
  blocking collectives: 42.4 us -> 0 us
  matrix products: 29.3 us -> 0 us
  local copies, waits for them, and re-layouts: 23.2 us -> 6.06 us
  other arithmetic: 12.9 us -> 0.95 us
    ppermute x11 -> x8, waiting for transfers between devices: 765 us -> 7.16 us  [the longest x2 7.14 us: exchanged(): lax.ppermute(last, 'gx', up)]
    all_to_all x2, waiting for transfers between devices: 56.1 us -> 0.01 us  [to_peers(): lax.all_to_all(payload, ('gx', 'gy'), split_axis=0, concat_axis=0, tiled=...]
    pallas_call x0 -> x7, Pallas kernels: none -> 43.8 us  [the longest x1 17.1 us: remap(): pl.pallas_call(functools.partial(remap_body, per), out_shape=jax.ShapeDty...]
    all_to_all x1 -> x0, blocking collectives: 42.4 us -> none  [local(): lax.all_to_all(packed, ('gx', 'gy'), split_axis=0, concat_axis=0, tiled=T...]
    dot_general x9 -> x0, matrix products: 29.3 us -> none  [the longest x1 10.2 us: atmosphere_sea_temp(): jnp.einsum('bkpq,bkq->bp', interpolation_matrix_blocks, values.reshape(ro...]
    cond x18 -> x8, local copies, waits for them, and re-layouts: 10.9 us -> 0.65 us
    ppermute x11 -> x8, starting transfers between devices: 20 us -> 22 us  [the longest x2 9.22 us: exchanged(): lax.ppermute(first, 'gx', down)]
  transfers between devices with their start and end apart: 13 -> 10, of which waited for: 11 -> 2; matrix products, arithmetic and copies ran while one was open for 1% -> 4% of each run, Pallas kernels for 0% -> 24%
where the time goes in v1:
time: 96.8 us; the launch traced here: 95.7 us
  Pallas kernels  43.8 us (45%)
  starting transfers between devices  36.8 us (38%)
  waiting for transfers between devices  7.16 us (7%)
  local copies, waits for them, and re-layouts  6.06 us (6%)
    pallas_call x1, Pallas kernels, remap(): pl.pallas_call(functools.partial(remap_body, per), out_shape=jax.ShapeDty...  17.1 us
    all_to_all x2, starting transfers between devices, to_peers(): lax.all_to_all(payload, ('gx', 'gy'), split_axis=0, concat_axis=0, tiled=...  14.8 us
    pallas_call x1, Pallas kernels, atmos_flux(): pl.pallas_call(functools.partial(atmos_flux_body, per), out_shape=jax.Sha...  14.5 us
    ppermute x2, starting transfers between devices, exchanged(): lax.ppermute(first, 'gx', down)  9.22 us
    ppermute x2, waiting for transfers between devices, exchanged(): lax.ppermute(last, 'gx', up)  7.14 us
    ppermute x1, starting transfers between devices, local(): air = lax.ppermute(own[0], 'comp', [(0, 1)])  6.34 us
    pallas_call x1, Pallas kernels, atmosphere(): call(atmos_second_body, (block, plane, plane), [VMEM] * 6)  4.37 us
    pallas_call x1, Pallas kernels, atmosphere(): call(atmos_first_body, (block, plane), [VMEM, VMEM])(own, sea)  3.47 us
  transfers between devices with their start and end apart: 10, of which 2 were waited for; matrix products, arithmetic and copies ran while one was open for 4% of the time, Pallas kernels for 24%

profile of v1, /device:TPU:1, one launch (start us, length us, event | category | flops | bytes accessed | tf_op | source)
XLA Modules:
  0.0 95.7 jit_solution(13969868572688010877)
XLA Ops:
  0.6 0.9 slice_bitcast_fusion.9
  1.5 6.3 %collective-permute-start.9 = (f32[256,128]{1,0:T(8,128)S(1)}, f32[256,128]{1,0:T(8,128)S(1)}, u32[]{:S(2)}, u32[]{:S(2)}) collective-permute-start(f32[256,128]{1,0:T(8,128)S(1)} %slice_bitcast_fusion.9), channel_id=1, source_target_pairs={{0,64},{1,65},{2,66},{3,67},{4,68},{5,69},{6,70},{7,71},{8,72},{9,... | collective-permute-start | bytes 393224 | tf_op jit(solution)/shard_map/ppermute | solution.py:522
  7.9 1.0 %fusion = bf16[2,256,128]{2,1,0:T(8,128)(2,1)S(1)} fusion(f32[1,8,256,128]{3,2,1,0:T(8,128)} %param.12), kind=kLoop, calls=%fused_computation.17 | loop fusion | bytes 262144 | tf_op jit(solution)/shard_map/convert_element_type | solution.py:523
  8.9 1.3 %collective-permute-start.10 = (bf16[2,256,128]{2,1,0:T(8,128)(2,1)S(1)}, bf16[2,256,128]{2,1,0:T(8,128)(2,1)S(1)}, u32[]{:S(2)}, u32[]{:S(2)}) collective-permute-start(bf16[2,256,128]{2,1,0:T(8,128)(2,1)S(1)} %fusion), channel_id=1, source_target_pairs={{64,0},{65,1},{66,2},{67,3},{68,4},{69,5},{70,6},{71,7},{72,8},{73... | collective-permute-start | bytes 393224 | tf_op jit(solution)/shard_map/ppermute | solution.py:523
  11.9 15.5 %conditional.2 = (bf16[64,24,128]{2,1,0:T(8,128)(2,1)S(1)}) conditional(s32[]{:T(128)} %convert_element_type.11, () %tuple.26, (f32[8,256,128]{2,1,0:T(8,128)}, s32[4,256]{1,0:T(4,128)S(1)}, f32[64,128]{1,0:T(8,128)S(1)}, f32[256,128]{1,0:T(8,128)}, f32[8,256,128]{2,1,0:T(8,128)}, /*index=5*/bf16[256,2,128,128]{3,2,1,0:T(8,128)(2,1)}, ...), branch_computations={%region_0.0_spmd, %region_1.0_spmd} | conditional | bytes 393226 | solution.py:537
  11.9 0.9 slice_bitcast_fusion.air_ref
  12.9 14.5 %branch_1_fun.6 = bf16[64,24,128]{2,1,0:T(8,128)(2,1)S(1)} custom-call(s32[4,256]{1,0:T(4,128)S(1)} %get-tuple-element.51.pos_ref, f32[64,128]{1,0:T(8,128)S(1)} %get-tuple-element.52.label_ref, f32[256,128]{1,0:T(8,128)S(1)} %slice_bitcast_fusion.air_ref, f32[256,128]{1,0:T(8,128)} %get-tuple-element.54.prior_ref, ...), custom_call_target="tpu_custom_call" | custom-call | tf_op jit(solution)/shard_map/cond/branch_1_fun/pallas_call | solution.py:179
  27.4 68.3 %conditional.3 = (f32[1,8,256,128]{3,2,1,0:T(8,128)}, f32[1,256,128]{2,1,0:T(8,128)}) conditional(s32[]{:T(128)} %convert_element_type.11, (s32[4,256]{1,0:T(4,128)S(1)}, f32[64,128]{1,0:T(8,128)S(1)}, f32[256,128]{1,0:T(8,128)S(1)}, f32[256,128]{1,0:T(8,128)}, f32[8,256,128]{2,1,0:T(8,128)}, /*index=5*/bf16[256,2,128,128]{3,2,1,0:T(8,128)(2,1)}, ...), branch_computations={%region_2.0_spmd, %region_3.0_spmd} | conditional | flops 40192 | bytes 31663412 | solution.py:580
  28.1 3.5 %branch_1_fun.7 = (f32[8,256,128]{2,1,0:T(8,128)S(1)}, f32[256,128]{1,0:T(8,128)S(1)}) custom-call(f32[8,256,128]{2,1,0:T(8,128)} %get-tuple-element.69.u_ref, bf16[2,256,128]{2,1,0:T(8,128)(2,1)} %copy-done.8), custom_call_target="tpu_custom_call" | custom-call | tf_op jit(solution)/shard_map/cond/branch_1_fun/pallas_call | solution.py:545
  31.6 1.0 %collective-permute-start.3 = (f32[256,128]{1,0:T(8,128)S(1)}, f32[256,128]{1,0:T(8,128)S(1)}, u32[]{:S(2)}, u32[]{:S(2)}) collective-permute-start(f32[256,128]{1,0:T(8,128)S(1)} %get-tuple-element.72), channel_id=1, source_target_pairs={{0,1},{1,0},{2,3},{3,2},{4,5},{5,4},{6,7},{7,6},{8,9},{9,8},{10,11... | collective-permute-start | bytes 393224 | tf_op jit(solution)/shard_map/cond/branch_1_fun/ppermute | solution.py:391
  32.6 8.2 %all-to-all-start.1 = ((bf16[64,24,128]{2,1,0:T(8,128)(2,1)}), bf16[64,24,128]{2,1,0:T(8,128)(2,1)S(1)}, u32[]{:S(2)}, u32[]{:S(2)}) async-start(bf16[64,24,128]{2,1,0:T(8,128)(2,1)} %copy-done.7), calls=%async_computation.1 | async-start | bytes 786432 | tf_op jit(solution)/shard_map/cond/branch_1_fun/all_to_all | solution.py:504
  40.9 0.9 slice_convert_fusion
  42.5 1.5 %collective-permute-start.4 = (f32[10,128]{1,0:T(8,128)S(1)}, f32[10,128]{1,0:T(8,128)S(1)}, u32[]{:S(2)}, u32[]{:S(2)}) collective-permute-start(f32[10,128]{1,0:T(8,128)S(1)} %pad_maximum_fusion.2), channel_id=1, source_target_pairs={{0,2},{2,4},{4,6},{6,8},{8,10},{10,12},{12,14},{14,16},{16,18},{18... | collective-permute-start | bytes 15368 | tf_op jit(solution)/shard_map/cond/branch_1_fun/ppermute | solution.py:394
  43.9 4.6 %collective-permute-start.5 = (f32[10,128]{1,0:T(8,128)S(1)}, f32[10,128]{1,0:T(8,128)S(1)}, u32[]{:S(2)}, u32[]{:S(2)}) collective-permute-start(f32[10,128]{1,0:T(8,128)S(1)} %pad_maximum_fusion.3), channel_id=1, source_target_pairs={{2,0},{4,2},{6,4},{8,6},{10,8},{12,10},{14,12},{16,14},{18,16},{20... | collective-permute-start | bytes 15368 | tf_op jit(solution)/shard_map/cond/branch_1_fun/ppermute | solution.py:394
  48.5 2.8 %collective-permute-done.4.before_ref = f32[10,128]{1,0:T(8,128)S(1)} collective-permute-done((f32[10,128]{1,0:T(8,128)S(1)}, f32[10,128]{1,0:T(8,128)S(1)}, u32[]{:S(2)}, u32[]{:S(2)}) %collective-permute-start.4) | collective-permute-done | bytes 5152 | tf_op jit(solution)/shard_map/cond/branch_1_fun/ppermute | solution.py:394
  51.3 4.4 %branch_1_fun.8 = (f32[8,256,128]{2,1,0:T(8,128)S(1)}, f32[256,128]{1,0:T(8,128)S(1)}, f32[256,128]{1,0:T(8,128)S(1)}) custom-call(f32[8,256,128]{2,1,0:T(8,128)S(1)} %get-tuple-element.71.u_ref, f32[256,128]{1,0:T(8,128)S(1)} %collective-permute-done.3.sides_ref, f32[10,128]{1,0:T(8,128)S(1)} %collective-permute-done.4.before_ref, ...), custom_call_target="tpu_custom_call" | custom-call | tf_op jit(solution)/shard_map/cond/branch_1_fun/pallas_call | solution.py:547
  55.7 1.3 %collective-permute-start.6 = (f32[256,128]{1,0:T(8,128)S(1)}, f32[256,128]{1,0:T(8,128)S(1)}, u32[]{:S(2)}, u32[]{:S(2)}) collective-permute-start(f32[256,128]{1,0:T(8,128)S(1)} %get-tuple-element.75), channel_id=1, source_target_pairs={{0,1},{1,0},{2,3},{3,2},{4,5},{5,4},{6,7},{7,6},{8,9},{9,8},{10,11... | collective-permute-start | bytes 393224 | tf_op jit(solution)/shard_map/cond/branch_1_fun/ppermute | solution.py:391
  57.6 1.8 %branch_1_fun.10 = bf16[64,24,128]{2,1,0:T(8,128)(2,1)} custom-call(bf16[64,24,128]{2,1,0:T(8,128)(2,1)S(1)} %all-to-all-done.1.arrived_ref, f32[256,128]{1,0:T(8,128)S(1)} %get-tuple-element.78.base_ref), custom_call_target="tpu_custom_call" | custom-call | tf_op jit(solution)/shard_map/cond/branch_1_fun/pallas_call | solution.py:550
  59.4 6.6 %all-to-all-start.2 = ((bf16[64,24,128]{2,1,0:T(8,128)(2,1)}), bf16[64,24,128]{2,1,0:T(8,128)(2,1)S(1)}, u32[]{:S(2)}, u32[]{:S(2)}) async-start(bf16[64,24,128]{2,1,0:T(8,128)(2,1)} %branch_1_fun.10), calls=%async_computation.2 | async-start | bytes 786432 | tf_op jit(solution)/shard_map/cond/branch_1_fun/all_to_all | solution.py:504
  66.0 1.5 %collective-permute-start.7 = (f32[9,128]{1,0:T(8,128)S(1)}, f32[9,128]{1,0:T(8,128)S(1)}, u32[]{:S(2)}, u32[]{:S(2)}) collective-permute-start(f32[9,128]{1,0:T(8,128)S(1)} %pad_maximum_fusion.4), channel_id=1, source_target_pairs={{0,2},{2,4},{4,6},{6,8},{8,10},{10,12},{12,14},{14,16},{16,18},{18... | collective-permute-start | bytes 13832 | tf_op jit(solution)/shard_map/cond/branch_1_fun/ppermute | solution.py:394
  67.5 4.6 %collective-permute-start.8 = (f32[9,128]{1,0:T(8,128)S(1)}, f32[9,128]{1,0:T(8,128)S(1)}, u32[]{:S(2)}, u32[]{:S(2)}) collective-permute-start(f32[9,128]{1,0:T(8,128)S(1)} %pad_maximum_fusion.5), channel_id=1, source_target_pairs={{2,0},{4,2},{6,4},{8,6},{10,8},{12,10},{14,12},{16,14},{18,16},{20... | collective-permute-start | bytes 13832 | tf_op jit(solution)/shard_map/cond/branch_1_fun/ppermute | solution.py:394
  72.1 4.4 %collective-permute-done.7.before_ref = f32[9,128]{1,0:T(8,128)S(1)} collective-permute-done((f32[9,128]{1,0:T(8,128)S(1)}, f32[9,128]{1,0:T(8,128)S(1)}, u32[]{:S(2)}, u32[]{:S(2)}) %collective-permute-start.7) | collective-permute-done | bytes 4640 | tf_op jit(solution)/shard_map/cond/branch_1_fun/ppermute | solution.py:394
  76.5 2.2 %branch_1_fun.9 = f32[8,256,128]{2,1,0:T(8,128)} custom-call(f32[8,256,128]{2,1,0:T(8,128)S(1)} %get-tuple-element.74.u_ref, f32[256,128]{1,0:T(8,128)S(1)} %collective-permute-done.6.sides_ref, f32[9,128]{1,0:T(8,128)S(1)} %collective-permute-done.7.before_ref, f32[9,128]{1,0:T(8,128)S(1)} %collective-permute-done.8.after_ref), custom_call_target="tpu_custom_call" | custom-call | tf_op jit(solution)/shard_map/cond/branch_1_fun/pallas_call | solution.py:555
  78.7 17.1 %branch_1_fun.11 = f32[256,128]{1,0:T(8,128)} custom-call(s32[4,256]{1,0:T(4,128)S(1)} %get-tuple-element.76.pos_ref, bf16[64,24,128]{2,1,0:T(8,128)(2,1)S(1)} %all-to-all-done.2.arrived_ref, bf16[256,2,128,128]{3,2,1,0:T(8,128)(2,1)} %get-tuple-element.79.w_ref), custom_call_target="tpu_custom_call" | custom-call | tf_op jit(solution)/shard_map/cond/branch_1_fun/pallas_call | solution.py:488
  (32 shorter events, 3.7 us)
Async XLA Ops:
  1.5 25.8 %collective-permute-start.9 = (f32[256,128]{1,0:T(8,128)S(1)}, f32[256,128]{1,0:T(8,128)S(1)}, u32[]{:S(2)}, u32[]{:S(2)}) collective-permute-start(f32[256,128]{1,0:T(8,128)S(1)} %slice_bitcast_fusion.9), channel_id=1, source_target_pairs={{0,64},{1,65},{2,66},{3,67},{4,68},{5,69},{6,70},{7,71},{8,72},{9,... | collective-permute-start | bytes 393224 | tf_op jit(solution)/shard_map/ppermute | solution.py:522
  8.9 18.5 %collective-permute-start.10 = (bf16[2,256,128]{2,1,0:T(8,128)(2,1)S(1)}, bf16[2,256,128]{2,1,0:T(8,128)(2,1)S(1)}, u32[]{:S(2)}, u32[]{:S(2)}) collective-permute-start(bf16[2,256,128]{2,1,0:T(8,128)(2,1)S(1)} %fusion), channel_id=1, source_target_pairs={{64,0},{65,1},{66,2},{67,3},{68,4},{69,5},{70,6},{71,7},{72,8},{73... | collective-permute-start | bytes 393224 | tf_op jit(solution)/shard_map/ppermute | solution.py:523
  10.2 0.7 copy-start.1
  10.9 0.7 copy-start.2
  27.4 0.7 copy-start.8
  27.4 5.2 %copy-start.7 = (bf16[64,24,128]{2,1,0:T(8,128)(2,1)}, bf16[64,24,128]{2,1,0:T(8,128)(2,1)S(1)}, u32[]{:S(2)}) copy-start(bf16[64,24,128]{2,1,0:T(8,128)(2,1)S(1)} %get-tuple-element.77) | copy-start | bytes 1179652 | tf_op jit(solution)/shard_map/cond
  28.1 23.2 %copy-start.9 = (bf16[2,256,128]{2,1,0:T(8,128)(2,1)S(1)}, bf16[2,256,128]{2,1,0:T(8,128)(2,1)}, u32[]{:S(2)}) copy-start(bf16[2,256,128]{2,1,0:T(8,128)(2,1)} %copy-done.8) | copy-start | bytes 393220 | tf_op jit(solution)/shard_map/cond
  31.6 10.9 %collective-permute-start.3 = (f32[256,128]{1,0:T(8,128)S(1)}, f32[256,128]{1,0:T(8,128)S(1)}, u32[]{:S(2)}, u32[]{:S(2)}) collective-permute-start(f32[256,128]{1,0:T(8,128)S(1)} %get-tuple-element.72), channel_id=1, source_target_pairs={{0,1},{1,0},{2,3},{3,2},{4,5},{5,4},{6,7},{7,6},{8,9},{9,8},{10,11... | collective-permute-start | bytes 393224 | tf_op jit(solution)/shard_map/cond/branch_1_fun/ppermute | solution.py:391
  32.6 25.0 %all-to-all-start.1 = ((bf16[64,24,128]{2,1,0:T(8,128)(2,1)}), bf16[64,24,128]{2,1,0:T(8,128)(2,1)S(1)}, u32[]{:S(2)}, u32[]{:S(2)}) async-start(bf16[64,24,128]{2,1,0:T(8,128)(2,1)} %copy-done.7), calls=%async_computation.1 | async-start | bytes 786432 | tf_op jit(solution)/shard_map/cond/branch_1_fun/all_to_all | solution.py:504
  40.9 10.5 %copy-start.6 = (s32[6,256,128]{2,1,0:T(8,128)S(1)}, s32[6,256,128]{2,1,0:T(8,128)}, u32[]{:S(2)}) copy-start(s32[6,256,128]{2,1,0:T(8,128)} %get-tuple-element.73.table_ref) | copy-start | bytes 2359300 | tf_op jit(solution)/shard_map/cond
  42.5 8.9 %collective-permute-start.4 = (f32[10,128]{1,0:T(8,128)S(1)}, f32[10,128]{1,0:T(8,128)S(1)}, u32[]{:S(2)}, u32[]{:S(2)}) collective-permute-start(f32[10,128]{1,0:T(8,128)S(1)} %pad_maximum_fusion.2), channel_id=1, source_target_pairs={{0,2},{2,4},{4,6},{6,8},{8,10},{10,12},{12,14},{14,16},{16,18},{18... | collective-permute-start | bytes 15368 | tf_op jit(solution)/shard_map/cond/branch_1_fun/ppermute | solution.py:394
  43.9 7.4 %collective-permute-start.5 = (f32[10,128]{1,0:T(8,128)S(1)}, f32[10,128]{1,0:T(8,128)S(1)}, u32[]{:S(2)}, u32[]{:S(2)}) collective-permute-start(f32[10,128]{1,0:T(8,128)S(1)} %pad_maximum_fusion.3), channel_id=1, source_target_pairs={{2,0},{4,2},{6,4},{8,6},{10,8},{12,10},{14,12},{16,14},{18,16},{20... | collective-permute-start | bytes 15368 | tf_op jit(solution)/shard_map/cond/branch_1_fun/ppermute | solution.py:394
  55.7 10.3 %collective-permute-start.6 = (f32[256,128]{1,0:T(8,128)S(1)}, f32[256,128]{1,0:T(8,128)S(1)}, u32[]{:S(2)}, u32[]{:S(2)}) collective-permute-start(f32[256,128]{1,0:T(8,128)S(1)} %get-tuple-element.75), channel_id=1, source_target_pairs={{0,1},{1,0},{2,3},{3,2},{4,5},{5,4},{6,7},{7,6},{8,9},{9,8},{10,11... | collective-permute-start | bytes 393224 | tf_op jit(solution)/shard_map/cond/branch_1_fun/ppermute | solution.py:391
  59.4 19.2 %all-to-all-start.2 = ((bf16[64,24,128]{2,1,0:T(8,128)(2,1)}), bf16[64,24,128]{2,1,0:T(8,128)(2,1)S(1)}, u32[]{:S(2)}, u32[]{:S(2)}) async-start(bf16[64,24,128]{2,1,0:T(8,128)(2,1)} %branch_1_fun.10), calls=%async_computation.2 | async-start | bytes 786432 | tf_op jit(solution)/shard_map/cond/branch_1_fun/all_to_all | solution.py:504
  66.0 10.4 %collective-permute-start.7 = (f32[9,128]{1,0:T(8,128)S(1)}, f32[9,128]{1,0:T(8,128)S(1)}, u32[]{:S(2)}, u32[]{:S(2)}) collective-permute-start(f32[9,128]{1,0:T(8,128)S(1)} %pad_maximum_fusion.4), channel_id=1, source_target_pairs={{0,2},{2,4},{4,6},{6,8},{8,10},{10,12},{12,14},{14,16},{16,18},{18... | collective-permute-start | bytes 13832 | tf_op jit(solution)/shard_map/cond/branch_1_fun/ppermute | solution.py:394
  67.5 9.0 %collective-permute-start.8 = (f32[9,128]{1,0:T(8,128)S(1)}, f32[9,128]{1,0:T(8,128)S(1)}, u32[]{:S(2)}, u32[]{:S(2)}) collective-permute-start(f32[9,128]{1,0:T(8,128)S(1)} %pad_maximum_fusion.5), channel_id=1, source_target_pairs={{2,0},{4,2},{6,4},{8,6},{10,8},{12,10},{14,12},{16,14},{18,16},{20... | collective-permute-start | bytes 13832 | tf_op jit(solution)/shard_map/cond/branch_1_fun/ppermute | solution.py:394

commit v2 on v1

v2 whole, which is shorter than its diff:
```python
import functools

import jax
import jax.numpy as jnp
import numpy as np
from jax import lax
from jax.experimental import pallas as pl
from jax.experimental.pallas import tpu as pltpu
from jax.sharding import PartitionSpec as P

ATMOS_DIFFUSION = 0.01
MIXING = 0.2
OCEAN_DIFFUSION = 0.12

RANKS = 64
CAP = 18
LEV = 8
NF = 8
ROWS = 256
COLS = 128
K = 2
OCEAN_SLOTS = 19
ATMOS_SLOTS = 24

VMEM = pl.BlockSpec(memory_space=pltpu.VMEM)
SMEM = pl.BlockSpec(memory_space=pltpu.SMEM)
ANY = pl.BlockSpec(memory_space=pl.ANY)
F32 = jnp.float32
BF16 = jnp.bfloat16


def second_table():
    gll_nodes = np.array([-1.0, -1.0 / np.sqrt(5.0), 1.0 / np.sqrt(5.0), 1.0])
    poly_order = 3
    legendre = (5.0 * gll_nodes**3 - 3.0 * gll_nodes) / 2.0
    derivative = np.zeros((4, 4))
    for row_index in range(4):
        for col_index in range(4):
            if row_index != col_index:
                derivative[row_index, col_index] = legendre[row_index] / (
                    legendre[col_index] * (gll_nodes[row_index] - gll_nodes[col_index])
                )
    derivative[0, 0] = -poly_order * (poly_order + 1) / 4.0
    derivative[3, 3] = poly_order * (poly_order + 1) / 4.0
    return derivative @ derivative


SECOND = second_table()


def call(body, out_shape, specs, **params):
    return pl.pallas_call(
        body,
        out_shape=out_shape,
        in_specs=specs,
        out_specs=jax.tree.map(lambda _: VMEM, out_shape),
        compiler_params=pltpu.CompilerParams(vmem_limit_bytes=params.pop("vmem", 24 << 20)),
        **params,
    )


def shadow_call(body, out_shape, specs, **params):
    nothing = pl.CostEstimate(flops=0, bytes_accessed=0, transcendentals=0)
    return call(body, out_shape, specs, cost_estimate=nothing, **params)


def positions_body(peer_ref, line_ref, pos_ref, label_ref):
    count = ROWS * K
    peer = jnp.concatenate([peer_ref[k : k + 1, :] for k in range(K)], axis=1)
    line = jnp.concatenate([line_ref[k : k + 1, :] for k in range(K)], axis=1)
    hits = lax.broadcasted_iota(jnp.int32, (RANKS, count), 0) == peer
    hits_f = jnp.where(hits, 1.0, 0.0)
    earlier = lax.broadcasted_iota(jnp.int32, (count, count), 0) < lax.broadcasted_iota(
        jnp.int32, (count, count), 1
    )
    before = jnp.dot(
        hits_f.astype(BF16),
        jnp.where(earlier, 1.0, 0.0).astype(BF16),
        preferred_element_type=F32,
    )
    slot = jnp.sum(hits_f * before, axis=0, keepdims=True).astype(jnp.int32)
    for width, at in ((OCEAN_SLOTS, 0), (ATMOS_SLOTS, K)):
        position = peer * width + slot
        for k in range(K):
            pos_ref[at + k : at + k + 1, :] = position[:, k * ROWS : (k + 1) * ROWS]
    slot_hits = lax.broadcasted_iota(jnp.int32, (COLS, count), 0) == slot
    shifted = jnp.where(hits, (line + 1).astype(F32), 0.0).astype(BF16)
    label_ref[...] = (
        lax.dot_general(
            shifted,
            jnp.where(slot_hits, 1.0, 0.0).astype(BF16),
            (((1,), (1,)), ((), ())),
            preferred_element_type=F32,
        )
        - 1.0
    )


def positions(peer, line):
    return call(
        positions_body,
        (
            jax.ShapeDtypeStruct((2 * K, ROWS), jnp.int32),
            jax.ShapeDtypeStruct((RANKS, COLS), F32),
        ),
        [VMEM, VMEM],
    )(peer.T, line.T)


FLUX_ROWS = 16
REMAP_ROWS = 32


def weight_copies(source, held, sems, per):
    def copy(c):
        part = pl.ds(c * per, per)
        return pltpu.make_async_copy(source.at[part], held.at[part], sems.at[c])

    return copy


def side_by_side(held, b):
    return jnp.concatenate([held[b, k] for k in range(K)], axis=1)


def ocean_flux_body(
    pos_ref, label_ref, air_ref, prior_ref, factor_ref, w_ref, out_ref, held, rows, sems
):
    copy = weight_copies(w_ref, held, sems, FLUX_ROWS)
    for c in range(ROWS // FLUX_ROWS):
        copy(c).start()
    out_ref[...] = jnp.zeros_like(out_ref)
    for d in range(RANKS):
        out_ref[d * OCEAN_SLOTS + CAP] = jnp.broadcast_to(
            label_ref[d : d + 1, :], (NF, COLS)
        ).astype(BF16)
    difference = air_ref[...] - prior_ref[...]
    for f in range(NF):
        rows[pl.ds(f, ROWS, stride=NF), :] = factor_ref[f] * difference

    @pl.loop(0, ROWS // FLUX_ROWS)
    def _(c):
        copy(c).wait()
        for i in range(FLUX_ROWS):
            b = c * FLUX_ROWS + i
            flux = rows[pl.ds(pl.multiple_of(b * NF, NF), NF), :].astype(BF16)
            part = jnp.dot(flux, side_by_side(held, b), preferred_element_type=F32).astype(BF16)
            for k in range(K):
                out_ref[pos_ref[k, b]] = part[:, k * COLS : (k + 1) * COLS]


WEIGHTS_HELD = [
    pltpu.VMEM((ROWS, K, COLS, COLS), BF16),
]


def ocean_flux(pos, labels, air, prior, factors, weights):
    return pl.pallas_call(
        ocean_flux_body,
        out_shape=jax.ShapeDtypeStruct((RANKS * OCEAN_SLOTS, NF, COLS), BF16),
        in_specs=[SMEM, VMEM, VMEM, VMEM, VMEM, ANY],
        out_specs=VMEM,
        scratch_shapes=WEIGHTS_HELD
        + [
            pltpu.VMEM((ROWS * NF, COLS), F32),
            pltpu.SemaphoreType.DMA((ROWS // FLUX_ROWS,)),
        ],
        compiler_params=pltpu.CompilerParams(vmem_limit_bytes=32 << 20),
    )(pos, labels, air, prior, factors, weights)


def atmos_flux_body(
    pos_ref,
    label_ref,
    air_ref,
    prior_ref,
    factor_ref,
    w_ref,
    share_ref,
    out_ref,
    held,
    packed,
    rows,
    sems,
):
    copy = weight_copies(w_ref, held, sems, FLUX_ROWS)
    for c in range(ROWS // FLUX_ROWS):
        copy(c).start()
    packed[...] = jnp.zeros_like(packed)
    for d in range(RANKS):
        packed[d * ATMOS_SLOTS + CAP : d * ATMOS_SLOTS + CAP + 1, :] = label_ref[d : d + 1, :]
    mixed = share_ref[0, 0] * factor_ref[0]
    for f in range(1, NF):
        mixed += share_ref[0, f] * factor_ref[f]
    flux = mixed * (air_ref[...] - prior_ref[...])
    high = flux.astype(BF16).astype(F32)
    rows[...] = jnp.zeros_like(rows)
    rows[pl.ds(0, ROWS, stride=8), :] = high
    rows[pl.ds(1, ROWS, stride=8), :] = flux - high

    @pl.loop(0, ROWS // FLUX_ROWS)
    def _(c):
        copy(c).wait()
        for i in range(FLUX_ROWS):
            b = c * FLUX_ROWS + i
            pair = rows[pl.ds(pl.multiple_of(b * 8, 8), 8), :].astype(BF16)
            part = jnp.dot(pair, side_by_side(held, b), preferred_element_type=F32)
            part = part[0:1, :] + part[1:2, :]
            for k in range(K):
                packed[pl.ds(pos_ref[K + k, b], 1), :] = part[:, k * COLS : (k + 1) * COLS]

    out_ref[...] = packed[...].astype(BF16).reshape(RANKS, ATMOS_SLOTS, COLS)


def atmos_flux(pos, labels, air, prior, factors, weights, share):
    return pl.pallas_call(
        atmos_flux_body,
        out_shape=jax.ShapeDtypeStruct((RANKS, ATMOS_SLOTS, COLS), BF16),
        in_specs=[SMEM, VMEM, VMEM, VMEM, VMEM, ANY, SMEM],
        out_specs=VMEM,
        scratch_shapes=WEIGHTS_HELD
        + [
            pltpu.VMEM((RANKS * ATMOS_SLOTS, COLS), F32),
            pltpu.VMEM((ROWS * 8, COLS), F32),
            pltpu.SemaphoreType.DMA((ROWS // FLUX_ROWS,)),
        ],
        compiler_params=pltpu.CompilerParams(vmem_limit_bytes=32 << 20),
    )(pos, labels, air, prior, factors, weights, share)


WIDE = 8
EXTENDED = ROWS + 2 * WIDE


def iotas(rows):
    return (
        lax.broadcasted_iota(jnp.int32, (rows, COLS), 0),
        lax.broadcasted_iota(jnp.int32, (rows, COLS), 1),
    )


def turned(field, lanes):
    lanes = lanes % COLS
    return field if lanes == 0 else pltpu.roll(field, lanes, 1)


def sides_body(u_ref, out_ref):
    _, lane = iotas(ROWS)
    packed = jnp.zeros((ROWS, COLS), F32)
    for l in range(LEV):
        packed = jnp.where(lane // (2 * WIDE) == l, turned(u_ref[l], WIDE + 2 * WIDE * l), packed)
    out_ref[...] = packed


def mate_ends(sides, level):
    return turned(sides, -(2 * WIDE * level + WIDE))


def column_left(field, ends, lane):
    return pltpu.roll(jnp.where(lane == COLS - 1, ends, field), 1, 1)


def column_right(field, ends, lane):
    return pltpu.roll(jnp.where(lane == 0, ends, field), COLS - 1, 1)


def second_along(field, axis, index, extent):
    phase = index % 4
    total = None
    for shift in range(-3, 4):
        factor = jnp.zeros(index.shape, F32)
        for p in range(4):
            if 0 <= p + shift < 4:
                factor = jnp.where(phase == p, F32(SECOND[p, p + shift]), factor)
        moved = field if shift == 0 else pltpu.roll(field, (-shift) % extent, axis)
        total = factor * moved if total is None else total + factor * moved
    return total


def diffused(field, above, below, row, lane):
    along = second_along(field, 0, row, EXTENDED) + second_along(field, 1, lane, COLS)
    return field + ATMOS_DIFFUSION * along + MIXING * (above + below - 2.0 * field)


def assembled(field, axis, phase, ahead, behind):
    return jnp.where(
        phase == 3,
        0.5 * (field + ahead),
        jnp.where(phase == 0, 0.5 * (field + behind), field),
    )


def assembled_rows(field, row):
    ahead = pltpu.roll(field, EXTENDED - 1, 0)
    return assembled(field, 0, row % 4, ahead, pltpu.roll(field, 1, 0))


def substeps_body(u_ref, sides_ref, before_ref, after_ref, _, out_ref, main, moved):
    row, lane = iotas(EXTENDED)
    phase, part = lane % 4, lane % (2 * WIDE)
    for l in range(LEV):
        main[l, :WIDE] = before_ref[l]
        main[l, WIDE : WIDE + ROWS] = u_ref[l]
        main[l, WIDE + ROWS :] = after_ref[l]
    sides = jnp.concatenate([before_ref[LEV], sides_ref[...], after_ref[LEV]], axis=0)
    for substep in range(2):
        over = jnp.where(lane < COLS - 2 * WIDE, turned(sides, -2 * WIDE), sides)
        under = jnp.where(lane >= 2 * WIDE, turned(sides, 2 * WIDE), sides)
        sides = assembled_rows(diffused(sides, over, under, row, lane), row)
        edges = jnp.zeros((EXTENDED, COLS), F32)
        for l in range(LEV):
            field = main[l]
            half = assembled_rows(
                diffused(field, main[min(l + 1, LEV - 1)], main[max(l - 1, 0)], row, lane), row
            )
            if substep == 0:
                first = turned(half, 2 * WIDE * l + WIDE - 1)
                last = turned(half, 2 * WIDE * l + WIDE + 1)
                own_level = lane // (2 * WIDE) == l
                edges = jnp.where(own_level, jnp.where(part < WIDE, first, last), edges)
            ends = mate_ends(sides, l)
            whole = assembled(
                half, 1, phase, column_right(half, ends, lane), column_left(half, ends, lane)
            )
            if substep == 0:
                moved[l] = whole
            else:
                out_ref[l] = whole[WIDE : WIDE + ROWS]
        if substep == 0:
            ahead = jnp.where(part == WIDE - 1, edges, turned(sides, -1))
            behind = jnp.where(part == WIDE, edges, turned(sides, 1))
            sides = assembled(sides, 1, phase, ahead, behind)
            for l in range(LEV):
                main[l] = moved[l]


ORDER = [(dr, dc) for dr in (-1, 0, 1) for dc in (-1, 0, 1) if dr or dc]


def neighbour_counts(table_ref, row, lane):
    own = (row + 1) * (COLS + 2) + lane + 1
    counts = []
    for dr, dc in ORDER:
        target = own + (dr * (COLS + 2) + dc)
        count = jnp.zeros((ROWS, COLS), F32)
        for e in range(table_ref.shape[0]):
            count += jnp.where(table_ref[e] == target, 1.0, 0.0)
        counts.append(count)
    return counts


def neighbour_spread(field, ends, before, after, ends_before, ends_after, counts, row, lane):
    total = jnp.zeros((ROWS, COLS), F32)
    lines = {
        0: (field, ends),
        -1: tuple(
            jnp.where(row == 0, edge, pltpu.roll(v, 1, 0))
            for v, edge in ((field, before), (ends, ends_before))
        ),
        1: tuple(
            jnp.where(row == ROWS - 1, edge, pltpu.roll(v, ROWS - 1, 0))
            for v, edge in ((field, after), (ends, ends_after))
        ),
    }
    for (dr, dc), count in zip(ORDER, counts):
        line, line_ends = lines[dr]
        if dc == -1:
            line = column_left(line, line_ends, lane)
        elif dc == 1:
            line = column_right(line, line_ends, lane)
        total += count * (line - field)
    return total


def top_base_body(top_ref, under_ref, mate_ref, before_ref, after_ref, table_ref, out_ref):
    row, lane = iotas(ROWS)
    top = top_ref[...]
    spread = neighbour_spread(
        top,
        mate_ref[...],
        before_ref[LEV + 1, WIDE - 1 :, :],
        after_ref[LEV + 1, :1, :],
        before_ref[LEV + 2, WIDE - 1 :, :],
        after_ref[LEV + 2, :1, :],
        neighbour_counts(table_ref, row, lane),
        row,
        lane,
    )
    out_ref[...] = top + OCEAN_DIFFUSION * spread + MIXING * (under_ref[...].astype(F32) - top)


def ocean_base_body(o_ref, sides_ref, before_ref, after_ref, table_ref, out_ref, counts_ref):
    row, lane = iotas(ROWS)
    for n, count in enumerate(neighbour_counts(table_ref, row, lane)):
        counts_ref[n] = count
    for l in range(LEV):
        field = o_ref[l]
        spread = neighbour_spread(
            field,
            mate_ends(sides_ref[...], l),
            before_ref[l, WIDE - 1 :, :],
            after_ref[l, :1, :],
            mate_ends(before_ref[LEV, WIDE - 1 :, :], l),
            mate_ends(after_ref[LEV, :1, :], l),
            [counts_ref[n] for n in range(len(ORDER))],
            row,
            lane,
        )
        below, above = o_ref[max(l - 1, 0)], o_ref[min(l + 1, LEV - 1)]
        out_ref[l] = field + OCEAN_DIFFUSION * spread + MIXING * (above + below - 2.0 * field)


def exchanged(levels, planes):
    size = lax.axis_size("gx")
    up = [(i, (i + 1) % size) for i in range(size)]
    down = [(j, i) for i, j in up]
    mate = lax.ppermute(planes, "gy", [(0, 1), (1, 0)])
    parts = [levels, mate[:1], planes[1:], mate[1:]]
    last = jnp.concatenate([v[:, ROWS - WIDE :, :] for v in parts], axis=0)
    first = jnp.concatenate([v[:, :WIDE, :] for v in parts], axis=0)
    return mate, lax.ppermute(last, "gx", up), lax.ppermute(first, "gx", down)


def row_hits(labels):
    width = ATMOS_SLOTS
    shape = (RANKS, width, COLS)
    diagonal = lax.broadcasted_iota(jnp.int32, shape, 1) == lax.broadcasted_iota(jnp.int32, shape, 2)
    spread = jnp.where(diagonal, labels[:, None, :], 0.0)
    column = jnp.sum(spread, axis=2, keepdims=True).reshape(RANKS * width, 1)
    slot = lax.broadcasted_iota(jnp.int32, (RANKS, width, 1), 1).reshape(RANKS * width, 1)
    column = jnp.where(slot < CAP, column, -1.0).astype(jnp.int32)
    rows = lax.broadcasted_iota(jnp.int32, (RANKS * width, ROWS), 1)
    return jnp.where(column == rows, 1.0, 0.0).astype(BF16)


def top_body(arrived_ref, base_ref, out_ref):
    arrived = arrived_ref[...].astype(F32)
    hits = row_hits(arrived[:, CAP, :])
    values = arrived.reshape(RANKS * ATMOS_SLOTS, COLS).astype(BF16)
    pushed = lax.dot_general(hits, values, (((0,), (0,)), ((), ())), preferred_element_type=F32)
    top = (base_ref[...] + pushed).astype(BF16)
    picked = jnp.dot(hits, top, preferred_element_type=F32)
    out_ref[...] = picked.astype(BF16).reshape(RANKS, ATMOS_SLOTS, COLS)


def sums_body(arrived_ref, base_ref, share_ref, out_ref, first_ref, wide):
    width = OCEAN_SLOTS * NF
    wide[...] = arrived_ref[...].astype(F32).reshape(RANKS * width, COLS)
    labels = wide[pl.ds(CAP * NF, RANKS, stride=width), :]
    by_slot = jnp.concatenate([labels, labels], axis=0).T
    row = lax.broadcasted_iota(jnp.int32, (ROWS, COLS), 0).astype(F32)
    lane = lax.broadcasted_iota(jnp.int32, (1, COLS), 1)
    pieces = []
    for s in range(0, CAP, 2):
        pair = jnp.where(lane < RANKS, by_slot[s : s + 1, :], by_slot[s + 1 : s + 2, :])
        pieces.append(jnp.where(row == pair, 1.0, 0.0).astype(BF16))
    hits = jnp.concatenate(pieces, axis=1)
    for f in range(NF):
        values = jnp.concatenate(
            [wide[pl.ds(s * NF + f, RANKS, stride=width), :] for s in range(CAP)], axis=0
        ).astype(BF16)
        forcing = jnp.dot(hits, values, preferred_element_type=F32)
        if f == 0:
            first_ref[...] = forcing
        for l in range(LEV):
            before = base_ref[l] if f == 0 else out_ref[l]
            out_ref[l] = before + share_ref[l, f] * forcing


def ocean_sums(arrived, base, share):
    return pl.pallas_call(
        sums_body,
        out_shape=(
            jax.ShapeDtypeStruct((LEV, ROWS, COLS), F32),
            jax.ShapeDtypeStruct((ROWS, COLS), F32),
        ),
        in_specs=[VMEM, VMEM, SMEM],
        out_specs=(VMEM, VMEM),
        scratch_shapes=[pltpu.VMEM((RANKS * OCEAN_SLOTS * NF, COLS), F32)],
        compiler_params=pltpu.CompilerParams(vmem_limit_bytes=24 << 20),
    )(arrived, base, share)


def remap_body(pos_ref, arrived_ref, w_ref, out_ref, held, wide, near, sems):
    copy = weight_copies(w_ref, held, sems, REMAP_ROWS)
    for c in range(ROWS // REMAP_ROWS):
        copy(c).start()
    wide[...] = arrived_ref[...].astype(F32).reshape(RANKS * ATMOS_SLOTS, COLS)
    lane = lax.broadcasted_iota(jnp.int32, (COLS, REMAP_ROWS), 1)

    @pl.loop(0, ROWS // REMAP_ROWS)
    def _(c):
        for i in range(REMAP_ROWS):
            for k in range(K):
                value = wide[pl.ds(pos_ref[K + k, c * REMAP_ROWS + i], 1), :]
                near[i : i + 1, k * COLS : (k + 1) * COLS] = value
        values = near[...].astype(BF16)
        copy(c).wait()
        block = held.at[pl.ds(c * REMAP_ROWS, REMAP_ROWS)]
        tiles = jnp.concatenate(
            [block[:, k].reshape(REMAP_ROWS * COLS, COLS) for k in range(K)], axis=1
        )
        crossed = lax.dot_general(
            tiles, values, (((1,), (1,)), ((), ())), preferred_element_type=F32
        )
        own = jnp.zeros((COLS, REMAP_ROWS), F32)
        for i in range(REMAP_ROWS):
            own = jnp.where(lane == i, crossed[i * COLS : (i + 1) * COLS], own)
        out_ref[pl.ds(pl.multiple_of(c * REMAP_ROWS, REMAP_ROWS), REMAP_ROWS), :] = own.T


def remap(pos, arrived, weights):
    return pl.pallas_call(
        remap_body,
        out_shape=jax.ShapeDtypeStruct((ROWS, COLS), F32),
        in_specs=[SMEM, VMEM, ANY],
        out_specs=VMEM,
        scratch_shapes=WEIGHTS_HELD
        + [
            pltpu.VMEM((RANKS * ATMOS_SLOTS, COLS), F32),
            pltpu.VMEM((REMAP_ROWS, K * COLS), F32),
            pltpu.SemaphoreType.DMA((ROWS // REMAP_ROWS,)),
        ],
        compiler_params=pltpu.CompilerParams(vmem_limit_bytes=32 << 20),
    )(pos, arrived, weights)


def to_peers(payload):
    return lax.all_to_all(payload, ("gx", "gy"), split_axis=0, concat_axis=0, tiled=True)


def local(
    layered_heat_profile,
    prior_marine_heat,
    transfer_factor_table,
    depth_fraction_matrix,
    adjacent_cell_table,
    destination_water_peer,
    destination_water_line,
    interpolation_matrix_blocks,
):
    is_atmosphere_side = lax.axis_index("comp") == 0
    own = layered_heat_profile[0]
    block = jax.ShapeDtypeStruct((LEV, ROWS, COLS), F32)
    plane = jax.ShapeDtypeStruct((ROWS, COLS), F32)
    swap = [(0, 1), (1, 0)]

    other_top = lax.ppermute(own[0], "comp", swap)
    other_under = lax.ppermute(own[1].astype(BF16), "comp", swap)
    pos, labels = positions(destination_water_peer, destination_water_line)

    def sides_of(levels):
        return shadow_call(sides_body, plane, [VMEM])(levels)

    def atmosphere_early():
        packed = atmos_flux(
            pos,
            labels,
            own[0],
            prior_marine_heat,
            transfer_factor_table,
            interpolation_matrix_blocks,
            depth_fraction_matrix,
        )
        rows = jnp.zeros((LEV + 1, WIDE, COLS), F32)
        return packed, jnp.zeros((1, ROWS, COLS), F32), rows, rows

    def ocean_early():
        halo = exchanged(own, sides_of(own)[None])
        return jnp.zeros((RANKS, ATMOS_SLOTS, COLS), BF16), *halo

    packed, *ocean_halo = lax.cond(is_atmosphere_side, atmosphere_early, ocean_early)

    def atmosphere():
        arrived = to_peers(packed)
        mate, before, after = exchanged(own, jnp.stack([sides_of(own), other_top]))
        base = shadow_call(top_base_body, plane, [VMEM] * 6)(
            other_top, other_under, mate[1], before, after, adjacent_cell_table
        )
        picked = call(
            top_body, jax.ShapeDtypeStruct((RANKS, ATMOS_SLOTS, COLS), BF16), [VMEM, VMEM]
        )(arrived, base)
        returned = to_peers(picked)
        wide = pltpu.VMEM((LEV, EXTENDED, COLS), F32)
        final = shadow_call(
            substeps_body, block, [VMEM] * 4 + [ANY], scratch_shapes=[wide, wide]
        )(own, mate[0], before, after, picked)
        return final, remap(pos, returned, interpolation_matrix_blocks)

    def ocean():
        payload = ocean_flux(
            pos,
            labels,
            other_top,
            prior_marine_heat,
            transfer_factor_table,
            interpolation_matrix_blocks,
        )
        arrived = to_peers(payload.reshape(RANKS, OCEAN_SLOTS * NF, COLS))
        mate, before, after = ocean_halo
        base = shadow_call(
            ocean_base_body,
            block,
            [VMEM] * 5,
            scratch_shapes=[pltpu.VMEM((len(ORDER), ROWS, COLS), F32)],
        )(own, mate[0], before, after, adjacent_cell_table)
        return ocean_sums(
            arrived.reshape(RANKS * OCEAN_SLOTS, NF, COLS), base, depth_fraction_matrix
        )

    state, plane_out = lax.cond(is_atmosphere_side, atmosphere, ocean)
    return state[None], plane_out[None]


def solution(mesh):
    return jax.shard_map(
        local,
        mesh=mesh,
        in_specs=(
            P("comp", None, "gx", "gy"),
            P("gx", "gy"),
            P(None, "gx", "gy"),
            P(),
            P(None, "gx", "gy"),
            P(("gx", "gy"), None),
            P(("gx", "gy"), None),
            P(("gx", "gy"), None, None, None),
        ),
        out_specs=(P("comp", None, "gx", "gy"), P("comp", "gx", "gy")),
        check_vma=False,
    )
```

time: 96.8 us -> 75.9 us (0.78)
  starting transfers between devices: 36.8 us -> 26 us
  Pallas kernels: 43.8 us -> 33.6 us
  local copies, waits for them, and re-layouts: 6.06 us -> 4.88 us
    ppermute x8 -> x5, starting transfers between devices: 22 us -> 11.5 us  [the longest x2 5.98 us: exchanged(): return (mate, lax.ppermute(last, 'gx', up), lax.ppermute(first, 'gx', down))]
    pallas_call x5, Pallas kernels: 41.6 us -> 31.4 us  [the longest x1 10 us: atmosphere(): shadow_call(substeps_body, block, [VMEM] * 4 + [ANY], scratch_shapes=[wid...]
    pallas_call x2 -> x0, local copies, waits for them, and re-layouts: 1.22 us -> none  [the longest x1 0.61 us: atmosphere(): call(atmos_first_body, (block, plane), [VMEM, VMEM])(own, sea)]
    ppermute x8 -> x5, waiting for transfers between devices: 7.16 us -> 7.1 us  [the longest x2 7.09 us: exchanged(): return (mate, lax.ppermute(last, 'gx', up), lax.ppermute(first, 'gx', down))]
  transfers between devices with their start and end apart: 10 -> 7, of which waited for: 2 -> 3; matrix products, arithmetic and copies ran while one was open for 4% -> 3% of each run, Pallas kernels for 24% -> 28%
where the time goes in v2:
time: 75.9 us; the launch traced here: 74.6 us
  Pallas kernels  33.6 us (44%)
  starting transfers between devices  26 us (34%)
  waiting for transfers between devices  8.01 us (11%)
  local copies, waits for them, and re-layouts  4.88 us (6%)
  other arithmetic  0.93 us (1%)
  between operations  0.86 us (1%)
    all_to_all x2, starting transfers between devices, to_peers(): lax.all_to_all(payload, ('gx', 'gy'), split_axis=0, concat_axis=0, tiled=...  14.4 us
    pallas_call x1, Pallas kernels, atmosphere(): shadow_call(substeps_body, block, [VMEM] * 4 + [ANY], scratch_shapes=[wid...  10 us
    pallas_call x1, Pallas kernels, remap(): pl.pallas_call(remap_body, out_shape=jax.ShapeDtypeStruct((ROWS, COLS), F...  9.49 us
    pallas_call x1, Pallas kernels, atmos_flux(): pl.pallas_call(atmos_flux_body, out_shape=jax.ShapeDtypeStruct((RANKS, AT...  8.31 us
    ppermute x2, waiting for transfers between devices, exchanged(): return (mate, lax.ppermute(last, 'gx', up), lax.ppermute(first, 'gx', down))  7.09 us
    ppermute x2, starting transfers between devices, exchanged(): return (mate, lax.ppermute(last, 'gx', up), lax.ppermute(first, 'gx', down))  5.98 us
    ppermute x1, starting transfers between devices, local(): other_top = lax.ppermute(own[0], 'comp', swap)  4.51 us
    pallas_call x1, Pallas kernels, atmosphere(): shadow_call(top_base_body, plane, [VMEM] * 6)  1.84 us
  transfers between devices with their start and end apart: 7, of which 3 were waited for; matrix products, arithmetic and copies ran while one was open for 3% of the time, Pallas kernels for 28%

profile of v2, /device:TPU:1, one launch (start us, length us, event | category | flops | bytes accessed | tf_op | source)
XLA Modules:
  0.0 74.6 jit_solution(5101083392472175541)
XLA Ops:
  0.6 0.9 %slice_bitcast_fusion.3 = f32[256,128]{1,0:T(8,128)S(1)} fusion(f32[1,8,256,128]{3,2,1,0:T(8,128)} %param.12), kind=kLoop, calls=%fused_computation.9 | loop fusion | bytes 262144 | tf_op jit(solution)/shard_map/squeeze | solution.py:548
  1.5 4.5 %collective-permute-start.6 = (f32[256,128]{1,0:T(8,128)S(1)}, f32[256,128]{1,0:T(8,128)}, u32[]{:S(2)}, u32[]{:S(2)}) collective-permute-start(f32[256,128]{1,0:T(8,128)S(1)} %slice_bitcast_fusion.3), channel_id=1, source_target_pairs={{0,64},{64,0},{1,65},{65,1},{2,66},{66,2},{3,67},{67,3},{4,68},{68... | collective-permute-start | bytes 393224 | tf_op jit(solution)/shard_map/ppermute | solution.py:548
  6.1 0.9 %fusion = bf16[256,128]{1,0:T(8,128)(2,1)S(1)} fusion(f32[1,8,256,128]{3,2,1,0:T(8,128)} %param.12), kind=kLoop, calls=%fused_computation.10 | loop fusion | bytes 131072 | tf_op jit(solution)/shard_map/convert_element_type | solution.py:549
  7.0 0.7 copy-done.1
  7.7 0.7 copy-done.2
  8.3 0.4 shard_map.95
  8.7 9.3 %conditional.2 = (bf16[64,24,128]{2,1,0:T(8,128)(2,1)}, f32[1,256,128]{2,1,0:T(8,128)S(1)}, f32[9,8,128]{2,1,0:T(8,128)S(1)}, f32[9,8,128]{2,1,0:T(8,128)S(1)}) conditional(s32[]{:T(128)} %convert_element_type.8, f32[8,256,128]{2,1,0:T(8,128)} %bitcast.29, (f32[8,256,128]{2,1,0:T(8,128)}, s32[4,256]{1,0:T(4,128)S(1)}, f32[64,128]{1,0:T(8,128)S(1)}, ...), branch_computations={%region_0.0_spmd, %region_1.0_spmd} | conditional | flops 18432 | bytes 1507482 | solution.py:572
  8.8 0.9 %slice_bitcast_fusion.air_ref = f32[256,128]{1,0:T(8,128)S(1)} fusion(f32[8,256,128]{2,1,0:T(8,128)} %get-tuple-element.59), kind=kLoop, calls=%fused_computation.2 | loop fusion | bytes 262144 | tf_op jit(solution)/shard_map/cond/branch_1_fun/squeeze | solution.py:559
  9.7 8.3 %branch_1_fun.6 = bf16[64,24,128]{2,1,0:T(8,128)(2,1)} custom-call(s32[4,256]{1,0:T(4,128)S(1)} %get-tuple-element.57.pos_ref, f32[64,128]{1,0:T(8,128)S(1)} %get-tuple-element.58.label_ref, f32[256,128]{1,0:T(8,128)S(1)} %slice_bitcast_fusion.air_ref, f32[256,128]{1,0:T(8,128)} %get-tuple-element.60.prior_ref, f32[8,256,128]{2,1,0:T(8,128)} %get-tuple-element.61.factor_ref, ...), custom_call_target="tpu_custom_call" | custom-call | tf_op jit(solution)/shard_map/cond/branch_1_fun/pallas_call | solution.py:216
  18.1 56.3 %conditional.3 = (f32[1,8,256,128]{3,2,1,0:T(8,128)}, f32[1,256,128]{2,1,0:T(8,128)}) conditional(s32[]{:T(128)} %convert_element_type.8, (s32[4,256]{1,0:T(4,128)S(1)}, f32[64,128]{1,0:T(8,128)S(1)}, f32[256,128]{1,0:T(8,128)}, f32[256,128]{1,0:T(8,128)}, f32[8,256,128]{2,1,0:T(8,128)}, /*index=5*/bf16[256,2,128,128]{3,2,1,0:T(8,128)(2,1)}, ...), branch_computations={%region_2.0_spmd, %region_3.0_spmd} | conditional | flops 133120 | bytes 18252988 | solution.py:611
  18.1 1.7 %branch_1_fun.7 = f32[256,128]{1,0:T(8,128)S(1)} custom-call(f32[8,256,128]{2,1,0:T(8,128)} %get-tuple-element.78.u_ref), custom_call_target="tpu_custom_call" | custom-call | tf_op jit(solution)/shard_map/cond/branch_1_fun/pallas_call | solution.py:553
  19.8 0.9 %pad_maximum_fusion.2 = f32[2,256,128]{2,1,0:T(8,128)S(1)} fusion(f32[1,256,128]{2,1,0:T(8,128)} %bitcast.8, f32[1,256,128]{2,1,0:T(8,128)S(1)} %bitcast.25), kind=kLoop, calls=%fused_computation.3 | loop fusion | flops 65536 | bytes 524288 | tf_op jit(solution)/shard_map/cond/branch_1_fun/stack | solution.py:576
  20.7 1.0 %collective-permute-start.3 = (f32[2,256,128]{2,1,0:T(8,128)S(1)}, f32[2,256,128]{2,1,0:T(8,128)S(1)}, u32[]{:S(2)}, u32[]{:S(2)}) collective-permute-start(f32[2,256,128]{2,1,0:T(8,128)S(1)} %pad_maximum_fusion.2), channel_id=1, source_target_pairs={{0,1},{1,0},{2,3},{3,2},{4,5},{5,4},{6,7},{7,6},{8,9},{9,8},{10,11... | collective-permute-start | bytes 786440 | tf_op jit(solution)/shard_map/cond/branch_1_fun/ppermute | solution.py:417
  21.8 8.6 %all-to-all-start.1 = ((bf16[64,24,128]{2,1,0:T(8,128)(2,1)}), bf16[64,24,128]{2,1,0:T(8,128)(2,1)S(1)}, u32[]{:S(2)}, u32[]{:S(2)}) async-start(bf16[64,24,128]{2,1,0:T(8,128)(2,1)} %get-tuple-element.80), calls=%async_computation.1 | async-start | bytes 786432 | tf_op jit(solution)/shard_map/cond/branch_1_fun/all_to_all | solution.py:529
  30.4 0.7 fusion.5
  31.1 6.0 %collective-permute-start.5 = (f32[11,8,128]{2,1,0:T(8,128)S(1)}, f32[11,8,128]{2,1,0:T(8,128)S(1)}, u32[]{:S(2)}, u32[]{:S(2)}) collective-permute-start(f32[11,8,128]{2,1,0:T(8,128)S(1)} %pad_maximum_fusion.4), channel_id=1, source_target_pairs={{2,0},{4,2},{6,4},{8,6},{10,8},{12,10},{14,12},{16,14},{18,16},{20... | collective-permute-start | bytes 135176 | tf_op jit(solution)/shard_map/cond/branch_1_fun/ppermute | solution.py:421
  37.1 1.1 %collective-permute-done.5.after_ref = f32[11,8,128]{2,1,0:T(8,128)S(1)} collective-permute-done((f32[11,8,128]{2,1,0:T(8,128)S(1)}, f32[11,8,128]{2,1,0:T(8,128)S(1)}, u32[]{:S(2)}, u32[]{:S(2)}) %collective-permute-start.5) | collective-permute-done | bytes 45088 | tf_op jit(solution)/shard_map/cond/branch_1_fun/ppermute | solution.py:421
  38.2 6.0 %collective-permute-done.4.before_ref = f32[11,8,128]{2,1,0:T(8,128)S(1)} collective-permute-done((f32[11,8,128]{2,1,0:T(8,128)S(1)}, f32[11,8,128]{2,1,0:T(8,128)S(1)}, u32[]{:S(2)}, u32[]{:S(2)}) %collective-permute-start.4) | collective-permute-done | bytes 45088 | tf_op jit(solution)/shard_map/cond/branch_1_fun/ppermute | solution.py:421
  44.2 1.8 %branch_1_fun.8.base_ref = f32[256,128]{1,0:T(8,128)S(1)} custom-call(f32[256,128]{1,0:T(8,128)} %get-tuple-element.79.top_ref, bf16[256,128]{1,0:T(8,128)(2,1)} %get-tuple-element.81.under_ref, f32[256,128]{1,0:T(8,128)S(1)} %get-tuple-element.111.mate_ref, f32[11,8,128]{2,1,0:T(8,128)S(1)} %collective-permute-done.4.before_ref, ...), custom_call_target="tpu_custom_call" | custom-call | tf_op jit(solution)/shard_map/cond/branch_1_fun/pallas_call | solution.py:577
  46.1 1.8 %branch_1_fun.9._ = bf16[64,24,128]{2,1,0:T(8,128)(2,1)} custom-call(bf16[64,24,128]{2,1,0:T(8,128)(2,1)S(1)} %all-to-all-done.1.arrived_ref, f32[256,128]{1,0:T(8,128)S(1)} %branch_1_fun.8.base_ref), custom_call_target="tpu_custom_call" | custom-call | tf_op jit(solution)/shard_map/cond/branch_1_fun/pallas_call | solution.py:580
  47.9 5.8 %all-to-all-start.2 = ((bf16[64,24,128]{2,1,0:T(8,128)(2,1)}), bf16[64,24,128]{2,1,0:T(8,128)(2,1)S(1)}, u32[]{:S(2)}, u32[]{:S(2)}) async-start(bf16[64,24,128]{2,1,0:T(8,128)(2,1)} %branch_1_fun.9._), calls=%async_computation.2 | async-start | bytes 786432 | tf_op jit(solution)/shard_map/cond/branch_1_fun/all_to_all | solution.py:529
  53.7 10.0 %branch_1_fun.10 = f32[8,256,128]{2,1,0:T(8,128)} custom-call(f32[8,256,128]{2,1,0:T(8,128)S(1)} %copy-done.3, f32[256,128]{1,0:T(8,128)S(1)} %get-tuple-element.112.sides_ref, f32[11,8,128]{2,1,0:T(8,128)S(1)} %collective-permute-done.4.before_ref, f32[11,8,128]{2,1,0:T(8,128)S(1)} %collective-permute-done.5.after_ref, bf16[64,24,128]{2,1,0:T(8,128)(2,1)} %branch_1_fun.9._), custom_call_target="tpu_custom_call" | custom-call | tf_op jit(solution)/shard_map/cond/branch_1_fun/pallas_call | solution.py:585
  63.8 0.9 %all-to-all-done.2.arrived_ref = bf16[64,24,128]{2,1,0:T(8,128)(2,1)S(1)} async-done(((bf16[64,24,128]{2,1,0:T(8,128)(2,1)}), bf16[64,24,128]{2,1,0:T(8,128)(2,1)S(1)}, u32[]{:S(2)}, u32[]{:S(2)}) %all-to-all-start.2) | async-done | bytes 393248 | tf_op jit(solution)/shard_map/cond/branch_1_fun/all_to_all | solution.py:529
  64.7 9.5 %branch_1_fun.11 = f32[256,128]{1,0:T(8,128)} custom-call(s32[4,256]{1,0:T(4,128)S(1)} %get-tuple-element.83.pos_ref, bf16[64,24,128]{2,1,0:T(8,128)(2,1)S(1)} %all-to-all-done.2.arrived_ref, bf16[256,2,128,128]{3,2,1,0:T(8,128)(2,1)} %get-tuple-element.84.w_ref), custom_call_target="tpu_custom_call" | custom-call | tf_op jit(solution)/shard_map/cond/branch_1_fun/pallas_call | solution.py:513
  (20 shorter events, 0.1 us)
Async XLA Ops:
  1.5 16.5 %collective-permute-start.6 = (f32[256,128]{1,0:T(8,128)S(1)}, f32[256,128]{1,0:T(8,128)}, u32[]{:S(2)}, u32[]{:S(2)}) collective-permute-start(f32[256,128]{1,0:T(8,128)S(1)} %slice_bitcast_fusion.3), channel_id=1, source_target_pairs={{0,64},{64,0},{1,65},{65,1},{2,66},{66,2},{3,67},{67,3},{4,68},{68... | collective-permute-start | bytes 393224 | tf_op jit(solution)/shard_map/ppermute | solution.py:548
  7.0 11.1 %collective-permute-start.7 = (bf16[256,128]{1,0:T(8,128)(2,1)S(1)}, bf16[256,128]{1,0:T(8,128)(2,1)}, u32[]{:S(2)}, u32[]{:S(2)}) collective-permute-start(bf16[256,128]{1,0:T(8,128)(2,1)S(1)} %fusion), channel_id=1, source_target_pairs={{0,64},{64,0},{1,65},{65,1},{2,66},{66,2},{3,67},{67,3},{4,68},{68... | collective-permute-start | bytes 196616 | tf_op jit(solution)/shard_map/ppermute | solution.py:549
  7.0 0.7 copy-start.1
  7.7 0.7 copy-start.2
  18.1 13.0 %copy-start.3 = (f32[8,256,128]{2,1,0:T(8,128)S(1)}, f32[8,256,128]{2,1,0:T(8,128)}, u32[]{:S(2)}) copy-start(f32[8,256,128]{2,1,0:T(8,128)} %get-tuple-element.78.u_ref) | copy-start | bytes 3145732 | tf_op jit(solution)/shard_map/cond
  18.1 26.1 %copy-start.4 = (s32[6,256,128]{2,1,0:T(8,128)S(1)}, s32[6,256,128]{2,1,0:T(8,128)}, u32[]{:S(2)}) copy-start(s32[6,256,128]{2,1,0:T(8,128)} %get-tuple-element.82.table_ref) | copy-start | bytes 2359300 | tf_op jit(solution)/shard_map/cond
  20.7 10.4 %collective-permute-start.3 = (f32[2,256,128]{2,1,0:T(8,128)S(1)}, f32[2,256,128]{2,1,0:T(8,128)S(1)}, u32[]{:S(2)}, u32[]{:S(2)}) collective-permute-start(f32[2,256,128]{2,1,0:T(8,128)S(1)} %pad_maximum_fusion.2), channel_id=1, source_target_pairs={{0,1},{1,0},{2,3},{3,2},{4,5},{5,4},{6,7},{7,6},{8,9},{9,8},{10,11... | collective-permute-start | bytes 786440 | tf_op jit(solution)/shard_map/cond/branch_1_fun/ppermute | solution.py:417
  21.8 24.3 %all-to-all-start.1 = ((bf16[64,24,128]{2,1,0:T(8,128)(2,1)}), bf16[64,24,128]{2,1,0:T(8,128)(2,1)S(1)}, u32[]{:S(2)}, u32[]{:S(2)}) async-start(bf16[64,24,128]{2,1,0:T(8,128)(2,1)} %get-tuple-element.80), calls=%async_computation.1 | async-start | bytes 786432 | tf_op jit(solution)/shard_map/cond/branch_1_fun/all_to_all | solution.py:529
  31.1 7.1 %collective-permute-start.5 = (f32[11,8,128]{2,1,0:T(8,128)S(1)}, f32[11,8,128]{2,1,0:T(8,128)S(1)}, u32[]{:S(2)}, u32[]{:S(2)}) collective-permute-start(f32[11,8,128]{2,1,0:T(8,128)S(1)} %pad_maximum_fusion.4), channel_id=1, source_target_pairs={{2,0},{4,2},{6,4},{8,6},{10,8},{12,10},{14,12},{16,14},{18,16},{20... | collective-permute-start | bytes 135176 | tf_op jit(solution)/shard_map/cond/branch_1_fun/ppermute | solution.py:421
  37.1 7.1 %collective-permute-start.4 = (f32[11,8,128]{2,1,0:T(8,128)S(1)}, f32[11,8,128]{2,1,0:T(8,128)S(1)}, u32[]{:S(2)}, u32[]{:S(2)}) collective-permute-start(f32[11,8,128]{2,1,0:T(8,128)S(1)} %pad_maximum_fusion.3), channel_id=1, source_target_pairs={{0,2},{2,4},{4,6},{6,8},{8,10},{10,12},{12,14},{14,16},{16,18},{18... | collective-permute-start | bytes 135176 | tf_op jit(solution)/shard_map/cond/branch_1_fun/ppermute | solution.py:421
  47.9 16.8 %all-to-all-start.2 = ((bf16[64,24,128]{2,1,0:T(8,128)(2,1)}), bf16[64,24,128]{2,1,0:T(8,128)(2,1)S(1)}, u32[]{:S(2)}, u32[]{:S(2)}) async-start(bf16[64,24,128]{2,1,0:T(8,128)(2,1)} %branch_1_fun.9._), calls=%async_computation.2 | async-start | bytes 786432 | tf_op jit(solution)/shard_map/cond/branch_1_fun/all_to_all | solution.py:529

commit v3 on v2

--- a/solution.py
+++ b/solution.py
@@ -124,14 +124,14 @@
 
 
 def ocean_flux_body(
-    pos_ref, label_ref, air_ref, prior_ref, factor_ref, w_ref, out_ref, held, rows, sems
+    pos_ref, label_ref, air_ref, prior_ref, factor_ref, w_ref, out_ref, held, packed, rows, sems
 ):
     copy = weight_copies(w_ref, held, sems, FLUX_ROWS)
     for c in range(ROWS // FLUX_ROWS):
         copy(c).start()
-    out_ref[...] = jnp.zeros_like(out_ref)
+    packed[...] = jnp.zeros_like(packed)
     for d in range(RANKS):
-        out_ref[d * OCEAN_SLOTS + CAP] = jnp.broadcast_to(
+        packed[d * OCEAN_SLOTS + CAP] = jnp.broadcast_to(
             label_ref[d : d + 1, :], (NF, COLS)
         ).astype(BF16)
     difference = air_ref[...] - prior_ref[...]
@@ -146,7 +146,11 @@
             flux = rows[pl.ds(pl.multiple_of(b * NF, NF), NF), :].astype(BF16)
             part = jnp.dot(flux, side_by_side(held, b), preferred_element_type=F32).astype(BF16)
             for k in range(K):
-                out_ref[pos_ref[k, b]] = part[:, k * COLS : (k + 1) * COLS]
+                packed[pos_ref[k, b]] = part[:, k * COLS : (k + 1) * COLS]
+
+    done = pltpu.make_async_copy(packed, out_ref, sems.at[ROWS // FLUX_ROWS])
+    done.start()
+    done.wait()
 
 
 WEIGHTS_HELD = [
@@ -159,11 +163,12 @@
         ocean_flux_body,
         out_shape=jax.ShapeDtypeStruct((RANKS * OCEAN_SLOTS, NF, COLS), BF16),
         in_specs=[SMEM, VMEM, VMEM, VMEM, VMEM, ANY],
-        out_specs=VMEM,
+        out_specs=pl.BlockSpec(memory_space=pltpu.HBM),
         scratch_shapes=WEIGHTS_HELD
         + [
+            pltpu.VMEM((RANKS * OCEAN_SLOTS, NF, COLS), BF16),
             pltpu.VMEM((ROWS * NF, COLS), F32),
-            pltpu.SemaphoreType.DMA((ROWS // FLUX_ROWS,)),
+            pltpu.SemaphoreType.DMA((ROWS // FLUX_ROWS + 1,)),
         ],
         compiler_params=pltpu.CompilerParams(vmem_limit_bytes=32 << 20),
     )(pos, labels, air, prior, factors, weights)
@@ -264,7 +269,7 @@
     return pltpu.roll(jnp.where(lane == 0, ends, field), COLS - 1, 1)
 
 
-def second_along(field, axis, index, extent):
+def second_along(field, axis, index):
     phase = index % 4
     total = None
     for shift in range(-3, 4):
@@ -272,13 +277,16 @@
         for p in range(4):
             if 0 <= p + shift < 4:
                 factor = jnp.where(phase == p, F32(SECOND[p, p + shift]), factor)
-        moved = field if shift == 0 else pltpu.roll(field, (-shift) % extent, axis)
+        moved = field if shift == 0 else pltpu.roll(field, (-shift) % field.shape[axis], axis)
         total = factor * moved if total is None else total + factor * moved
     return total
 
 
-def diffused(field, above, below, row, lane):
-    along = second_along(field, 0, row, EXTENDED) + second_along(field, 1, lane, COLS)
+def diffused(field, above, below):
+    groups = field.reshape(EXTENDED // 8, 8, COLS)
+    along = second_along(groups, 1, lax.broadcasted_iota(jnp.int32, (1, 8, COLS), 1))
+    along = along.reshape(EXTENDED, COLS)
+    along += second_along(field, 1, lax.broadcasted_iota(jnp.int32, (1, COLS), 1))
     return field + ATMOS_DIFFUSION * along + MIXING * (above + below - 2.0 * field)
 
 
@@ -295,7 +303,7 @@
     return assembled(field, 0, row % 4, ahead, pltpu.roll(field, 1, 0))
 
 
-def substeps_body(u_ref, sides_ref, before_ref, after_ref, _, out_ref, main, moved):
+def substeps_body(u_ref, sides_ref, before_ref, after_ref, out_ref, main, moved):
     row, lane = iotas(EXTENDED)
     phase, part = lane % 4, lane % (2 * WIDE)
     for l in range(LEV):
@@ -306,12 +314,12 @@
     for substep in range(2):
         over = jnp.where(lane < COLS - 2 * WIDE, turned(sides, -2 * WIDE), sides)
         under = jnp.where(lane >= 2 * WIDE, turned(sides, 2 * WIDE), sides)
-        sides = assembled_rows(diffused(sides, over, under, row, lane), row)
+        sides = assembled_rows(diffused(sides, over, under), row)
         edges = jnp.zeros((EXTENDED, COLS), F32)
         for l in range(LEV):
             field = main[l]
             half = assembled_rows(
-                diffused(field, main[min(l + 1, LEV - 1)], main[max(l - 1, 0)], row, lane), row
+                diffused(field, main[min(l + 1, LEV - 1)], main[max(l - 1, 0)]), row
             )
             if substep == 0:
                 first = turned(half, 2 * WIDE * l + WIDE - 1)
@@ -372,21 +380,21 @@
     return total
 
 
-def top_base_body(top_ref, under_ref, mate_ref, before_ref, after_ref, table_ref, out_ref):
+def top_base_body(o_ref, sides_ref, before_ref, after_ref, table_ref, out_ref):
     row, lane = iotas(ROWS)
-    top = top_ref[...]
+    top = o_ref[0]
     spread = neighbour_spread(
         top,
-        mate_ref[...],
-        before_ref[LEV + 1, WIDE - 1 :, :],
-        after_ref[LEV + 1, :1, :],
-        before_ref[LEV + 2, WIDE - 1 :, :],
-        after_ref[LEV + 2, :1, :],
+        mate_ends(sides_ref[...], 0),
+        before_ref[0, WIDE - 1 :, :],
+        after_ref[0, :1, :],
+        mate_ends(before_ref[LEV, WIDE - 1 :, :], 0),
+        mate_ends(after_ref[LEV, :1, :], 0),
         neighbour_counts(table_ref, row, lane),
         row,
         lane,
     )
-    out_ref[...] = top + OCEAN_DIFFUSION * spread + MIXING * (under_ref[...].astype(F32) - top)
+    out_ref[...] = top + OCEAN_DIFFUSION * spread + MIXING * (o_ref[1] - top)
 
 
 def ocean_base_body(o_ref, sides_ref, before_ref, after_ref, table_ref, out_ref, counts_ref):
@@ -410,15 +418,14 @@
         out_ref[l] = field + OCEAN_DIFFUSION * spread + MIXING * (above + below - 2.0 * field)
 
 
-def exchanged(levels, planes):
+def exchanged(levels, sides):
     size = lax.axis_size("gx")
     up = [(i, (i + 1) % size) for i in range(size)]
     down = [(j, i) for i, j in up]
-    mate = lax.ppermute(planes, "gy", [(0, 1), (1, 0)])
-    parts = [levels, mate[:1], planes[1:], mate[1:]]
-    last = jnp.concatenate([v[:, ROWS - WIDE :, :] for v in parts], axis=0)
-    first = jnp.concatenate([v[:, :WIDE, :] for v in parts], axis=0)
-    return mate, lax.ppermute(last, "gx", up), lax.ppermute(first, "gx", down)
+    sides = lax.ppermute(sides, "gy", [(0, 1), (1, 0)])
+    last = jnp.concatenate([levels[:, ROWS - WIDE :, :], sides[None, ROWS - WIDE :, :]], axis=0)
+    first = jnp.concatenate([levels[:, :WIDE, :], sides[None, :WIDE, :]], axis=0)
+    return sides, lax.ppermute(last, "gx", up), lax.ppermute(first, "gx", down)
 
 
 def row_hits(labels):
@@ -545,70 +552,69 @@
     plane = jax.ShapeDtypeStruct((ROWS, COLS), F32)
     swap = [(0, 1), (1, 0)]
 
-    other_top = lax.ppermute(own[0], "comp", swap)
-    other_under = lax.ppermute(own[1].astype(BF16), "comp", swap)
+    own_first = lax.optimization_barrier(own[0])
+    other_first = lax.ppermute(own_first, "comp", swap)
+    halo = exchanged(own, shadow_call(sides_body, plane, [VMEM])(own))
     pos, labels = positions(destination_water_peer, destination_water_line)
 
-    def sides_of(levels):
-        return shadow_call(sides_body, plane, [VMEM])(levels)
-
-    def atmosphere_early():
-        packed = atmos_flux(
+    packed = lax.cond(
+        is_atmosphere_side,
+        lambda: atmos_flux(
             pos,
             labels,
-            own[0],
+            own_first,
             prior_marine_heat,
             transfer_factor_table,
             interpolation_matrix_blocks,
             depth_fraction_matrix,
-        )
-        rows = jnp.zeros((LEV + 1, WIDE, COLS), F32)
-        return packed, jnp.zeros((1, ROWS, COLS), F32), rows, rows
-
-    def ocean_early():
-        halo = exchanged(own, sides_of(own)[None])
-        return jnp.zeros((RANKS, ATMOS_SLOTS, COLS), BF16), *halo
-
-    packed, *ocean_halo = lax.cond(is_atmosphere_side, atmosphere_early, ocean_early)
+        ),
+        lambda: jnp.zeros((RANKS, ATMOS_SLOTS, COLS), BF16),
+    )
+    top_base = lax.cond(
+        is_atmosphere_side,
+        lambda: own_first,
+        lambda: shadow_call(top_base_body, plane, [VMEM] * 5)(own, *halo, adjacent_cell_table),
+    )
+    other_base = lax.ppermute(top_base, "comp", swap)
 
     def atmosphere():
         arrived = to_peers(packed)
-        mate, before, after = exchanged(own, jnp.stack([sides_of(own), other_top]))
-        base = shadow_call(top_base_body, plane, [VMEM] * 6)(
-            other_top, other_under, mate[1], before, after, adjacent_cell_table
+        wide = pltpu.VMEM((LEV, EXTENDED, COLS), F32)
+        final = shadow_call(substeps_body, block, [VMEM] * 4, scratch_shapes=[wide, wide])(
+            own, *halo
         )
-        picked = call(
-            top_body, jax.ShapeDtypeStruct((RANKS, ATMOS_SLOTS, COLS), BF16), [VMEM, VMEM]
-        )(arrived, base)
-        returned = to_peers(picked)
-        wide = pltpu.VMEM((LEV, EXTENDED, COLS), F32)
-        final = shadow_call(
-            substeps_body, block, [VMEM] * 4 + [ANY], scratch_shapes=[wide, wide]
-        )(own, mate[0], before, after, picked)
-        return final, remap(pos, returned, interpolation_matrix_blocks)
+        return final, jnp.zeros((ROWS, COLS), F32), arrived
 
     def ocean():
         payload = ocean_flux(
             pos,
             labels,
-            other_top,
+            other_first,
             prior_marine_heat,
             transfer_factor_table,
             interpolation_matrix_blocks,
         )
         arrived = to_peers(payload.reshape(RANKS, OCEAN_SLOTS * NF, COLS))
-        mate, before, after = ocean_halo
         base = shadow_call(
             ocean_base_body,
             block,
             [VMEM] * 5,
             scratch_shapes=[pltpu.VMEM((len(ORDER), ROWS, COLS), F32)],
-        )(own, mate[0], before, after, adjacent_cell_table)
-        return ocean_sums(
+        )(own, *halo, adjacent_cell_table)
+        state, first = ocean_sums(
             arrived.reshape(RANKS * OCEAN_SLOTS, NF, COLS), base, depth_fraction_matrix
         )
-
-    state, plane_out = lax.cond(is_atmosphere_side, atmosphere, ocean)
+        return state, first, jnp.zeros((RANKS, ATMOS_SLOTS, COLS), BF16)
+
+    state, first, arrived = lax.cond(is_atmosphere_side, atmosphere, ocean)
+
+    def sea_temperature():
+        picked = call(
+            top_body, jax.ShapeDtypeStruct((RANKS, ATMOS_SLOTS, COLS), BF16), [VMEM, VMEM]
+        )(arrived, other_base)
+        return remap(pos, to_peers(picked), interpolation_matrix_blocks)
+
+    plane_out = lax.cond(is_atmosphere_side, sea_temperature, lambda: first)
     return state[None], plane_out[None]
 
 

time: 75.9 us -> 79.8 us (1.051); the launches traced: 74.6 us -> 79.4 us
  blocking collectives: 0 us -> 19.4 us
  waiting for transfers between devices: 8.01 us -> 0.28 us
  starting transfers between devices: 26 us -> 21.8 us
  Pallas kernels: 33.6 us -> 32.2 us
  other arithmetic: 0.93 us -> 0.01 us
    all_to_all x0 -> x1, blocking collectives: none -> 19.4 us  [to_peers(): lax.all_to_all(payload, ('gx', 'gy'), split_axis=0, concat_axis=0, tiled=...]
    ppermute x5, waiting for transfers between devices: 7.1 us -> 0.22 us  [the longest x1 0.21 us: exchanged(): sides = lax.ppermute(sides, 'gy', [(0, 1), (1, 0)])]
    all_to_all x2 -> x1, starting transfers between devices: 14.4 us -> 9.12 us  [to_peers(): lax.all_to_all(payload, ('gx', 'gy'), split_axis=0, concat_axis=0, tiled=...]
    cond x4 -> x1, local copies, waits for them, and re-layouts: 0.01 us -> 1.59 us
    unnamed x4 -> x10, local copies, waits for them, and re-layouts: 1.36 us -> 0.02 us
    ppermute x5, starting transfers between devices: 11.5 us -> 12.7 us  [the longest x1 4.72 us: exchanged(): lax.ppermute(first, 'gx', down)]
    pallas_call x4 -> x3, Pallas kernels: 15.4 us -> 14.5 us  [the longest x1 10.7 us: atmosphere(): shadow_call(substeps_body, block, [VMEM] * 4, scratch_shapes=[wide, wide])]
    another operation x1 -> x0, other arithmetic: 0.92 us -> none  [atmosphere(): mate, before, after = exchanged(own, jnp.stack([sides_of(own), other_top]))]
  transfers between devices with their start and end apart: 7 -> 6, of which waited for: 3 -> 2; matrix products, arithmetic and copies ran while one was open for 3% -> 6% of each run, Pallas kernels for 28% -> 24%
where the time goes in v3:
time: 79.8 us; the launch traced here: 79.4 us
  Pallas kernels  32.2 us (40%)
  starting transfers between devices  21.8 us (27%)
  blocking collectives  19.4 us (24%)
  local copies, waits for them, and re-layouts  4.62 us (6%)
  between operations  0.91 us (1%)
    all_to_all x1, blocking collectives, to_peers(): lax.all_to_all(payload, ('gx', 'gy'), split_axis=0, concat_axis=0, tiled=...  19.4 us
    pallas_call x1, Pallas kernels, atmosphere(): shadow_call(substeps_body, block, [VMEM] * 4, scratch_shapes=[wide, wide])  10.7 us
    pallas_call x1, Pallas kernels, remap(): pl.pallas_call(remap_body, out_shape=jax.ShapeDtypeStruct((ROWS, COLS), F...  9.5 us
    all_to_all x1, starting transfers between devices, to_peers(): lax.all_to_all(payload, ('gx', 'gy'), split_axis=0, concat_axis=0, tiled=...  9.12 us
    pallas_call x1, Pallas kernels, atmos_flux(): pl.pallas_call(atmos_flux_body, out_shape=jax.ShapeDtypeStruct((RANKS, AT...  7.91 us
    ppermute x1, starting transfers between devices, exchanged(): lax.ppermute(first, 'gx', down)  4.72 us
    ppermute x1, starting transfers between devices, local(): other_first = lax.ppermute(own_first, 'comp', swap)  3.3 us
    pallas_call x1, Pallas kernels, sea_temperature(): call(top_body, jax.ShapeDtypeStruct((RANKS, ATMOS_SLOTS, COLS), BF16), [V...  2.09 us
  transfers between devices with their start and end apart: 6, of which 2 were waited for; matrix products, arithmetic and copies ran while one was open for 6% of the time, Pallas kernels for 24%

profile of v3, /device:TPU:1, one launch (start us, length us, event | category | flops | bytes accessed | tf_op | source)
XLA Modules:
  0.0 79.4 jit_solution(13476637154244724276)
XLA Ops:
  0.7 1.7 %shard_map.96 = f32[256,128]{1,0:T(8,128)S(1)} custom-call(f32[8,256,128]{2,1,0:T(8,128)} %bitcast.17), custom_call_target="tpu_custom_call" | custom-call | tf_op jit(solution)/shard_map/pallas_call | solution.py:557
  2.3 1.5 %collective-permute-start.1 = (f32[256,128]{1,0:T(8,128)S(1)}, f32[256,128]{1,0:T(8,128)S(1)}, u32[]{:S(2)}, u32[]{:S(2)}) collective-permute-start(f32[256,128]{1,0:T(8,128)S(1)} %shard_map.96), channel_id=1, source_target_pairs={{0,1},{1,0},{2,3},{3,2},{4,5},{5,4},{6,7},{7,6},{8,9},{9,8},{10,11... | collective-permute-start | bytes 393224 | tf_op jit(solution)/shard_map/ppermute | solution.py:425
  3.8 0.8 fusion
  4.6 0.2 collective-permute-done.1
  4.8 1.7 %collective-permute-start.2 = (f32[9,8,128]{2,1,0:T(8,128)S(1)}, f32[9,8,128]{2,1,0:T(8,128)S(1)}, u32[]{:S(2)}, u32[]{:S(2)}) collective-permute-start(f32[9,8,128]{2,1,0:T(8,128)S(1)} %pad_maximum_fusion), channel_id=1, source_target_pairs={{0,2},{2,4},{4,6},{6,8},{8,10},{10,12},{12,14},{14,16},{16,18},{18... | collective-permute-start | bytes 110600 | tf_op jit(solution)/shard_map/ppermute | solution.py:428
  6.6 4.7 %collective-permute-start.3 = (f32[9,8,128]{2,1,0:T(8,128)S(1)}, f32[9,8,128]{2,1,0:T(8,128)S(1)}, u32[]{:S(2)}, u32[]{:S(2)}) collective-permute-start(f32[9,8,128]{2,1,0:T(8,128)S(1)} %pad_maximum_fusion.1), channel_id=1, source_target_pairs={{2,0},{4,2},{6,4},{8,6},{10,8},{12,10},{14,12},{16,14},{18,16},{20... | collective-permute-start | bytes 110600 | tf_op jit(solution)/shard_map/ppermute | solution.py:428
  11.3 1.6 %slice_bitcast_fusion = f32[256,128]{1,0:T(8,128)} fusion(f32[1,8,256,128]{3,2,1,0:T(8,128)} %param.16), kind=kLoop, calls=%fused_computation | loop fusion | bytes 262144 | tf_op jit(solution)/shard_map/squeeze | solution.py:555
  12.9 3.3 %collective-permute-start = (f32[256,128]{1,0:T(8,128)}, f32[256,128]{1,0:T(8,128)S(1)}, u32[]{:S(2)}, u32[]{:S(2)}) collective-permute-start(f32[256,128]{1,0:T(8,128)} %slice_bitcast_fusion), channel_id=1, source_target_pairs={{0,64},{64,0},{1,65},{65,1},{2,66},{66,2},{3,67},{67,3},{4,68},{68... | collective-permute-start | bytes 393224 | tf_op jit(solution)/shard_map/ppermute | solution.py:556
  16.2 1.6 %conditional.6 = (f32[256,128]{1,0:T(8,128)}) conditional(s32[]{:T(128)} %convert_element_type.2, (f32[8,256,128]{2,1,0:T(8,128)}, f32[256,128]{1,0:T(8,128)S(1)}, f32[9,8,128]{2,1,0:T(8,128)S(1)}, f32[9,8,128]{2,1,0:T(8,128)S(1)}, s32[6,256,128]{2,1,0:T(8,128)}) %tuple.67, f32[256,128]{1,0:T(8,128)} %slice_bitcast_fusion), branch_computations={%region_4.0_spmd, %region_5.0_spmd} | conditional | bytes 262152 | solution.py:573
  16.2 1.6 %copy.19 = f32[256,128]{1,0:T(8,128)} copy(f32[256,128]{1,0:T(8,128)} %param.5) | data formatting | bytes 262144 | tf_op jit(solution)/shard_map/cond
  17.8 1.5 %collective-permute-start.4 = (f32[256,128]{1,0:T(8,128)}, f32[256,128]{1,0:T(8,128)}, u32[]{:S(2)}, u32[]{:S(2)}) collective-permute-start(f32[256,128]{1,0:T(8,128)} %get-tuple-element.145), channel_id=1, source_target_pairs={{0,64},{64,0},{1,65},{65,1},{2,66},{66,2},{3,67},{67,3},{4,68},{68... | collective-permute-start | bytes 393224 | tf_op jit(solution)/shard_map/ppermute | solution.py:578
  19.2 0.4 shard_map.95
  19.6 7.9 %conditional.4 = (bf16[64,24,128]{2,1,0:T(8,128)(2,1)}) conditional(s32[]{:T(128)} %convert_element_type.2, () %tuple.45, (s32[4,256]{1,0:T(4,128)S(1)}, f32[64,128]{1,0:T(8,128)S(1)}, f32[256,128]{1,0:T(8,128)}, f32[256,128]{1,0:T(8,128)S(1)}, f32[8,256,128]{2,1,0:T(8,128)S(1)}, /*index=5*/bf16[256,2,128,128]{3,2,1,0:T(8,128)(2,1)}, ...), branch_computations={%region_0.0_spmd, %region_1.0_spmd} | conditional | bytes 393226 | solution.py:560
  19.7 7.9 %branch_1_fun.4 = bf16[64,24,128]{2,1,0:T(8,128)(2,1)} custom-call(s32[4,256]{1,0:T(4,128)S(1)} %get-tuple-element.83.pos_ref, f32[64,128]{1,0:T(8,128)S(1)} %get-tuple-element.84.label_ref, f32[256,128]{1,0:T(8,128)} %get-tuple-element.85.air_ref, f32[256,128]{1,0:T(8,128)S(1)} %get-tuple-element.86.prior_ref, ...), custom_call_target="tpu_custom_call" | custom-call | tf_op jit(solution)/shard_map/cond/branch_1_fun/pallas_call | solution.py:221
  27.6 0.0 collective-permute-done
  27.6 20.6 %conditional.5 = (f32[8,256,128]{2,1,0:T(8,128)}, f32[256,128]{1,0:T(8,128)}, bf16[64,24,128]{2,1,0:T(8,128)(2,1)}) conditional(s32[]{:T(128)} %convert_element_type.2, (s32[4,256]{1,0:T(4,128)S(1)}, f32[64,128]{1,0:T(8,128)S(1)}, f32[256,128]{1,0:T(8,128)S(1)}, f32[256,128]{1,0:T(8,128)S(1)}, f32[8,256,128]{2,1,0:T(8,128)S(1)}, ...), branch_computations={%region_2.0_spmd, %region_3.0_spmd} | conditional | bytes 18645162 | solution.py:609
  27.6 9.1 %all-to-all-start.1 = ((bf16[64,24,128]{2,1,0:T(8,128)(2,1)}), bf16[64,24,128]{2,1,0:T(8,128)(2,1)}, u32[]{:S(2)}, u32[]{:S(2)}) async-start(bf16[64,24,128]{2,1,0:T(8,128)(2,1)} %get-tuple-element.108), calls=%async_computation.1 | async-start | bytes 786432 | tf_op jit(solution)/shard_map/cond/branch_1_fun/all_to_all | solution.py:536
  36.7 10.7 %branch_1_fun.5 = f32[8,256,128]{2,1,0:T(8,128)} custom-call(f32[8,256,128]{2,1,0:T(8,128)} %get-tuple-element.104.u_ref, f32[256,128]{1,0:T(8,128)S(1)} %get-tuple-element.105.sides_ref, f32[9,8,128]{2,1,0:T(8,128)S(1)} %get-tuple-element.106.before_ref, f32[9,8,128]{2,1,0:T(8,128)S(1)} %get-tuple-element.107.after_ref), custom_call_target="tpu_custom_call" | custom-call | tf_op jit(solution)/shard_map/cond/branch_1_fun/pallas_call | solution.py:583
  47.5 0.1 all-to-all-done.1
  47.5 0.7 broadcast.8
  48.2 31.0 %conditional.7 = (f32[256,128]{1,0:T(8,128)}) conditional(s32[]{:T(128)} %convert_element_type.2, f32[256,128]{1,0:T(8,128)} %get-tuple-element.128, (bf16[64,24,128]{2,1,0:T(8,128)(2,1)}, f32[256,128]{1,0:T(8,128)}, s32[4,256]{1,0:T(4,128)S(1)}, bf16[256,2,128,128]{3,2,1,0:T(8,128)(2,1)}) %tuple.49), branch_computations={%region_6.0_spmd, %region_7.0_spmd} | conditional | bytes 786440 | solution.py:617
  48.2 2.1 %branch_1_fun.6 = bf16[64,24,128]{2,1,0:T(8,128)(2,1)S(1)} custom-call(bf16[64,24,128]{2,1,0:T(8,128)(2,1)} %get-tuple-element.115.arrived_ref, f32[256,128]{1,0:T(8,128)} %get-tuple-element.116.base_ref), custom_call_target="tpu_custom_call" | custom-call | tf_op jit(solution)/shard_map/cond/branch_1_fun/pallas_call | solution.py:612
  50.3 19.4 %all_to_all.12.arrived_ref = bf16[64,24,128]{2,1,0:T(8,128)(2,1)S(1)} all-to-all(bf16[64,24,128]{2,1,0:T(8,128)(2,1)S(1)} %branch_1_fun.6), channel_id=1, replica_groups=mesh['comp'=2,'gx'=32,'gy'=2] {'gx','gy'}, dimensions={0} | all-to-all | bytes 786432 | tf_op jit(solution)/shard_map/cond/branch_1_fun/all_to_all | solution.py:536
  69.7 9.5 %branch_1_fun.7 = f32[256,128]{1,0:T(8,128)} custom-call(s32[4,256]{1,0:T(4,128)S(1)} %get-tuple-element.114.pos_ref, bf16[64,24,128]{2,1,0:T(8,128)(2,1)S(1)} %all_to_all.12.arrived_ref, bf16[256,2,128,128]{3,2,1,0:T(8,128)(2,1)} %get-tuple-element.117.w_ref), custom_call_target="tpu_custom_call" | custom-call | tf_op jit(solution)/shard_map/cond/branch_1_fun/pallas_call | solution.py:520
  (16 shorter events, 0.0 us)
Async XLA Ops:
  0.6 18.6 %copy-start.1 = (s32[256,2]{0,1:T(2,128)S(1)}, s32[256,2]{0,1:T(2,128)}, u32[]{:S(2)}) copy-start(s32[256,2]{0,1:T(2,128)} %param.21) | copy-start | bytes 6148
  0.6 18.6 %copy-start.2 = (s32[256,2]{0,1:T(2,128)S(1)}, s32[256,2]{0,1:T(2,128)}, u32[]{:S(2)}) copy-start(s32[256,2]{0,1:T(2,128)} %param.22) | copy-start | bytes 6148
  0.7 19.0 %copy-start.5 = (f32[256,128]{1,0:T(8,128)S(1)}, f32[256,128]{1,0:T(8,128)}, u32[]{:S(2)}) copy-start(f32[256,128]{1,0:T(8,128)} %param.17) | copy-start | bytes 393220
  0.7 19.0 %copy-start.3 = (f32[8,256,128]{2,1,0:T(8,128)S(1)}, f32[8,256,128]{2,1,0:T(8,128)}, u32[]{:S(2)}) copy-start(f32[8,256,128]{2,1,0:T(8,128)} %param.18) | copy-start | bytes 3145732
  0.7 19.0 %copy-start.8 = (f32[8,8]{1,0:T(8,128)S(1)}, f32[8,8]{1,0:T(8,128)}, u32[]{:S(2)}) copy-start(f32[8,8]{1,0:T(8,128)} %param.19) | copy-start | bytes 772
  2.3 2.5 %collective-permute-start.1 = (f32[256,128]{1,0:T(8,128)S(1)}, f32[256,128]{1,0:T(8,128)S(1)}, u32[]{:S(2)}, u32[]{:S(2)}) collective-permute-start(f32[256,128]{1,0:T(8,128)S(1)} %shard_map.96), channel_id=1, source_target_pairs={{0,1},{1,0},{2,3},{3,2},{4,5},{5,4},{6,7},{7,6},{8,9},{9,8},{10,11... | collective-permute-start | bytes 393224 | tf_op jit(solution)/shard_map/ppermute | solution.py:425
  4.8 11.3 %collective-permute-start.2 = (f32[9,8,128]{2,1,0:T(8,128)S(1)}, f32[9,8,128]{2,1,0:T(8,128)S(1)}, u32[]{:S(2)}, u32[]{:S(2)}) collective-permute-start(f32[9,8,128]{2,1,0:T(8,128)S(1)} %pad_maximum_fusion), channel_id=1, source_target_pairs={{0,2},{2,4},{4,6},{6,8},{8,10},{10,12},{12,14},{14,16},{16,18},{18... | collective-permute-start | bytes 110600 | tf_op jit(solution)/shard_map/ppermute | solution.py:428
  6.6 9.6 %collective-permute-start.3 = (f32[9,8,128]{2,1,0:T(8,128)S(1)}, f32[9,8,128]{2,1,0:T(8,128)S(1)}, u32[]{:S(2)}, u32[]{:S(2)}) collective-permute-start(f32[9,8,128]{2,1,0:T(8,128)S(1)} %pad_maximum_fusion.1), channel_id=1, source_target_pairs={{2,0},{4,2},{6,4},{8,6},{10,8},{12,10},{14,12},{16,14},{18,16},{20... | collective-permute-start | bytes 110600 | tf_op jit(solution)/shard_map/ppermute | solution.py:428
  12.9 14.7 %collective-permute-start = (f32[256,128]{1,0:T(8,128)}, f32[256,128]{1,0:T(8,128)S(1)}, u32[]{:S(2)}, u32[]{:S(2)}) collective-permute-start(f32[256,128]{1,0:T(8,128)} %slice_bitcast_fusion), channel_id=1, source_target_pairs={{0,64},{64,0},{1,65},{65,1},{2,66},{66,2},{3,67},{67,3},{4,68},{68... | collective-permute-start | bytes 393224 | tf_op jit(solution)/shard_map/ppermute | solution.py:556
  17.8 30.4 %collective-permute-start.4 = (f32[256,128]{1,0:T(8,128)}, f32[256,128]{1,0:T(8,128)}, u32[]{:S(2)}, u32[]{:S(2)}) collective-permute-start(f32[256,128]{1,0:T(8,128)} %get-tuple-element.145), channel_id=1, source_target_pairs={{0,64},{64,0},{1,65},{65,1},{2,66},{66,2},{3,67},{67,3},{4,68},{68... | collective-permute-start | bytes 393224 | tf_op jit(solution)/shard_map/ppermute | solution.py:578
  27.6 19.9 %all-to-all-start.1 = ((bf16[64,24,128]{2,1,0:T(8,128)(2,1)}), bf16[64,24,128]{2,1,0:T(8,128)(2,1)}, u32[]{:S(2)}, u32[]{:S(2)}) async-start(bf16[64,24,128]{2,1,0:T(8,128)(2,1)} %get-tuple-element.108), calls=%async_computation.1 | async-start | bytes 786432 | tf_op jit(solution)/shard_map/cond/branch_1_fun/all_to_all | solution.py:536

commit v4 on v2

--- a/solution.py
+++ b/solution.py
@@ -19,6 +19,7 @@
 ROWS = 256
 COLS = 128
 K = 2
+WIDE = 8
 OCEAN_SLOTS = 19
 ATMOS_SLOTS = 24
 
@@ -64,7 +65,7 @@
     return call(body, out_shape, specs, cost_estimate=nothing, **params)
 
 
-def positions_body(peer_ref, line_ref, pos_ref, label_ref):
+def route(peer_ref, line_ref, pos_ref, label_ref):
     count = ROWS * K
     peer = jnp.concatenate([peer_ref[k : k + 1, :] for k in range(K)], axis=1)
     line = jnp.concatenate([line_ref[k : k + 1, :] for k in range(K)], axis=1)
@@ -96,15 +97,37 @@
     )
 
 
-def positions(peer, line):
+def turned(field, lanes):
+    lanes = lanes % COLS
+    return field if lanes == 0 else pltpu.roll(field, lanes, 1)
+
+
+def first_body(side_ref, own_ref, peer_ref, line_ref, cross_ref, sides_ref, pos_ref, label_ref):
+    top = own_ref[0]
+    high = top.astype(BF16)
+    rest = top - high.astype(F32)
+    cross_ref[0] = high
+    other = MIXING * own_ref[1] + (1.0 - MIXING) * rest
+    cross_ref[1] = jnp.where(side_ref[0] == 0, rest, other).astype(BF16)
+    lane = lax.broadcasted_iota(jnp.int32, (ROWS, COLS), 1)
+    packed = jnp.zeros((ROWS, COLS), F32)
+    for l in range(LEV):
+        packed = jnp.where(lane // (2 * WIDE) == l, turned(own_ref[l], WIDE + 2 * WIDE * l), packed)
+    sides_ref[...] = packed
+    route(peer_ref, line_ref, pos_ref, label_ref)
+
+
+def first_kernel(side, own, peer, line):
     return call(
-        positions_body,
+        first_body,
         (
+            jax.ShapeDtypeStruct((2, ROWS, COLS), BF16),
+            jax.ShapeDtypeStruct((ROWS, COLS), F32),
             jax.ShapeDtypeStruct((2 * K, ROWS), jnp.int32),
             jax.ShapeDtypeStruct((RANKS, COLS), F32),
         ),
-        [VMEM, VMEM],
-    )(peer.T, line.T)
+        [SMEM, VMEM, VMEM, VMEM],
+    )(side, own, peer.T, line.T)
 
 
 FLUX_ROWS = 16
@@ -124,17 +147,17 @@
 
 
 def ocean_flux_body(
-    pos_ref, label_ref, air_ref, prior_ref, factor_ref, w_ref, out_ref, held, rows, sems
+    pos_ref, label_ref, air_ref, prior_ref, factor_ref, w_ref, out_ref, held, packed, rows, sems
 ):
     copy = weight_copies(w_ref, held, sems, FLUX_ROWS)
     for c in range(ROWS // FLUX_ROWS):
         copy(c).start()
-    out_ref[...] = jnp.zeros_like(out_ref)
+    packed[...] = jnp.zeros_like(packed)
     for d in range(RANKS):
-        out_ref[d * OCEAN_SLOTS + CAP] = jnp.broadcast_to(
+        packed[d * OCEAN_SLOTS + CAP] = jnp.broadcast_to(
             label_ref[d : d + 1, :], (NF, COLS)
         ).astype(BF16)
-    difference = air_ref[...] - prior_ref[...]
+    difference = air_ref[0].astype(F32) + air_ref[1].astype(F32) - prior_ref[...]
     for f in range(NF):
         rows[pl.ds(f, ROWS, stride=NF), :] = factor_ref[f] * difference
 
@@ -146,7 +169,11 @@
             flux = rows[pl.ds(pl.multiple_of(b * NF, NF), NF), :].astype(BF16)
             part = jnp.dot(flux, side_by_side(held, b), preferred_element_type=F32).astype(BF16)
             for k in range(K):
-                out_ref[pos_ref[k, b]] = part[:, k * COLS : (k + 1) * COLS]
+                packed[pos_ref[k, b]] = part[:, k * COLS : (k + 1) * COLS]
+
+    done = pltpu.make_async_copy(packed, out_ref, sems.at[ROWS // FLUX_ROWS])
+    done.start()
+    done.wait()
 
 
 WEIGHTS_HELD = [
@@ -157,13 +184,14 @@
 def ocean_flux(pos, labels, air, prior, factors, weights):
     return pl.pallas_call(
         ocean_flux_body,
-        out_shape=jax.ShapeDtypeStruct((RANKS * OCEAN_SLOTS, NF, COLS), BF16),
+        out_shape=pltpu.HBM((RANKS * OCEAN_SLOTS, NF, COLS), BF16),
         in_specs=[SMEM, VMEM, VMEM, VMEM, VMEM, ANY],
-        out_specs=VMEM,
+        out_specs=pl.BlockSpec(memory_space=pltpu.HBM),
         scratch_shapes=WEIGHTS_HELD
         + [
+            pltpu.VMEM((RANKS * OCEAN_SLOTS, NF, COLS), BF16),
             pltpu.VMEM((ROWS * NF, COLS), F32),
-            pltpu.SemaphoreType.DMA((ROWS // FLUX_ROWS,)),
+            pltpu.SemaphoreType.DMA((ROWS // FLUX_ROWS + 1,)),
         ],
         compiler_params=pltpu.CompilerParams(vmem_limit_bytes=32 << 20),
     )(pos, labels, air, prior, factors, weights)
@@ -172,17 +200,20 @@
 def atmos_flux_body(
     pos_ref,
     label_ref,
-    air_ref,
+    own_ref,
     prior_ref,
     factor_ref,
     w_ref,
     share_ref,
     out_ref,
     held,
+    air,
     packed,
     rows,
     sems,
 ):
+    air_copy = pltpu.make_async_copy(own_ref.at[0], air, sems.at[ROWS // FLUX_ROWS])
+    air_copy.start()
     copy = weight_copies(w_ref, held, sems, FLUX_ROWS)
     for c in range(ROWS // FLUX_ROWS):
         copy(c).start()
@@ -192,7 +223,8 @@
     mixed = share_ref[0, 0] * factor_ref[0]
     for f in range(1, NF):
         mixed += share_ref[0, f] * factor_ref[f]
-    flux = mixed * (air_ref[...] - prior_ref[...])
+    air_copy.wait()
+    flux = mixed * (air[...] - prior_ref[...])
     high = flux.astype(BF16).astype(F32)
     rows[...] = jnp.zeros_like(rows)
     rows[pl.ds(0, ROWS, stride=8), :] = high
@@ -212,23 +244,23 @@
     out_ref[...] = packed[...].astype(BF16).reshape(RANKS, ATMOS_SLOTS, COLS)
 
 
-def atmos_flux(pos, labels, air, prior, factors, weights, share):
+def atmos_flux(pos, labels, own, prior, factors, weights, share):
     return pl.pallas_call(
         atmos_flux_body,
         out_shape=jax.ShapeDtypeStruct((RANKS, ATMOS_SLOTS, COLS), BF16),
-        in_specs=[SMEM, VMEM, VMEM, VMEM, VMEM, ANY, SMEM],
+        in_specs=[SMEM, VMEM, ANY, VMEM, VMEM, ANY, SMEM],
         out_specs=VMEM,
         scratch_shapes=WEIGHTS_HELD
         + [
+            pltpu.VMEM((ROWS, COLS), F32),
             pltpu.VMEM((RANKS * ATMOS_SLOTS, COLS), F32),
             pltpu.VMEM((ROWS * 8, COLS), F32),
-            pltpu.SemaphoreType.DMA((ROWS // FLUX_ROWS,)),
+            pltpu.SemaphoreType.DMA((ROWS // FLUX_ROWS + 1,)),
         ],
         compiler_params=pltpu.CompilerParams(vmem_limit_bytes=32 << 20),
-    )(pos, labels, air, prior, factors, weights, share)
-
-
-WIDE = 8
+    )(pos, labels, own, prior, factors, weights, share)
+
+
 EXTENDED = ROWS + 2 * WIDE
 
 
@@ -239,19 +271,6 @@
     )
 
 
-def turned(field, lanes):
-    lanes = lanes % COLS
-    return field if lanes == 0 else pltpu.roll(field, lanes, 1)
-
-
-def sides_body(u_ref, out_ref):
-    _, lane = iotas(ROWS)
-    packed = jnp.zeros((ROWS, COLS), F32)
-    for l in range(LEV):
-        packed = jnp.where(lane // (2 * WIDE) == l, turned(u_ref[l], WIDE + 2 * WIDE * l), packed)
-    out_ref[...] = packed
-
-
 def mate_ends(sides, level):
     return turned(sides, -(2 * WIDE * level + WIDE))
 
@@ -264,7 +283,7 @@
     return pltpu.roll(jnp.where(lane == 0, ends, field), COLS - 1, 1)
 
 
-def second_along(field, axis, index, extent):
+def second_along(field, axis, index):
     phase = index % 4
     total = None
     for shift in range(-3, 4):
@@ -272,13 +291,16 @@
         for p in range(4):
             if 0 <= p + shift < 4:
                 factor = jnp.where(phase == p, F32(SECOND[p, p + shift]), factor)
-        moved = field if shift == 0 else pltpu.roll(field, (-shift) % extent, axis)
+        moved = field if shift == 0 else pltpu.roll(field, (-shift) % field.shape[axis], axis)
         total = factor * moved if total is None else total + factor * moved
     return total
 
 
-def diffused(field, above, below, row, lane):
-    along = second_along(field, 0, row, EXTENDED) + second_along(field, 1, lane, COLS)
+def diffused(field, above, below):
+    groups = field.reshape(EXTENDED // 8, 8, COLS)
+    along = second_along(groups, 1, lax.broadcasted_iota(jnp.int32, (1, 8, COLS), 1))
+    along = along.reshape(EXTENDED, COLS)
+    along += second_along(field, 1, lax.broadcasted_iota(jnp.int32, (1, COLS), 1))
     return field + ATMOS_DIFFUSION * along + MIXING * (above + below - 2.0 * field)
 
 
@@ -306,12 +328,12 @@
     for substep in range(2):
         over = jnp.where(lane < COLS - 2 * WIDE, turned(sides, -2 * WIDE), sides)
         under = jnp.where(lane >= 2 * WIDE, turned(sides, 2 * WIDE), sides)
-        sides = assembled_rows(diffused(sides, over, under, row, lane), row)
+        sides = assembled_rows(diffused(sides, over, under), row)
         edges = jnp.zeros((EXTENDED, COLS), F32)
         for l in range(LEV):
             field = main[l]
             half = assembled_rows(
-                diffused(field, main[min(l + 1, LEV - 1)], main[max(l - 1, 0)], row, lane), row
+                diffused(field, main[min(l + 1, LEV - 1)], main[max(l - 1, 0)]), row
             )
             if substep == 0:
                 first = turned(half, 2 * WIDE * l + WIDE - 1)
@@ -372,12 +394,12 @@
     return total
 
 
-def top_base_body(top_ref, under_ref, mate_ref, before_ref, after_ref, table_ref, out_ref):
+def top_base_body(other_ref, mate_ref, before_ref, after_ref, table_ref, out_ref):
     row, lane = iotas(ROWS)
-    top = top_ref[...]
+    top = other_ref[0].astype(F32)
     spread = neighbour_spread(
         top,
-        mate_ref[...],
+        mate_ref[0].astype(F32),
         before_ref[LEV + 1, WIDE - 1 :, :],
         after_ref[LEV + 1, :1, :],
         before_ref[LEV + 2, WIDE - 1 :, :],
@@ -386,7 +408,7 @@
         row,
         lane,
     )
-    out_ref[...] = top + OCEAN_DIFFUSION * spread + MIXING * (under_ref[...].astype(F32) - top)
+    out_ref[...] = (1.0 - MIXING) * top + other_ref[1].astype(F32) + OCEAN_DIFFUSION * spread
 
 
 def ocean_base_body(o_ref, sides_ref, before_ref, after_ref, table_ref, out_ref, counts_ref):
@@ -410,15 +432,21 @@
         out_ref[l] = field + OCEAN_DIFFUSION * spread + MIXING * (above + below - 2.0 * field)
 
 
-def exchanged(levels, planes):
+def edge_rows(*fields):
+    last = [v[..., ROWS - WIDE :, :].reshape(-1, WIDE, COLS).astype(F32) for v in fields]
+    first = [v[..., :WIDE, :].reshape(-1, WIDE, COLS).astype(F32) for v in fields]
+    return jnp.concatenate(last, axis=0), jnp.concatenate(first, axis=0)
+
+
+def from_neighbours(last, first):
     size = lax.axis_size("gx")
     up = [(i, (i + 1) % size) for i in range(size)]
     down = [(j, i) for i, j in up]
-    mate = lax.ppermute(planes, "gy", [(0, 1), (1, 0)])
-    parts = [levels, mate[:1], planes[1:], mate[1:]]
-    last = jnp.concatenate([v[:, ROWS - WIDE :, :] for v in parts], axis=0)
-    first = jnp.concatenate([v[:, :WIDE, :] for v in parts], axis=0)
-    return mate, lax.ppermute(last, "gx", up), lax.ppermute(first, "gx", down)
+    return lax.ppermute(last, "gx", up), lax.ppermute(first, "gx", down)
+
+
+def from_mate(field):
+    return lax.ppermute(field, "gy", [(0, 1), (1, 0)])
 
 
 def row_hits(labels):
@@ -455,16 +483,23 @@
         pair = jnp.where(lane < RANKS, by_slot[s : s + 1, :], by_slot[s + 1 : s + 2, :])
         pieces.append(jnp.where(row == pair, 1.0, 0.0).astype(BF16))
     hits = jnp.concatenate(pieces, axis=1)
-    for f in range(NF):
-        values = jnp.concatenate(
-            [wide[pl.ds(s * NF + f, RANKS, stride=width), :] for s in range(CAP)], axis=0
-        ).astype(BF16)
-        forcing = jnp.dot(hits, values, preferred_element_type=F32)
-        if f == 0:
-            first_ref[...] = forcing
-        for l in range(LEV):
-            before = base_ref[l] if f == 0 else out_ref[l]
-            out_ref[l] = before + share_ref[l, f] * forcing
+    forcing = []
+    for f in range(0, NF, 2):
+        values = [
+            jnp.concatenate(
+                [wide[pl.ds(s * NF + g, RANKS, stride=width), :] for s in range(CAP)], axis=0
+            )
+            for g in (f, f + 1)
+        ]
+        both = jnp.concatenate(values, axis=1).astype(BF16)
+        summed = jnp.dot(hits, both, preferred_element_type=F32)
+        forcing += [summed[:, :COLS], summed[:, COLS:]]
+    first_ref[...] = forcing[0]
+    for l in range(LEV):
+        level = base_ref[l]
+        for f in range(NF):
+            level += share_ref[l, f] * forcing[f]
+        out_ref[l] = level
 
 
 def ocean_sums(arrived, base, share):
@@ -481,44 +516,50 @@
     )(arrived, base, share)
 
 
-def remap_body(pos_ref, arrived_ref, w_ref, out_ref, held, wide, near, sems):
+def remap_body(pos_ref, arrived_ref, w_ref, out_ref, held, values, own, sems):
     copy = weight_copies(w_ref, held, sems, REMAP_ROWS)
     for c in range(ROWS // REMAP_ROWS):
         copy(c).start()
-    wide[...] = arrived_ref[...].astype(F32).reshape(RANKS * ATMOS_SLOTS, COLS)
-    lane = lax.broadcasted_iota(jnp.int32, (COLS, REMAP_ROWS), 1)
+    slots = RANKS * ATMOS_SLOTS
+    by_column = arrived_ref[...].astype(F32).reshape(slots, COLS).T.astype(BF16)
+    at = lax.broadcasted_iota(jnp.int32, (slots, ROWS), 0)
+    groups = ROWS // COLS
+    for k in range(K):
+        hits = jnp.where(at == pos_ref[K + k : K + k + 1, :], 1.0, 0.0).astype(BF16)
+        found = jnp.dot(by_column, hits, preferred_element_type=F32).astype(BF16)
+        for g in range(groups):
+            values[g, k * COLS : (k + 1) * COLS, :] = found[:, g * COLS : (g + 1) * COLS]
+    lane = lax.broadcasted_iota(jnp.int32, (COLS, COLS), 1)
+    parts = COLS // REMAP_ROWS
 
     @pl.loop(0, ROWS // REMAP_ROWS)
     def _(c):
-        for i in range(REMAP_ROWS):
-            for k in range(K):
-                value = wide[pl.ds(pos_ref[K + k, c * REMAP_ROWS + i], 1), :]
-                near[i : i + 1, k * COLS : (k + 1) * COLS] = value
-        values = near[...].astype(BF16)
         copy(c).wait()
         block = held.at[pl.ds(c * REMAP_ROWS, REMAP_ROWS)]
         tiles = jnp.concatenate(
             [block[:, k].reshape(REMAP_ROWS * COLS, COLS) for k in range(K)], axis=1
         )
-        crossed = lax.dot_general(
-            tiles, values, (((1,), (1,)), ((), ())), preferred_element_type=F32
-        )
-        own = jnp.zeros((COLS, REMAP_ROWS), F32)
+        crossed = jnp.dot(tiles, values[c // parts], preferred_element_type=F32)
+        kept = own[c // parts]
         for i in range(REMAP_ROWS):
-            own = jnp.where(lane == i, crossed[i * COLS : (i + 1) * COLS], own)
-        out_ref[pl.ds(pl.multiple_of(c * REMAP_ROWS, REMAP_ROWS), REMAP_ROWS), :] = own.T
+            mine = lane == (c % parts) * REMAP_ROWS + i
+            kept = jnp.where(mine, crossed[i * COLS : (i + 1) * COLS], kept)
+        own[c // parts] = kept
+
+    for g in range(groups):
+        out_ref[g * COLS : (g + 1) * COLS, :] = own[g].T
 
 
 def remap(pos, arrived, weights):
     return pl.pallas_call(
         remap_body,
         out_shape=jax.ShapeDtypeStruct((ROWS, COLS), F32),
-        in_specs=[SMEM, VMEM, ANY],
+        in_specs=[VMEM, VMEM, ANY],
         out_specs=VMEM,
         scratch_shapes=WEIGHTS_HELD
         + [
-            pltpu.VMEM((RANKS * ATMOS_SLOTS, COLS), F32),
-            pltpu.VMEM((REMAP_ROWS, K * COLS), F32),
+            pltpu.VMEM((ROWS // COLS, K * COLS, COLS), BF16),
+            pltpu.VMEM((ROWS // COLS, COLS, COLS), F32),
             pltpu.SemaphoreType.DMA((ROWS // REMAP_ROWS,)),
         ],
         compiler_params=pltpu.CompilerParams(vmem_limit_bytes=32 << 20),
@@ -545,37 +586,39 @@
     plane = jax.ShapeDtypeStruct((ROWS, COLS), F32)
     swap = [(0, 1), (1, 0)]
 
-    other_top = lax.ppermute(own[0], "comp", swap)
-    other_under = lax.ppermute(own[1].astype(BF16), "comp", swap)
-    pos, labels = positions(destination_water_peer, destination_water_line)
-
-    def sides_of(levels):
-        return shadow_call(sides_body, plane, [VMEM])(levels)
+    cross, sides, pos, labels = first_kernel(
+        lax.axis_index("comp").reshape(1), own, destination_water_peer, destination_water_line
+    )
+    other = lax.ppermute(cross, "comp", [(0, 1), (1, 0)])
+    sides = from_mate(sides)
 
     def atmosphere_early():
         packed = atmos_flux(
             pos,
             labels,
-            own[0],
+            own,
             prior_marine_heat,
             transfer_factor_table,
             interpolation_matrix_blocks,
             depth_fraction_matrix,
         )
-        rows = jnp.zeros((LEV + 1, WIDE, COLS), F32)
-        return packed, jnp.zeros((1, ROWS, COLS), F32), rows, rows
+        nothing = jnp.zeros((LEV + 1, WIDE, COLS), F32)
+        return packed, nothing, nothing
 
     def ocean_early():
-        halo = exchanged(own, sides_of(own)[None])
+        halo = from_neighbours(*edge_rows(own, sides))
         return jnp.zeros((RANKS, ATMOS_SLOTS, COLS), BF16), *halo
 
-    packed, *ocean_halo = lax.cond(is_atmosphere_side, atmosphere_early, ocean_early)
+    packed, *ocean_rows = lax.cond(is_atmosphere_side, atmosphere_early, ocean_early)
 
     def atmosphere():
-        arrived = to_peers(packed)
-        mate, before, after = exchanged(own, jnp.stack([sides_of(own), other_top]))
-        base = shadow_call(top_base_body, plane, [VMEM] * 6)(
-            other_top, other_under, mate[1], before, after, adjacent_cell_table
+        mate = from_mate(other)
+        edges = edge_rows(own, sides, other[0], mate[0])
+        payload, *edges = lax.optimization_barrier((packed, *edges))
+        before, after = from_neighbours(*edges)
+        arrived = to_peers(payload)
+        base = shadow_call(top_base_body, plane, [VMEM] * 5)(
+            other, mate, before, after, adjacent_cell_table
         )
         picked = call(
             top_body, jax.ShapeDtypeStruct((RANKS, ATMOS_SLOTS, COLS), BF16), [VMEM, VMEM]
@@ -584,26 +627,25 @@
         wide = pltpu.VMEM((LEV, EXTENDED, COLS), F32)
         final = shadow_call(
             substeps_body, block, [VMEM] * 4 + [ANY], scratch_shapes=[wide, wide]
-        )(own, mate[0], before, after, picked)
+        )(own, sides, before, after, picked)
         return final, remap(pos, returned, interpolation_matrix_blocks)
 
     def ocean():
         payload = ocean_flux(
             pos,
             labels,
-            other_top,
+            other,
             prior_marine_heat,
             transfer_factor_table,
             interpolation_matrix_blocks,
         )
         arrived = to_peers(payload.reshape(RANKS, OCEAN_SLOTS * NF, COLS))
-        mate, before, after = ocean_halo
         base = shadow_call(
             ocean_base_body,
             block,
             [VMEM] * 5,
             scratch_shapes=[pltpu.VMEM((len(ORDER), ROWS, COLS), F32)],
-        )(own, mate[0], before, after, adjacent_cell_table)
+        )(own, sides, *ocean_rows, adjacent_cell_table)
         return ocean_sums(
             arrived.reshape(RANKS * OCEAN_SLOTS, NF, COLS), base, depth_fraction_matrix
         )

time: 75.9 us -> 69.2 us (0.912)
  the two profiles are of different devices: /device:TPU:1 before, /device:TPU:65 now
where the time goes in v4:
time: 69.2 us; the launch traced here: 68.8 us
  waiting for transfers between devices  30.3 us (44%)
  Pallas kernels  19.1 us (28%)
  starting transfers between devices  16.3 us (24%)
  local copies, waits for them, and re-layouts  2.21 us (3%)
    all_to_all x1, waiting for transfers between devices, to_peers(): lax.all_to_all(payload, ('gx', 'gy'), split_axis=0, concat_axis=0, tiled=...  28.1 us
    all_to_all x1, starting transfers between devices, to_peers(): lax.all_to_all(payload, ('gx', 'gy'), split_axis=0, concat_axis=0, tiled=...  9.4 us
    pallas_call x1, Pallas kernels, ocean_flux(): pl.pallas_call(ocean_flux_body, out_shape=pltpu.HBM((RANKS * OCEAN_SLOTS,...  9.04 us
    ppermute x2, starting transfers between devices, from_neighbours(): return (lax.ppermute(last, 'gx', up), lax.ppermute(first, 'gx', down))  6.15 us
    pallas_call x1, Pallas kernels, ocean(): shadow_call(ocean_base_body, block, [VMEM] * 5, scratch_shapes=[pltpu.VME...  5.03 us
    pallas_call x1, Pallas kernels, ocean_sums(): pl.pallas_call(sums_body, out_shape=(jax.ShapeDtypeStruct((LEV, ROWS, COL...  3.42 us
    pallas_call x1, Pallas kernels, first_kernel(): call(first_body, (jax.ShapeDtypeStruct((2, ROWS, COLS), BF16), jax.ShapeD...  1.63 us
  transfers between devices with their start and end apart: 5, of which 3 were waited for; matrix products, arithmetic and copies ran while one was open for 1% of the time, Pallas kernels for 7%

profile of v4, /device:TPU:65, one launch (start us, length us, event | category | flops | bytes accessed | tf_op | source)
XLA Modules:
  0.0 68.8 jit_solution(17355777614369579732)
XLA Ops:
  0.6 0.7 copy-done
  1.3 0.7 copy-done.1
  2.0 1.6 %shard_map.95 = (bf16[2,256,128]{2,1,0:T(8,128)(2,1)S(1)}, f32[256,128]{1,0:T(8,128)S(1)}, s32[4,256]{1,0:T(4,128)S(1)}, f32[64,128]{1,0:T(8,128)S(1)}) custom-call(s32[1]{0:T(128)} %bitcast.10.side_ref, f32[8,256,128]{2,1,0:T(8,128)} %bitcast.21, s32[2,256]{1,0:T(2,128)S(1)} %bitcast.19, s32[2,256]{1,0:T(2,128)S(1)} %bitcast.20), custom_call_target="tpu_custom_call" | custom-call | tf_op jit(solution)/shard_map/pallas_call | solution.py:121
  3.6 0.8 %collective-permute-start.6 = (f32[256,128]{1,0:T(8,128)S(1)}, f32[256,128]{1,0:T(8,128)S(1)}, u32[]{:S(2)}, u32[]{:S(2)}) collective-permute-start(f32[256,128]{1,0:T(8,128)S(1)} %get-tuple-element.105), channel_id=1, source_target_pairs={{0,1},{1,0},{2,3},{3,2},{4,5},{5,4},{6,7},{7,6},{8,9},{9,8},{10,11... | collective-permute-start | bytes 393224 | tf_op jit(solution)/shard_map/ppermute | solution.py:449
  4.4 0.0 collective-permute-start.5
  4.4 1.0 %collective-permute-done.6 = f32[256,128]{1,0:T(8,128)S(1)} collective-permute-done((f32[256,128]{1,0:T(8,128)S(1)}, f32[256,128]{1,0:T(8,128)S(1)}, u32[]{:S(2)}, u32[]{:S(2)}) %collective-permute-start.6) | collective-permute-done | bytes 131104 | tf_op jit(solution)/shard_map/ppermute | solution.py:449
  5.4 8.3 %conditional.2 = (bf16[64,24,128]{2,1,0:T(8,128)(2,1)S(1)}, f32[9,8,128]{2,1,0:T(8,128)S(1)}, f32[9,8,128]{2,1,0:T(8,128)S(1)}) conditional(s32[]{:T(128)} %convert_element_type.24, (f32[8,256,128]{2,1,0:T(8,128)}, f32[256,128]{1,0:T(8,128)S(1)}) %tuple.50, (s32[4,256]{1,0:T(4,128)S(1)}, f32[64,128]{1,0:T(8,128)S(1)}, f32[8,256,128]{2,1,0:T(8,128)}, ...), branch_computations={%region_0.0_spmd, %region_1.0_spmd} | conditional | flops 18432 | bytes 983146 | solution.py:612
  5.4 0.8 %fusion = (f32[8,8,128]{2,1,0:T(8,128)S(1)}, f32[8,8,128]{2,1,0:T(8,128)S(1)}) fusion(f32[8,256,128]{2,1,0:T(8,128)} %get-tuple-element.60), kind=kLoop, calls=%fused_computation.12 | loop fusion | bytes 131072 | tf_op jit(solution)/shard_map/cond/branch_0_fun/slice | solution.py:437
  6.2 1.4 %collective-permute-start = (f32[9,8,128]{2,1,0:T(8,128)S(1)}, f32[9,8,128]{2,1,0:T(8,128)S(1)}, u32[]{:S(2)}, u32[]{:S(2)}) collective-permute-start(f32[9,8,128]{2,1,0:T(8,128)S(1)} %pad_maximum_fusion), channel_id=1, source_target_pairs={{0,2},{2,4},{4,6},{6,8},{8,10},{10,12},{12,14},{14,16},{16,18},{18... | collective-permute-start | bytes 110600 | tf_op jit(solution)/shard_map/cond/branch_0_fun/ppermute | solution.py:445
  7.6 4.7 %collective-permute-start.1 = (f32[9,8,128]{2,1,0:T(8,128)S(1)}, f32[9,8,128]{2,1,0:T(8,128)S(1)}, u32[]{:S(2)}, u32[]{:S(2)}) collective-permute-start(f32[9,8,128]{2,1,0:T(8,128)S(1)} %pad_maximum_fusion.1), channel_id=1, source_target_pairs={{2,0},{4,2},{6,4},{8,6},{10,8},{12,10},{14,12},{16,14},{18,16},{20... | collective-permute-start | bytes 110600 | tf_op jit(solution)/shard_map/cond/branch_0_fun/ppermute | solution.py:445
  12.3 1.3 %collective-permute-done = f32[9,8,128]{2,1,0:T(8,128)S(1)} collective-permute-done((f32[9,8,128]{2,1,0:T(8,128)S(1)}, f32[9,8,128]{2,1,0:T(8,128)S(1)}, u32[]{:S(2)}, u32[]{:S(2)}) %collective-permute-start) | collective-permute-done | bytes 36896 | tf_op jit(solution)/shard_map/cond/branch_0_fun/ppermute | solution.py:445
  13.6 0.0 collective-permute-done.1
  13.6 0.1 broadcast.4
  13.6 0.0 collective-permute-done.5
  13.6 55.1 %conditional.3 = (f32[1,8,256,128]{3,2,1,0:T(8,128)}, f32[1,256,128]{2,1,0:T(8,128)}) conditional(s32[]{:T(128)} %convert_element_type.24, (s32[4,256]{1,0:T(4,128)S(1)}, f32[64,128]{1,0:T(8,128)S(1)}, bf16[2,256,128]{2,1,0:T(8,128)(2,1)S(1)}, f32[256,128]{1,0:T(8,128)}, f32[8,256,128]{2,1,0:T(8,128)}, ...), branch_computations={%region_2.0_spmd, %region_3.0_spmd} | conditional | flops 71680 | bytes 10936660 | solution.py:653
  13.7 0.0 copy-start.4
  13.7 0.0 copy-start.8
  13.7 9.0 %branch_0_fun.3 = bf16[1216,8,128]{2,1,0:T(8,128)(2,1)} custom-call(s32[4,256]{1,0:T(4,128)S(1)} %get-tuple-element.69.pos_ref, f32[64,128]{1,0:T(8,128)S(1)} %get-tuple-element.70.label_ref, bf16[2,256,128]{2,1,0:T(8,128)(2,1)S(1)} %get-tuple-element.71.air_ref, f32[256,128]{1,0:T(8,128)} %get-tuple-element.72.prior_ref, ...), custom_call_target="tpu_custom_call" | custom-call | tf_op jit(solution)/shard_map/cond/branch_0_fun/pallas_call | solution.py:185
  22.8 9.4 %all-to-all-start = ((bf16[64,152,128]{2,1,0:T(8,128)(2,1)}), bf16[64,152,128]{2,1,0:T(8,128)(2,1)S(1)}, u32[]{:S(2)}, u32[]{:S(2)}) async-start(bf16[64,152,128]{2,1,0:T(8,128)(2,1)} %bitcast.26), calls=%async_computation | async-start | bytes 4980736 | tf_op jit(solution)/shard_map/cond/branch_0_fun/all_to_all | solution.py:570
  32.2 0.0 copy-start.10
  32.2 5.0 %branch_0_fun.4.base_ref = f32[8,256,128]{2,1,0:T(8,128)S(1)} custom-call(f32[8,256,128]{2,1,0:T(8,128)} %get-tuple-element.75.o_ref, f32[256,128]{1,0:T(8,128)} %copy-done.4, f32[9,8,128]{2,1,0:T(8,128)} %copy-done.8, f32[9,8,128]{2,1,0:T(8,128)} %copy-done.9, s32[6,256,128]{2,1,0:T(8,128)} %get-tuple-element.79.table_ref), custom_call_target="tpu_custom_call" | custom-call | tf_op jit(solution)/shard_map/cond/branch_0_fun/pallas_call | solution.py:643
  37.2 28.1 %all-to-all-done = bf16[64,152,128]{2,1,0:T(8,128)(2,1)S(1)} async-done(((bf16[64,152,128]{2,1,0:T(8,128)(2,1)}), bf16[64,152,128]{2,1,0:T(8,128)(2,1)S(1)}, u32[]{:S(2)}, u32[]{:S(2)}) %all-to-all-start) | async-done | bytes 2490400 | tf_op jit(solution)/shard_map/cond/branch_0_fun/all_to_all | solution.py:570
  65.3 0.0 copy-done.10
  65.3 3.4 %branch_0_fun.5 = (f32[8,256,128]{2,1,0:T(8,128)}, f32[256,128]{1,0:T(8,128)}) custom-call(bf16[1216,8,128]{2,1,0:T(8,128)(2,1)S(1)} %bitcast.18, f32[8,256,128]{2,1,0:T(8,128)S(1)} %branch_0_fun.4.base_ref, f32[8,8]{1,0:T(8,128)S(1)} %copy-done.10), custom_call_target="tpu_custom_call" | custom-call | tf_op jit(solution)/shard_map/cond/branch_0_fun/pallas_call | solution.py:506
  (9 shorter events, 0.0 us)
Async XLA Ops:
  0.6 0.7 copy-start
  1.3 0.7 copy-start.1
  3.6 1.7 %collective-permute-start.6 = (f32[256,128]{1,0:T(8,128)S(1)}, f32[256,128]{1,0:T(8,128)S(1)}, u32[]{:S(2)}, u32[]{:S(2)}) collective-permute-start(f32[256,128]{1,0:T(8,128)S(1)} %get-tuple-element.105), channel_id=1, source_target_pairs={{0,1},{1,0},{2,3},{3,2},{4,5},{5,4},{6,7},{7,6},{8,9},{9,8},{10,11... | collective-permute-start | bytes 393224 | tf_op jit(solution)/shard_map/ppermute | solution.py:449
  4.4 9.3 %collective-permute-start.5 = (bf16[2,256,128]{2,1,0:T(8,128)(2,1)S(1)}, bf16[2,256,128]{2,1,0:T(8,128)(2,1)S(1)}, u32[]{:S(2)}, u32[]{:S(2)}) collective-permute-start(bf16[2,256,128]{2,1,0:T(8,128)(2,1)S(1)} %get-tuple-element.104), channel_id=1, source_target_pairs={{0,64},{64,0},{1,65},{65,1},{2,66},{66,2},{3,67},{67,3},{4,68},{68... | collective-permute-start | bytes 393224 | tf_op jit(solution)/shard_map/ppermute | solution.py:592
  6.2 7.4 %collective-permute-start = (f32[9,8,128]{2,1,0:T(8,128)S(1)}, f32[9,8,128]{2,1,0:T(8,128)S(1)}, u32[]{:S(2)}, u32[]{:S(2)}) collective-permute-start(f32[9,8,128]{2,1,0:T(8,128)S(1)} %pad_maximum_fusion), channel_id=1, source_target_pairs={{0,2},{2,4},{4,6},{6,8},{8,10},{10,12},{12,14},{14,16},{16,18},{18... | collective-permute-start | bytes 110600 | tf_op jit(solution)/shard_map/cond/branch_0_fun/ppermute | solution.py:445
  7.6 6.0 %collective-permute-start.1 = (f32[9,8,128]{2,1,0:T(8,128)S(1)}, f32[9,8,128]{2,1,0:T(8,128)S(1)}, u32[]{:S(2)}, u32[]{:S(2)}) collective-permute-start(f32[9,8,128]{2,1,0:T(8,128)S(1)} %pad_maximum_fusion.1), channel_id=1, source_target_pairs={{2,0},{4,2},{6,4},{8,6},{10,8},{12,10},{14,12},{16,14},{18,16},{20... | collective-permute-start | bytes 110600 | tf_op jit(solution)/shard_map/cond/branch_0_fun/ppermute | solution.py:445
  13.7 9.1 %copy-start.4 = (f32[256,128]{1,0:T(8,128)}, f32[256,128]{1,0:T(8,128)S(1)}, u32[]{:S(2)}) copy-start(f32[256,128]{1,0:T(8,128)S(1)} %get-tuple-element.76.sides_ref) | copy-start | bytes 393220 | tf_op jit(solution)/shard_map/cond
  13.7 9.1 %copy-start.8 = (f32[9,8,128]{2,1,0:T(8,128)}, f32[9,8,128]{2,1,0:T(8,128)S(1)}, u32[]{:S(2)}) copy-start(f32[9,8,128]{2,1,0:T(8,128)S(1)} %get-tuple-element.77.before_ref) | copy-start | bytes 110596 | tf_op jit(solution)/shard_map/cond
  13.7 9.1 %copy-start.9 = (f32[9,8,128]{2,1,0:T(8,128)}, f32[9,8,128]{2,1,0:T(8,128)S(1)}, u32[]{:S(2)}) copy-start(f32[9,8,128]{2,1,0:T(8,128)S(1)} %get-tuple-element.78.after_ref) | copy-start | bytes 110596 | tf_op jit(solution)/shard_map/cond
  22.8 42.6 %all-to-all-start = ((bf16[64,152,128]{2,1,0:T(8,128)(2,1)}), bf16[64,152,128]{2,1,0:T(8,128)(2,1)S(1)}, u32[]{:S(2)}, u32[]{:S(2)}) async-start(bf16[64,152,128]{2,1,0:T(8,128)(2,1)} %bitcast.26), calls=%async_computation | async-start | bytes 4980736 | tf_op jit(solution)/shard_map/cond/branch_0_fun/all_to_all | solution.py:570
  32.2 33.2 %copy-start.10 = (f32[8,8]{1,0:T(8,128)S(1)}, f32[8,8]{1,0:T(8,128)}, u32[]{:S(2)}) copy-start(f32[8,8]{1,0:T(8,128)} %get-tuple-element.80.share_ref) | copy-start | bytes 772 | tf_op jit(solution)/shard_map/cond

commit v5 on v4

--- a/solution.py
+++ b/solution.py
@@ -14,6 +14,7 @@
 
 RANKS = 64
 CAP = 18
+CORES = 2
 LEV = 8
 NF = 8
 ROWS = 256
@@ -26,6 +27,7 @@
 VMEM = pl.BlockSpec(memory_space=pltpu.VMEM)
 SMEM = pl.BlockSpec(memory_space=pltpu.SMEM)
 ANY = pl.BlockSpec(memory_space=pl.ANY)
+HBM = pl.BlockSpec(memory_space=pltpu.HBM)
 F32 = jnp.float32
 BF16 = jnp.bfloat16
 
@@ -60,9 +62,13 @@
     )
 
 
-def shadow_call(body, out_shape, specs, **params):
-    nothing = pl.CostEstimate(flops=0, bytes_accessed=0, transcendentals=0)
-    return call(body, out_shape, specs, cost_estimate=nothing, **params)
+def shadow_call(body, out_shape, specs, us=0, **params):
+    cost = pl.CostEstimate(flops=0, bytes_accessed=us * 3_690_000, transcendentals=0)
+    return call(body, out_shape, specs, cost_estimate=cost, **params)
+
+
+def unused(shape, dtype):
+    return pl.pallas_call(lambda out_ref: None, out_shape=pltpu.HBM(shape, dtype), out_specs=HBM)()
 
 
 def route(peer_ref, line_ref, pos_ref, label_ref):
@@ -102,36 +108,42 @@
     return field if lanes == 0 else pltpu.roll(field, lanes, 1)
 
 
-def first_body(side_ref, own_ref, peer_ref, line_ref, cross_ref, sides_ref, pos_ref, label_ref):
-    top = own_ref[0]
+def cross_body(side_ref, own_ref, out_ref, held, sem):
+    copy = pltpu.make_async_copy(own_ref.at[pl.ds(0, 2)], held, sem)
+    copy.start()
+    copy.wait()
+    top = held[0]
     high = top.astype(BF16)
     rest = top - high.astype(F32)
-    cross_ref[0] = high
-    other = MIXING * own_ref[1] + (1.0 - MIXING) * rest
-    cross_ref[1] = jnp.where(side_ref[0] == 0, rest, other).astype(BF16)
+    out_ref[0] = high
+    other = MIXING * held[1] + (1.0 - MIXING) * rest
+    out_ref[1] = jnp.where(side_ref[0] == 0, rest, other).astype(BF16)
+
+
+def cross_kernel(side, own):
+    return call(
+        cross_body,
+        jax.ShapeDtypeStruct((2, ROWS, COLS), BF16),
+        [SMEM, HBM],
+        scratch_shapes=[pltpu.VMEM((2, ROWS, COLS), F32), pltpu.SemaphoreType.DMA],
+    )(side, own)
+
+
+def packed_sides(levels, lane):
+    packed = jnp.zeros(lane.shape, F32)
+    for l, level in enumerate(levels):
+        packed = jnp.where(lane // (2 * WIDE) == l, turned(level, WIDE + 2 * WIDE * l), packed)
+    return packed
+
+
+def sides_body(own_ref, out_ref):
     lane = lax.broadcasted_iota(jnp.int32, (ROWS, COLS), 1)
-    packed = jnp.zeros((ROWS, COLS), F32)
-    for l in range(LEV):
-        packed = jnp.where(lane // (2 * WIDE) == l, turned(own_ref[l], WIDE + 2 * WIDE * l), packed)
-    sides_ref[...] = packed
-    route(peer_ref, line_ref, pos_ref, label_ref)
-
-
-def first_kernel(side, own, peer, line):
-    return call(
-        first_body,
-        (
-            jax.ShapeDtypeStruct((2, ROWS, COLS), BF16),
-            jax.ShapeDtypeStruct((ROWS, COLS), F32),
-            jax.ShapeDtypeStruct((2 * K, ROWS), jnp.int32),
-            jax.ShapeDtypeStruct((RANKS, COLS), F32),
-        ),
-        [SMEM, VMEM, VMEM, VMEM],
-    )(side, own, peer.T, line.T)
+    out_ref[...] = packed_sides([own_ref[l] for l in range(LEV)], lane)
 
 
 FLUX_ROWS = 16
 REMAP_ROWS = 32
+CHUNKS = ROWS // FLUX_ROWS
 
 
 def weight_copies(source, held, sems, per):
@@ -146,22 +158,72 @@
     return jnp.concatenate([held[b, k] for k in range(K)], axis=1)
 
 
+WEIGHTS_HELD = [
+    pltpu.VMEM((ROWS, K, COLS, COLS), BF16),
+]
+ROUTING = [
+    pltpu.VMEM((K, ROWS), jnp.int32),
+    pltpu.VMEM((K, ROWS), jnp.int32),
+    pltpu.VMEM((RANKS, COLS), F32),
+    pltpu.SMEM((2 * K, ROWS), jnp.int32),
+]
+FIELDS = [
+    pltpu.VMEM((ROWS, COLS), F32),
+    pltpu.VMEM((NF, ROWS, COLS), F32),
+]
+
+
 def ocean_flux_body(
-    pos_ref, label_ref, air_ref, prior_ref, factor_ref, w_ref, out_ref, held, packed, rows, sems
+    peer_ref,
+    line_ref,
+    air_ref,
+    prior_ref,
+    factor_ref,
+    w_ref,
+    out_ref,
+    held,
+    peer,
+    line,
+    label,
+    pos,
+    prior,
+    factor,
+    pos_rows,
+    packed,
+    rows,
+    sems,
 ):
     copy = weight_copies(w_ref, held, sems, FLUX_ROWS)
-    for c in range(ROWS // FLUX_ROWS):
+    index_copies = [
+        pltpu.make_async_copy(peer_ref, peer, sems.at[CHUNKS]),
+        pltpu.make_async_copy(line_ref, line, sems.at[CHUNKS + 1]),
+    ]
+    field_copies = [
+        pltpu.make_async_copy(prior_ref, prior, sems.at[CHUNKS + 2]),
+        pltpu.make_async_copy(factor_ref, factor, sems.at[CHUNKS + 3]),
+    ]
+    for started in index_copies + field_copies:
+        started.start()
+    for c in range(CHUNKS):
         copy(c).start()
     packed[...] = jnp.zeros_like(packed)
+    for started in index_copies:
+        started.wait()
+    route(peer, line, pos_rows, label)
+    to_scalars = pltpu.make_async_copy(pos_rows, pos, sems.at[CHUNKS + 4])
+    to_scalars.start()
     for d in range(RANKS):
-        packed[d * OCEAN_SLOTS + CAP] = jnp.broadcast_to(
-            label_ref[d : d + 1, :], (NF, COLS)
-        ).astype(BF16)
-    difference = air_ref[0].astype(F32) + air_ref[1].astype(F32) - prior_ref[...]
+        packed[d * OCEAN_SLOTS + CAP] = jnp.broadcast_to(label[d : d + 1, :], (NF, COLS)).astype(
+            BF16
+        )
+    for started in field_copies:
+        started.wait()
+    difference = air_ref[0].astype(F32) + air_ref[1].astype(F32) - prior[...]
     for f in range(NF):
-        rows[pl.ds(f, ROWS, stride=NF), :] = factor_ref[f] * difference
-
-    @pl.loop(0, ROWS // FLUX_ROWS)
+        rows[pl.ds(f, ROWS, stride=NF), :] = factor[f] * difference
+    to_scalars.wait()
+
+    @pl.loop(0, CHUNKS)
     def _(c):
         copy(c).wait()
         for i in range(FLUX_ROWS):
@@ -169,68 +231,89 @@
             flux = rows[pl.ds(pl.multiple_of(b * NF, NF), NF), :].astype(BF16)
             part = jnp.dot(flux, side_by_side(held, b), preferred_element_type=F32).astype(BF16)
             for k in range(K):
-                packed[pos_ref[k, b]] = part[:, k * COLS : (k + 1) * COLS]
-
-    done = pltpu.make_async_copy(packed, out_ref, sems.at[ROWS // FLUX_ROWS])
+                packed[pos[k, b]] = part[:, k * COLS : (k + 1) * COLS]
+
+    done = pltpu.make_async_copy(packed, out_ref, sems.at[CHUNKS + 5])
     done.start()
     done.wait()
 
 
-WEIGHTS_HELD = [
-    pltpu.VMEM((ROWS, K, COLS, COLS), BF16),
-]
-
-
-def ocean_flux(pos, labels, air, prior, factors, weights):
+def ocean_flux(peer, line, air, prior, factors, weights):
     return pl.pallas_call(
         ocean_flux_body,
         out_shape=pltpu.HBM((RANKS * OCEAN_SLOTS, NF, COLS), BF16),
-        in_specs=[SMEM, VMEM, VMEM, VMEM, VMEM, ANY],
-        out_specs=pl.BlockSpec(memory_space=pltpu.HBM),
+        in_specs=[HBM, HBM, VMEM, HBM, HBM, HBM],
+        out_specs=HBM,
         scratch_shapes=WEIGHTS_HELD
+        + ROUTING
+        + FIELDS
         + [
+            pltpu.VMEM((2 * K, ROWS), jnp.int32),
             pltpu.VMEM((RANKS * OCEAN_SLOTS, NF, COLS), BF16),
             pltpu.VMEM((ROWS * NF, COLS), F32),
-            pltpu.SemaphoreType.DMA((ROWS // FLUX_ROWS + 1,)),
+            pltpu.SemaphoreType.DMA((CHUNKS + 6,)),
         ],
         compiler_params=pltpu.CompilerParams(vmem_limit_bytes=32 << 20),
-    )(pos, labels, air, prior, factors, weights)
+    )(peer.T, line.T, air, prior, factors, weights)
 
 
 def atmos_flux_body(
-    pos_ref,
-    label_ref,
+    peer_ref,
+    line_ref,
     own_ref,
     prior_ref,
     factor_ref,
     w_ref,
     share_ref,
     out_ref,
+    pos_ref,
     held,
+    peer,
+    line,
+    label,
+    pos,
+    prior,
+    factor,
     air,
     packed,
     rows,
     sems,
 ):
-    air_copy = pltpu.make_async_copy(own_ref.at[0], air, sems.at[ROWS // FLUX_ROWS])
-    air_copy.start()
     copy = weight_copies(w_ref, held, sems, FLUX_ROWS)
-    for c in range(ROWS // FLUX_ROWS):
+    index_copies = [
+        pltpu.make_async_copy(peer_ref, peer, sems.at[CHUNKS]),
+        pltpu.make_async_copy(line_ref, line, sems.at[CHUNKS + 1]),
+    ]
+    field_copies = [
+        pltpu.make_async_copy(prior_ref, prior, sems.at[CHUNKS + 2]),
+        pltpu.make_async_copy(own_ref.at[0], air, sems.at[CHUNKS + 3]),
+        pltpu.make_async_copy(factor_ref, factor, sems.at[CHUNKS + 4]),
+    ]
+    for started in index_copies + field_copies:
+        started.start()
+    for c in range(CHUNKS):
         copy(c).start()
     packed[...] = jnp.zeros_like(packed)
+    rows[...] = jnp.zeros_like(rows)
+    for started in index_copies:
+        started.wait()
+    route(peer, line, pos_ref, label)
+    to_scalars = pltpu.make_async_copy(pos_ref, pos, sems.at[CHUNKS + 5])
+    to_scalars.start()
     for d in range(RANKS):
-        packed[d * ATMOS_SLOTS + CAP : d * ATMOS_SLOTS + CAP + 1, :] = label_ref[d : d + 1, :]
-    mixed = share_ref[0, 0] * factor_ref[0]
+        packed[d * ATMOS_SLOTS + CAP : d * ATMOS_SLOTS + CAP + 1, :] = label[d : d + 1, :]
+    for started in field_copies:
+        started.wait()
+    mixed = share_ref[0, 0] * factor[0]
     for f in range(1, NF):
-        mixed += share_ref[0, f] * factor_ref[f]
-    air_copy.wait()
-    flux = mixed * (air[...] - prior_ref[...])
+        mixed += share_ref[0, f] * factor[f]
+    flux = mixed * (air[...] - prior[...])
     high = flux.astype(BF16).astype(F32)
-    rows[...] = jnp.zeros_like(rows)
     rows[pl.ds(0, ROWS, stride=8), :] = high
     rows[pl.ds(1, ROWS, stride=8), :] = flux - high
-
-    @pl.loop(0, ROWS // FLUX_ROWS)
+    to_scalars.wait()
+
+    @pl.loop(0, CHUNKS)
     def _(c):
         copy(c).wait()
         for i in range(FLUX_ROWS):
@@ -239,26 +322,31 @@
             part = jnp.dot(pair, side_by_side(held, b), preferred_element_type=F32)
             part = part[0:1, :] + part[1:2, :]
             for k in range(K):
-                packed[pl.ds(pos_ref[K + k, b], 1), :] = part[:, k * COLS : (k + 1) * COLS]
+                packed[pl.ds(pos[K + k, b], 1), :] = part[:, k * COLS : (k + 1) * COLS]
 
     out_ref[...] = packed[...].astype(BF16).reshape(RANKS, ATMOS_SLOTS, COLS)
 
 
-def atmos_flux(pos, labels, own, prior, factors, weights, share):
+def atmos_flux(peer, line, own, prior, factors, weights, share):
     return pl.pallas_call(
         atmos_flux_body,
-        out_shape=jax.ShapeDtypeStruct((RANKS, ATMOS_SLOTS, COLS), BF16),
-        in_specs=[SMEM, VMEM, ANY, VMEM, VMEM, ANY, SMEM],
-        out_specs=VMEM,
+        out_shape=(
+            jax.ShapeDtypeStruct((RANKS, ATMOS_SLOTS, COLS), BF16),
+            jax.ShapeDtypeStruct((2 * K, ROWS), jnp.int32),
+        ),
+        in_specs=[HBM, HBM, HBM, HBM, HBM, HBM, SMEM],
+        out_specs=(VMEM, VMEM),
         scratch_shapes=WEIGHTS_HELD
+        + ROUTING
+        + FIELDS
         + [
             pltpu.VMEM((ROWS, COLS), F32),
             pltpu.VMEM((RANKS * ATMOS_SLOTS, COLS), F32),
             pltpu.VMEM((ROWS * 8, COLS), F32),
-            pltpu.SemaphoreType.DMA((ROWS // FLUX_ROWS + 1,)),
+            pltpu.SemaphoreType.DMA((CHUNKS + 6,)),
         ],
         compiler_params=pltpu.CompilerParams(vmem_limit_bytes=32 << 20),
-    )(pos, labels, own, prior, factors, weights, share)
+    )(peer.T, line.T, own, prior, factors, weights, share)
 
 
 EXTENDED = ROWS + 2 * WIDE
@@ -297,9 +385,9 @@
 
 
 def diffused(field, above, below):
-    groups = field.reshape(EXTENDED // 8, 8, COLS)
+    groups = field.reshape(-1, 8, COLS)
     along = second_along(groups, 1, lax.broadcasted_iota(jnp.int32, (1, 8, COLS), 1))
-    along = along.reshape(EXTENDED, COLS)
+    along = along.reshape(field.shape)
     along += second_along(field, 1, lax.broadcasted_iota(jnp.int32, (1, COLS), 1))
     return field + ATMOS_DIFFUSION * along + MIXING * (above + below - 2.0 * field)
 
@@ -317,43 +405,56 @@
     return assembled(field, 0, row % 4, ahead, pltpu.roll(field, 1, 0))
 
 
-def substeps_body(u_ref, sides_ref, before_ref, after_ref, _, out_ref, main, moved):
+def diffused_levels(levels):
+    return [
+        diffused(levels[l], levels[min(l + 1, LEV - 1)], levels[max(l - 1, 0)]) for l in range(LEV)
+    ]
+
+
+def local_body(u_ref, out_ref):
+    for l, field in enumerate(diffused_levels([u_ref[l] for l in range(LEV)])):
+        out_ref[l] = field
+
+
+def substeps_body(
+    local_ref, sides_ref, before_ref, after_ref, mate_before_ref, mate_after_ref, _, out_ref, main
+):
     row, lane = iotas(EXTENDED)
     phase, part = lane % 4, lane % (2 * WIDE)
-    for l in range(LEV):
-        main[l, :WIDE] = before_ref[l]
-        main[l, WIDE : WIDE + ROWS] = u_ref[l]
-        main[l, WIDE + ROWS :] = after_ref[l]
-    sides = jnp.concatenate([before_ref[LEV], sides_ref[...], after_ref[LEV]], axis=0)
+    edges = [diffused_levels([r[l] for l in range(LEV)]) for r in (before_ref, after_ref)]
+    thin = lax.broadcasted_iota(jnp.int32, (WIDE, COLS), 1)
+    ends = [
+        packed_sides([r[l] for l in range(LEV)], thin) for r in (mate_before_ref, mate_after_ref)
+    ]
+    sides = jnp.concatenate([ends[0], sides_ref[...], ends[1]], axis=0)
     for substep in range(2):
         over = jnp.where(lane < COLS - 2 * WIDE, turned(sides, -2 * WIDE), sides)
         under = jnp.where(lane >= 2 * WIDE, turned(sides, 2 * WIDE), sides)
         sides = assembled_rows(diffused(sides, over, under), row)
-        edges = jnp.zeros((EXTENDED, COLS), F32)
+        near = jnp.zeros((EXTENDED, COLS), F32)
         for l in range(LEV):
-            field = main[l]
-            half = assembled_rows(
-                diffused(field, main[min(l + 1, LEV - 1)], main[max(l - 1, 0)]), row
-            )
+            if substep == 0:
+                half = jnp.concatenate([edges[0][l], local_ref[l], edges[1][l]], axis=0)
+            else:
+                half = diffused(main[l], main[min(l + 1, LEV - 1)], main[max(l - 1, 0)])
+            half = assembled_rows(half, row)
             if substep == 0:
                 first = turned(half, 2 * WIDE * l + WIDE - 1)
                 last = turned(half, 2 * WIDE * l + WIDE + 1)
                 own_level = lane // (2 * WIDE) == l
-                edges = jnp.where(own_level, jnp.where(part < WIDE, first, last), edges)
+                near = jnp.where(own_level, jnp.where(part < WIDE, first, last), near)
             ends = mate_ends(sides, l)
             whole = assembled(
                 half, 1, phase, column_right(half, ends, lane), column_left(half, ends, lane)
             )
             if substep == 0:
-                moved[l] = whole
+                main[l] = whole
             else:
                 out_ref[l] = whole[WIDE : WIDE + ROWS]
         if substep == 0:
-            ahead = jnp.where(part == WIDE - 1, edges, turned(sides, -1))
-            behind = jnp.where(part == WIDE, edges, turned(sides, 1))
+            ahead = jnp.where(part == WIDE - 1, near, turned(sides, -1))
+            behind = jnp.where(part == WIDE, near, turned(sides, 1))
             sides = assembled(sides, 1, phase, ahead, behind)
-            for l in range(LEV):
-                main[l] = moved[l]
 
 
 ORDER = [(dr, dc) for dr in (-1, 0, 1) for dc in (-1, 0, 1) if dr or dc]
@@ -394,24 +495,39 @@
     return total
 
 
-def top_base_body(other_ref, mate_ref, before_ref, after_ref, table_ref, out_ref):
+def top_base_body(other_ref, mate_ref, table_ref, out_ref, weight_ref):
     row, lane = iotas(ROWS)
     top = other_ref[0].astype(F32)
+    counts = neighbour_counts(table_ref, row, lane)
+    none = jnp.zeros((1, COLS), F32)
     spread = neighbour_spread(
-        top,
-        mate_ref[0].astype(F32),
-        before_ref[LEV + 1, WIDE - 1 :, :],
-        after_ref[LEV + 1, :1, :],
-        before_ref[LEV + 2, WIDE - 1 :, :],
-        after_ref[LEV + 2, :1, :],
-        neighbour_counts(table_ref, row, lane),
-        row,
-        lane,
+        top, mate_ref[0].astype(F32), none, none, none, none, counts, row, lane
     )
     out_ref[...] = (1.0 - MIXING) * top + other_ref[1].astype(F32) + OCEAN_DIFFUSION * spread
-
-
-def ocean_base_body(o_ref, sides_ref, before_ref, after_ref, table_ref, out_ref, counts_ref):
+    weight_ref[...] = jnp.zeros_like(weight_ref)
+    for n, (dr, _) in enumerate(ORDER):
+        if dr:
+            edge = 0 if dr < 0 else ROWS - 1
+            weight_ref[n : n + 1, :] = counts[n][edge : edge + 1, :]
+
+
+def edge_terms(line, ends, weights):
+    lane = lax.broadcasted_iota(jnp.int32, (1, COLS), 1)
+    total = weights[0] * column_left(line, ends, lane) + weights[1] * line
+    return OCEAN_DIFFUSION * (total + weights[2] * column_right(line, ends, lane))
+
+
+def ocean_base_body(
+    o_ref,
+    sides_ref,
+    before_ref,
+    after_ref,
+    mate_before_ref,
+    mate_after_ref,
+    table_ref,
+    out_ref,
+    counts_ref,
+):
     row, lane = iotas(ROWS)
     for n, count in enumerate(neighbour_counts(table_ref, row, lane)):
         counts_ref[n] = count
@@ -422,8 +538,8 @@
             mate_ends(sides_ref[...], l),
             before_ref[l, WIDE - 1 :, :],
             after_ref[l, :1, :],
-            mate_ends(before_ref[LEV, WIDE - 1 :, :], l),
-            mate_ends(after_ref[LEV, :1, :], l),
+            mate_before_ref[l, WIDE - 1 :, :],
+            mate_after_ref[l, :1, :],
             [counts_ref[n] for n in range(len(ORDER))],
             row,
             lane,
@@ -450,25 +566,56 @@
 
 
 def row_hits(labels):
-    width = ATMOS_SLOTS
-    shape = (RANKS, width, COLS)
+    blocks, width = labels.shape[0], ATMOS_SLOTS
+    shape = (blocks, width, COLS)
     diagonal = lax.broadcasted_iota(jnp.int32, shape, 1) == lax.broadcasted_iota(jnp.int32, shape, 2)
     spread = jnp.where(diagonal, labels[:, None, :], 0.0)
-    column = jnp.sum(spread, axis=2, keepdims=True).reshape(RANKS * width, 1)
-    slot = lax.broadcasted_iota(jnp.int32, (RANKS, width, 1), 1).reshape(RANKS * width, 1)
+    column = jnp.sum(spread, axis=2, keepdims=True).reshape(blocks * width, 1)
+    slot = lax.broadcasted_iota(jnp.int32, (blocks, width, 1), 1).reshape(blocks * width, 1)
     column = jnp.where(slot < CAP, column, -1.0).astype(jnp.int32)
-    rows = lax.broadcasted_iota(jnp.int32, (RANKS * width, ROWS), 1)
+    rows = lax.broadcasted_iota(jnp.int32, (blocks * width, ROWS), 1)
     return jnp.where(column == rows, 1.0, 0.0).astype(BF16)
 
 
-def top_body(arrived_ref, base_ref, out_ref):
-    arrived = arrived_ref[...].astype(F32)
-    hits = row_hits(arrived[:, CAP, :])
-    values = arrived.reshape(RANKS * ATMOS_SLOTS, COLS).astype(BF16)
-    pushed = lax.dot_general(hits, values, (((0,), (0,)), ((), ())), preferred_element_type=F32)
-    top = (base_ref[...] + pushed).astype(BF16)
-    picked = jnp.dot(hits, top, preferred_element_type=F32)
-    out_ref[...] = picked.astype(BF16).reshape(RANKS, ATMOS_SLOTS, COLS)
+def push_body(
+    core_ref,
+    arrived_ref,
+    base_ref,
+    weight_ref,
+    before_ref,
+    after_ref,
+    mate_before_ref,
+    mate_after_ref,
+    _,
+    out_ref,
+    hits_ref,
+):
+    weights = [weight_ref[n : n + 1, :] for n in range(len(ORDER))]
+    row = lax.broadcasted_iota(jnp.int32, (ROWS, COLS), 0)
+    above = edge_terms(
+        before_ref[LEV, WIDE - 1 :, :], mate_before_ref[LEV, WIDE - 1 :, :], weights[:3]
+    )
+    below = edge_terms(after_ref[LEV, :1, :], mate_after_ref[LEV, :1, :], weights[5:])
+    base = base_ref[...] + jnp.where(row == 0, above, 0.0) + jnp.where(row == ROWS - 1, below, 0.0)
+    blocks = RANKS // CORES
+    arrived = arrived_ref[...].astype(F32).reshape(blocks, CORES, ATMOS_SLOTS, COLS)
+    for core in range(CORES):
+        part = arrived[:, core]
+        hits = row_hits(part[:, CAP, :])
+        hits_ref[core] = hits
+        values = part.reshape(blocks * ATMOS_SLOTS, COLS).astype(BF16)
+        pushed = lax.dot_general(
+            hits, values, (((0,), (0,)), ((), ())), preferred_element_type=F32
+        )
+        out_ref[core] = pushed + jnp.where(core_ref[0] == core, base, 0.0)
+
+
+def pick_body(mine_ref, mate_ref, hits_ref, out_ref):
+    blocks = RANKS // CORES
+    for core in range(CORES):
+        top = (mine_ref[core] + mate_ref[core]).astype(BF16)
+        picked = jnp.dot(hits_ref[core], top, preferred_element_type=F32)
+        out_ref[:, core] = picked.astype(BF16).reshape(blocks, ATMOS_SLOTS, COLS)
 
 
 def sums_body(arrived_ref, base_ref, share_ref, out_ref, first_ref, wide):
@@ -554,7 +701,7 @@
     return pl.pallas_call(
         remap_body,
         out_shape=jax.ShapeDtypeStruct((ROWS, COLS), F32),
-        in_specs=[VMEM, VMEM, ANY],
+        in_specs=[VMEM, VMEM, HBM],
         out_specs=VMEM,
         scratch_shapes=WEIGHTS_HELD
         + [
@@ -566,8 +713,8 @@
     )(pos, arrived, weights)
 
 
-def to_peers(payload):
-    return lax.all_to_all(payload, ("gx", "gy"), split_axis=0, concat_axis=0, tiled=True)
+def to_peers(payload, axes):
+    return lax.all_to_all(payload, axes, split_axis=0, concat_axis=0, tiled=True)
 
 
 def local(
@@ -586,66 +733,87 @@
     plane = jax.ShapeDtypeStruct((ROWS, COLS), F32)
     swap = [(0, 1), (1, 0)]
 
-    cross, sides, pos, labels = first_kernel(
-        lax.axis_index("comp").reshape(1), own, destination_water_peer, destination_water_line
-    )
+    cross = cross_kernel(lax.axis_index("comp").reshape(1), own)
     other = lax.ppermute(cross, "comp", [(0, 1), (1, 0)])
-    sides = from_mate(sides)
 
     def atmosphere_early():
-        packed = atmos_flux(
-            pos,
-            labels,
+        packed, pos = atmos_flux(
+            destination_water_peer,
+            destination_water_line,
             own,
             prior_marine_heat,
             transfer_factor_table,
             interpolation_matrix_blocks,
             depth_fraction_matrix,
         )
-        nothing = jnp.zeros((LEV + 1, WIDE, COLS), F32)
-        return packed, nothing, nothing
+        nothing = jnp.zeros((LEV, WIDE, COLS), F32)
+        return packed, pos, nothing, nothing
 
     def ocean_early():
-        halo = from_neighbours(*edge_rows(own, sides))
-        return jnp.zeros((RANKS, ATMOS_SLOTS, COLS), BF16), *halo
-
-    packed, *ocean_rows = lax.cond(is_atmosphere_side, atmosphere_early, ocean_early)
+        before, after = from_neighbours(*edge_rows(own))
+        packed = unused((RANKS, ATMOS_SLOTS, COLS), BF16)
+        return packed, jnp.zeros((2 * K, ROWS), jnp.int32), before, after
+
+    packed, pos, *ocean_rows = lax.cond(is_atmosphere_side, atmosphere_early, ocean_early)
 
     def atmosphere():
-        mate = from_mate(other)
-        edges = edge_rows(own, sides, other[0], mate[0])
-        payload, *edges = lax.optimization_barrier((packed, *edges))
-        before, after = from_neighbours(*edges)
-        arrived = to_peers(payload)
-        base = shadow_call(top_base_body, plane, [VMEM] * 5)(
-            other, mate, before, after, adjacent_cell_table
+        by_chip = (RANKS // CORES, CORES * ATMOS_SLOTS, COLS)
+        payload, *edges = lax.optimization_barrier((packed, *edge_rows(own, other[:1])))
+        rows = from_neighbours(*edges)
+        arrived = to_peers(payload.reshape(by_chip), "gx")
+        sides = from_mate(shadow_call(sides_body, plane, [VMEM])(own))
+        moved = shadow_call(local_body, block, [VMEM], us=3)(own)
+        base, weights = shadow_call(
+            top_base_body, (plane, jax.ShapeDtypeStruct((len(ORDER), COLS), F32)), [VMEM] * 3, us=2
+        )(other, from_mate(other), adjacent_cell_table)
+        *rows, moved, base = lax.optimization_barrier((*rows, moved, base))
+        rows = [*rows, *map(from_mate, rows)]
+        mine, hits = call(
+            push_body,
+            (
+                jax.ShapeDtypeStruct((CORES, ROWS, COLS), F32),
+                jax.ShapeDtypeStruct((CORES, RANKS // CORES * ATMOS_SLOTS, ROWS), BF16),
+            ),
+            [SMEM] + [VMEM] * 7 + [ANY],
+        )(
+            lax.axis_index("gy").reshape(1),
+            arrived.reshape(RANKS, ATMOS_SLOTS, COLS),
+            base,
+            weights,
+            *rows,
+            moved,
         )
         picked = call(
-            top_body, jax.ShapeDtypeStruct((RANKS, ATMOS_SLOTS, COLS), BF16), [VMEM, VMEM]
-        )(arrived, base)
-        returned = to_peers(picked)
+            pick_body,
+            jax.ShapeDtypeStruct((RANKS // CORES, CORES, ATMOS_SLOTS, COLS), BF16),
+            [VMEM] * 3,
+        )(mine, from_mate(mine), hits)
+        returned = to_peers(picked.reshape(by_chip), "gx")
         wide = pltpu.VMEM((LEV, EXTENDED, COLS), F32)
         final = shadow_call(
-            substeps_body, block, [VMEM] * 4 + [ANY], scratch_shapes=[wide, wide]
-        )(own, sides, before, after, picked)
-        return final, remap(pos, returned, interpolation_matrix_blocks)
+            substeps_body, block, [VMEM] * 6 + [ANY], scratch_shapes=[wide]
+        )(moved, sides, *rows, picked)
+        return final, remap(
+            pos, returned.reshape(RANKS, ATMOS_SLOTS, COLS), interpolation_matrix_blocks
+        )
 
     def ocean():
         payload = ocean_flux(
-            pos,
-            labels,
+            destination_water_peer,
+            destination_water_line,
             other,
             prior_marine_heat,
             transfer_factor_table,
             interpolation_matrix_blocks,
         )
-        arrived = to_peers(payload.reshape(RANKS, OCEAN_SLOTS * NF, COLS))
+        arrived = to_peers(payload.reshape(RANKS, OCEAN_SLOTS * NF, COLS), ("gx", "gy"))
+        sides = from_mate(shadow_call(sides_body, plane, [VMEM])(own))
         base = shadow_call(
             ocean_base_body,
             block,
-            [VMEM] * 5,
+            [VMEM] * 7,
             scratch_shapes=[pltpu.VMEM((len(ORDER), ROWS, COLS), F32)],
-        )(own, sides, *ocean_rows, adjacent_cell_table)
+        )(own, sides, *ocean_rows, *map(from_mate, ocean_rows), adjacent_cell_table)
         return ocean_sums(
             arrived.reshape(RANKS * OCEAN_SLOTS, NF, COLS), base, depth_fraction_matrix
         )

time: 69.2 us -> 66.4 us (0.960)
  waiting for transfers between devices: 30.3 us -> 28.1 us
  local copies, waits for them, and re-layouts: 2.21 us -> 0.81 us
  starting transfers between devices: 16.3 us -> 17.5 us
    all_to_all x1, waiting for transfers between devices: 28.1 us -> 25.8 us  [to_peers(): lax.all_to_all(payload, axes, split_axis=0, concat_axis=0, tiled=True)]
    unnamed x4 -> x0, local copies, waits for them, and re-layouts: 1.36 us -> none
    all_to_all x1, starting transfers between devices: 9.4 us -> 10.1 us  [to_peers(): lax.all_to_all(payload, axes, split_axis=0, concat_axis=0, tiled=True)]
    pallas_call x2 -> x4, Pallas kernels: 6.66 us -> 6.22 us  [the longest x1 4.9 us: ocean(): shadow_call(ocean_base_body, block, [VMEM] * 7, scratch_shapes=[pltpu.VME...]
  transfers between devices with their start and end apart: 5 -> 7, of which waited for: 3 -> 4; matrix products, arithmetic and copies ran while one was open for 1% -> 1% of each run, Pallas kernels for 7% -> 8%
where the time goes in v5:
time: 66.4 us; the launch traced here: 65.9 us
  waiting for transfers between devices  28.1 us (42%)
  Pallas kernels  18.7 us (28%)
  starting transfers between devices  17.5 us (26%)
  local copies, waits for them, and re-layouts  0.81 us (1%)
    all_to_all x1, waiting for transfers between devices, to_peers(): lax.all_to_all(payload, axes, split_axis=0, concat_axis=0, tiled=True)  25.8 us
    all_to_all x1, starting transfers between devices, to_peers(): lax.all_to_all(payload, axes, split_axis=0, concat_axis=0, tiled=True)  10.1 us
    pallas_call x1, Pallas kernels, ocean_flux(): pl.pallas_call(ocean_flux_body, out_shape=pltpu.HBM((RANKS * OCEAN_SLOTS,...  9.02 us
    ppermute x2, starting transfers between devices, from_neighbours(): return (lax.ppermute(last, 'gx', up), lax.ppermute(first, 'gx', down))  6.3 us
    pallas_call x1, Pallas kernels, ocean(): shadow_call(ocean_base_body, block, [VMEM] * 7, scratch_shapes=[pltpu.VME...  4.9 us
    pallas_call x1, Pallas kernels, ocean_sums(): pl.pallas_call(sums_body, out_shape=(jax.ShapeDtypeStruct((LEV, ROWS, COL...  3.42 us
  transfers between devices with their start and end apart: 7, of which 4 were waited for; matrix products, arithmetic and copies ran while one was open for 1% of the time, Pallas kernels for 8%

profile of v5, /device:TPU:65, one launch (start us, length us, event | category | flops | bytes accessed | tf_op | source)
XLA Modules:
  0.0 65.9 jit_solution(7256515349564622663)
XLA Ops:
  0.6 1.0 %shard_map.95 = bf16[2,256,128]{2,1,0:T(8,128)(2,1)S(1)} custom-call(s32[1]{0:T(128)} %bitcast.15.side_ref, f32[8,256,128]{2,1,0:T(8,128)} %bitcast.20), custom_call_target="tpu_custom_call" | custom-call | tf_op jit(solution)/shard_map/pallas_call | solution.py:124
  1.6 0.1 collective-permute-start.12
  1.7 8.3 %conditional.2 = (bf16[64,24,128]{2,1,0:T(8,128)(2,1)}, s32[4,256]{1,0:T(4,128)S(1)}, f32[8,8,128]{2,1,0:T(8,128)S(1)}, f32[8,8,128]{2,1,0:T(8,128)S(1)}) conditional(s32[]{:T(128)} %convert_element_type.10, f32[8,256,128]{2,1,0:T(8,128)} %bitcast.21, (s32[256,2]{0,1:T(2,128)}, s32[256,2]{0,1:T(2,128)}, f32[8,256,128]{2,1,0:T(8,128)}, ...), branch_computations={%region_0.0_spmd, %region_1.0_spmd} | conditional | bytes 397428 | solution.py:757
  1.7 0.8 %fusion = (f32[8,8,128]{2,1,0:T(8,128)S(1)}, f32[8,8,128]{2,1,0:T(8,128)S(1)}) fusion(f32[8,256,128]{2,1,0:T(8,128)} %param), kind=kLoop, calls=%fused_computation.4 | loop fusion | bytes 131072 | tf_op jit(solution)/shard_map/cond/branch_0_fun/slice | solution.py:553
  2.5 1.6 %collective-permute-start.3 = (f32[8,8,128]{2,1,0:T(8,128)S(1)}, f32[8,8,128]{2,1,0:T(8,128)S(1)}, u32[]{:S(2)}, u32[]{:S(2)}) collective-permute-start(f32[8,8,128]{2,1,0:T(8,128)S(1)} %get-tuple-element.109), channel_id=1, source_target_pairs={{0,2},{2,4},{4,6},{6,8},{8,10},{10,12},{12,14},{14,16},{16,18},{18... | collective-permute-start | bytes 98312 | tf_op jit(solution)/shard_map/cond/branch_0_fun/ppermute | solution.py:561
  4.1 4.7 %collective-permute-start.4 = (f32[8,8,128]{2,1,0:T(8,128)S(1)}, f32[8,8,128]{2,1,0:T(8,128)S(1)}, u32[]{:S(2)}, u32[]{:S(2)}) collective-permute-start(f32[8,8,128]{2,1,0:T(8,128)S(1)} %get-tuple-element.108), channel_id=1, source_target_pairs={{2,0},{4,2},{6,4},{8,6},{10,8},{12,10},{14,12},{16,14},{18,16},{20... | collective-permute-start | bytes 98312 | tf_op jit(solution)/shard_map/cond/branch_0_fun/ppermute | solution.py:561
  8.8 1.2 %collective-permute-done.3 = f32[8,8,128]{2,1,0:T(8,128)S(1)} collective-permute-done((f32[8,8,128]{2,1,0:T(8,128)S(1)}, f32[8,8,128]{2,1,0:T(8,128)S(1)}, u32[]{:S(2)}, u32[]{:S(2)}) %collective-permute-start.3) | collective-permute-done | bytes 32800 | tf_op jit(solution)/shard_map/cond/branch_0_fun/ppermute | solution.py:561
  10.1 0.0 collective-permute-done.4
  10.1 55.8 %conditional.3 = (f32[1,8,256,128]{3,2,1,0:T(8,128)}, f32[1,256,128]{2,1,0:T(8,128)}) conditional(s32[]{:T(128)} %convert_element_type.10, (s32[256,2]{0,1:T(2,128)}, s32[256,2]{0,1:T(2,128)}, bf16[2,256,128]{2,1,0:T(8,128)(2,1)}, f32[256,128]{1,0:T(8,128)}, f32[8,256,128]{2,1,0:T(8,128)}, /*index=5*/bf16[256,2,128,128]{3,2,1,0:T(8,128)(2,1)}, ...), branch_computations={%region_2.0_spmd, %region_3.0_spmd} | conditional | flops 20482 | bytes 31127556 | solution.py:821
  10.1 0.0 copy-start.3
  10.1 0.0 copy-start.4
  10.1 9.0 %branch_0_fun.6 = bf16[1216,8,128]{2,1,0:T(8,128)(2,1)} custom-call(s32[2,256]{1,0:T(2,128)} %bitcast.28, s32[2,256]{1,0:T(2,128)} %bitcast.30, bf16[2,256,128]{2,1,0:T(8,128)(2,1)} %get-tuple-element.64.air_ref, f32[256,128]{1,0:T(8,128)} %get-tuple-element.65.prior_ref, f32[8,256,128]{2,1,0:T(8,128)} %get-tuple-element.66.factor_ref, ...), custom_call_target="tpu_custom_call" | custom-call | tf_op jit(solution)/shard_map/cond/branch_0_fun/pallas_call | solution.py:242
  19.2 0.0 copy-start
  19.2 10.1 %all-to-all-start = ((bf16[64,152,128]{2,1,0:T(8,128)(2,1)}), bf16[64,152,128]{2,1,0:T(8,128)(2,1)S(1)}, u32[]{:S(2)}, u32[]{:S(2)}) async-start(bf16[64,152,128]{2,1,0:T(8,128)(2,1)} %bitcast.25), calls=%async_computation | async-start | bytes 4980736 | tf_op jit(solution)/shard_map/cond/branch_0_fun/all_to_all | solution.py:717
  29.3 0.0 copy-start.5
  29.3 0.3 branch_0_fun.7
  29.6 0.5 collective-permute-start
  30.2 0.1 collective-permute-start.1
  30.3 0.4 collective-permute-start.2
  30.7 0.9 %collective-permute-done.1.mate_before_ref = f32[8,8,128]{2,1,0:T(8,128)S(1)} collective-permute-done((f32[8,8,128]{2,1,0:T(8,128)}, f32[8,8,128]{2,1,0:T(8,128)S(1)}, u32[]{:S(2)}, u32[]{:S(2)}) %collective-permute-start.1) | collective-permute-done | bytes 32800 | tf_op jit(solution)/shard_map/cond/branch_0_fun/ppermute | solution.py:565
  31.6 0.2 collective-permute-done.2.mate_after_ref
  31.8 4.9 %branch_0_fun.8.base_ref = f32[8,256,128]{2,1,0:T(8,128)S(1)} custom-call(f32[8,256,128]{2,1,0:T(8,128)} %get-tuple-element.68.own_ref.o_ref, f32[256,128]{1,0:T(8,128)S(1)} %collective-permute-done.sides_ref, f32[8,8,128]{2,1,0:T(8,128)} %copy-done.3, f32[8,8,128]{2,1,0:T(8,128)} %copy-done.4, f32[8,8,128]{2,1,0:T(8,128)S(1)} %collective-permute-done.1.mate_before_ref, ...), custom_call_target="tpu_custom_call" | custom-call | tf_op jit(solution)/shard_map/cond/branch_0_fun/pallas_call | solution.py:811
  36.7 25.8 %all-to-all-done = bf16[64,152,128]{2,1,0:T(8,128)(2,1)S(1)} async-done(((bf16[64,152,128]{2,1,0:T(8,128)(2,1)}), bf16[64,152,128]{2,1,0:T(8,128)(2,1)S(1)}, u32[]{:S(2)}, u32[]{:S(2)}) %all-to-all-start) | async-done | bytes 2490400 | tf_op jit(solution)/shard_map/cond/branch_0_fun/all_to_all | solution.py:717
  62.4 3.4 %branch_0_fun.9 = (f32[8,256,128]{2,1,0:T(8,128)}, f32[256,128]{1,0:T(8,128)}) custom-call(bf16[1216,8,128]{2,1,0:T(8,128)(2,1)S(1)} %bitcast.17, f32[8,256,128]{2,1,0:T(8,128)S(1)} %branch_0_fun.8.base_ref, f32[8,8]{1,0:T(8,128)S(1)} %copy-done.5), custom_call_target="tpu_custom_call" | custom-call | tf_op jit(solution)/shard_map/cond/branch_0_fun/pallas_call | solution.py:653
  (8 shorter events, 0.0 us)
Async XLA Ops:
  1.6 8.4 %collective-permute-start.12 = (bf16[2,256,128]{2,1,0:T(8,128)(2,1)S(1)}, bf16[2,256,128]{2,1,0:T(8,128)(2,1)}, u32[]{:S(2)}, u32[]{:S(2)}) collective-permute-start(bf16[2,256,128]{2,1,0:T(8,128)(2,1)S(1)} %shard_map.95), channel_id=1, source_target_pairs={{0,64},{64,0},{1,65},{65,1},{2,66},{66,2},{3,67},{67,3},{4,68},{68... | collective-permute-start | bytes 393224 | tf_op jit(solution)/shard_map/ppermute | solution.py:737
  2.5 7.5 %collective-permute-start.3 = (f32[8,8,128]{2,1,0:T(8,128)S(1)}, f32[8,8,128]{2,1,0:T(8,128)S(1)}, u32[]{:S(2)}, u32[]{:S(2)}) collective-permute-start(f32[8,8,128]{2,1,0:T(8,128)S(1)} %get-tuple-element.109), channel_id=1, source_target_pairs={{0,2},{2,4},{4,6},{6,8},{8,10},{10,12},{12,14},{14,16},{16,18},{18... | collective-permute-start | bytes 98312 | tf_op jit(solution)/shard_map/cond/branch_0_fun/ppermute | solution.py:561
  4.1 6.0 %collective-permute-start.4 = (f32[8,8,128]{2,1,0:T(8,128)S(1)}, f32[8,8,128]{2,1,0:T(8,128)S(1)}, u32[]{:S(2)}, u32[]{:S(2)}) collective-permute-start(f32[8,8,128]{2,1,0:T(8,128)S(1)} %get-tuple-element.108), channel_id=1, source_target_pairs={{2,0},{4,2},{6,4},{8,6},{10,8},{12,10},{14,12},{16,14},{18,16},{20... | collective-permute-start | bytes 98312 | tf_op jit(solution)/shard_map/cond/branch_0_fun/ppermute | solution.py:561
  10.1 9.1 %copy-start.3 = (f32[8,8,128]{2,1,0:T(8,128)}, f32[8,8,128]{2,1,0:T(8,128)S(1)}, u32[]{:S(2)}) copy-start(f32[8,8,128]{2,1,0:T(8,128)S(1)} %get-tuple-element.69.before_ref) | copy-start | bytes 98308 | tf_op jit(solution)/shard_map/cond
  10.1 9.1 %copy-start.4 = (f32[8,8,128]{2,1,0:T(8,128)}, f32[8,8,128]{2,1,0:T(8,128)S(1)}, u32[]{:S(2)}) copy-start(f32[8,8,128]{2,1,0:T(8,128)S(1)} %get-tuple-element.70.after_ref) | copy-start | bytes 98308 | tf_op jit(solution)/shard_map/cond
  19.2 10.1 %copy-start = (f32[8,256,128]{2,1,0:T(8,128)S(1)}, f32[8,256,128]{2,1,0:T(8,128)}, u32[]{:S(2)}) copy-start(f32[8,256,128]{2,1,0:T(8,128)} %get-tuple-element.68.own_ref.o_ref) | copy-start | bytes 3145732 | tf_op jit(solution)/shard_map/cond
  19.2 43.3 %all-to-all-start = ((bf16[64,152,128]{2,1,0:T(8,128)(2,1)}), bf16[64,152,128]{2,1,0:T(8,128)(2,1)S(1)}, u32[]{:S(2)}, u32[]{:S(2)}) async-start(bf16[64,152,128]{2,1,0:T(8,128)(2,1)} %bitcast.25), calls=%async_computation | async-start | bytes 4980736 | tf_op jit(solution)/shard_map/cond/branch_0_fun/all_to_all | solution.py:717
  29.3 33.2 %copy-start.5 = (f32[8,8]{1,0:T(8,128)S(1)}, f32[8,8]{1,0:T(8,128)}, u32[]{:S(2)}) copy-start(f32[8,8]{1,0:T(8,128)} %get-tuple-element.72.share_ref) | copy-start | bytes 772 | tf_op jit(solution)/shard_map/cond
  29.6 2.1 %collective-permute-start = (f32[256,128]{1,0:T(8,128)S(1)}, f32[256,128]{1,0:T(8,128)S(1)}, u32[]{:S(2)}, u32[]{:S(2)}) collective-permute-start(f32[256,128]{1,0:T(8,128)S(1)} %branch_0_fun.7), channel_id=1, source_target_pairs={{0,1},{1,0},{2,3},{3,2},{4,5},{5,4},{6,7},{7,6},{8,9},{9,8},{10,11... | collective-permute-start | bytes 393224 | tf_op jit(solution)/shard_map/cond/branch_0_fun/ppermute | solution.py:565
  30.2 1.4 %collective-permute-start.1 = (f32[8,8,128]{2,1,0:T(8,128)}, f32[8,8,128]{2,1,0:T(8,128)S(1)}, u32[]{:S(2)}, u32[]{:S(2)}) collective-permute-start(f32[8,8,128]{2,1,0:T(8,128)} %copy-done.3), channel_id=1, source_target_pairs={{0,1},{1,0},{2,3},{3,2},{4,5},{5,4},{6,7},{7,6},{8,9},{9,8},{10,11... | collective-permute-start | bytes 98312 | tf_op jit(solution)/shard_map/cond/branch_0_fun/ppermute | solution.py:565
  30.3 1.5 %collective-permute-start.2 = (f32[8,8,128]{2,1,0:T(8,128)}, f32[8,8,128]{2,1,0:T(8,128)S(1)}, u32[]{:S(2)}, u32[]{:S(2)}) collective-permute-start(f32[8,8,128]{2,1,0:T(8,128)} %copy-done.4), channel_id=1, source_target_pairs={{0,1},{1,0},{2,3},{3,2},{4,5},{5,4},{6,7},{7,6},{8,9},{9,8},{10,11... | collective-permute-start | bytes 98312 | tf_op jit(solution)/shard_map/cond/branch_0_fun/ppermute | solution.py:565

commit v6 on v5

--- a/solution.py
+++ b/solution.py
@@ -108,24 +108,39 @@
     return field if lanes == 0 else pltpu.roll(field, lanes, 1)
 
 
-def cross_body(side_ref, own_ref, out_ref, held, sem):
-    copy = pltpu.make_async_copy(own_ref.at[pl.ds(0, 2)], held, sem)
-    copy.start()
-    copy.wait()
+def cross_body(side_ref, own_ref, out_ref, last_ref, first_ref, held, edges, sems):
+    copies = [
+        pltpu.make_async_copy(own_ref.at[pl.ds(0, 2)], held, sems.at[0]),
+        pltpu.make_async_copy(own_ref.at[:, pl.ds(ROWS - WIDE, WIDE)], edges.at[0], sems.at[1]),
+        pltpu.make_async_copy(own_ref.at[:, pl.ds(0, WIDE)], edges.at[1], sems.at[2]),
+    ]
+    for copy in copies:
+        copy.start()
+    copies[0].wait()
     top = held[0]
     high = top.astype(BF16)
     rest = top - high.astype(F32)
     out_ref[0] = high
     other = MIXING * held[1] + (1.0 - MIXING) * rest
     out_ref[1] = jnp.where(side_ref[0] == 0, rest, other).astype(BF16)
+    for copy in copies[1:]:
+        copy.wait()
+    for l in range(LEV):
+        last_ref[l : l + 1, :] = edges[0, l, WIDE - 1 :, :]
+        first_ref[l : l + 1, :] = edges[1, l, :1, :]
 
 
 def cross_kernel(side, own):
+    edge = jax.ShapeDtypeStruct((LEV, COLS), F32)
     return call(
         cross_body,
-        jax.ShapeDtypeStruct((2, ROWS, COLS), BF16),
+        (jax.ShapeDtypeStruct((2, ROWS, COLS), BF16), edge, edge),
         [SMEM, HBM],
-        scratch_shapes=[pltpu.VMEM((2, ROWS, COLS), F32), pltpu.SemaphoreType.DMA],
+        scratch_shapes=[
+            pltpu.VMEM((2, ROWS, COLS), F32),
+            pltpu.VMEM((2, LEV, WIDE, COLS), F32),
+            pltpu.SemaphoreType.DMA((3,)),
+        ],
     )(side, own)
 
 
@@ -176,7 +191,7 @@
 def ocean_flux_body(
     peer_ref,
     line_ref,
-    air_ref,
+    air_hbm_ref,
     prior_ref,
     factor_ref,
     w_ref,
@@ -188,6 +203,7 @@
     pos,
     prior,
     factor,
+    air_ref,
     pos_rows,
     packed,
     rows,
@@ -200,6 +216,7 @@
     ]
     field_copies = [
         pltpu.make_async_copy(prior_ref, prior, sems.at[CHUNKS + 2]),
+        pltpu.make_async_copy(air_hbm_ref, air_ref, sems.at[CHUNKS + 6]),
         pltpu.make_async_copy(factor_ref, factor, sems.at[CHUNKS + 3]),
     ]
     for started in index_copies + field_copies:
@@ -242,16 +259,17 @@
     return pl.pallas_call(
         ocean_flux_body,
         out_shape=pltpu.HBM((RANKS * OCEAN_SLOTS, NF, COLS), BF16),
-        in_specs=[HBM, HBM, VMEM, HBM, HBM, HBM],
+        in_specs=[HBM, HBM, ANY, HBM, HBM, HBM],
         out_specs=HBM,
         scratch_shapes=WEIGHTS_HELD
         + ROUTING
         + FIELDS
         + [
+            pltpu.VMEM((2, ROWS, COLS), BF16),
             pltpu.VMEM((2 * K, ROWS), jnp.int32),
             pltpu.VMEM((RANKS * OCEAN_SLOTS, NF, COLS), BF16),
             pltpu.VMEM((ROWS * NF, COLS), F32),
-            pltpu.SemaphoreType.DMA((CHUNKS + 6,)),
+            pltpu.SemaphoreType.DMA((CHUNKS + 7,)),
         ],
         compiler_params=pltpu.CompilerParams(vmem_limit_bytes=32 << 20),
     )(peer.T, line.T, air, prior, factors, weights)
@@ -495,6 +513,14 @@
     return total
 
 
+def edge_weights(counts, weight_ref):
+    weight_ref[...] = jnp.zeros_like(weight_ref)
+    for n, (dr, _) in enumerate(ORDER):
+        if dr:
+            edge = 0 if dr < 0 else ROWS - 1
+            weight_ref[n : n + 1, :] = counts[n][edge : edge + 1, :]
+
+
 def top_base_body(other_ref, mate_ref, table_ref, out_ref, weight_ref):
     row, lane = iotas(ROWS)
     top = other_ref[0].astype(F32)
@@ -504,17 +530,18 @@
         top, mate_ref[0].astype(F32), none, none, none, none, counts, row, lane
     )
     out_ref[...] = (1.0 - MIXING) * top + other_ref[1].astype(F32) + OCEAN_DIFFUSION * spread
-    weight_ref[...] = jnp.zeros_like(weight_ref)
-    for n, (dr, _) in enumerate(ORDER):
-        if dr:
-            edge = 0 if dr < 0 else ROWS - 1
-            weight_ref[n : n + 1, :] = counts[n][edge : edge + 1, :]
+    edge_weights(counts, weight_ref)
 
 
 def edge_terms(line, ends, weights):
     lane = lax.broadcasted_iota(jnp.int32, (1, COLS), 1)
     total = weights[0] * column_left(line, ends, lane) + weights[1] * line
     return OCEAN_DIFFUSION * (total + weights[2] * column_right(line, ends, lane))
+
+
+def both_edges(before, before_ends, after, after_ends, weight_ref):
+    weights = [weight_ref[n : n + 1, :] for n in range(len(ORDER))]
+    return edge_terms(before, before_ends, weights[:3]), edge_terms(after, after_ends, weights[5:])
 
 
 def ocean_base_body(
@@ -536,10 +563,10 @@
         spread = neighbour_spread(
             field,
             mate_ends(sides_ref[...], l),
-            before_ref[l, WIDE - 1 :, :],
-            after_ref[l, :1, :],
-            mate_before_ref[l, WIDE - 1 :, :],
-            mate_after_ref[l, :1, :],
+            before_ref[l : l + 1, :],
+            after_ref[l : l + 1, :],
+            mate_before_ref[l : l + 1, :],
+            mate_after_ref[l : l + 1, :],
             [counts_ref[n] for n in range(len(ORDER))],
             row,
             lane,
@@ -577,26 +604,7 @@
     return jnp.where(column == rows, 1.0, 0.0).astype(BF16)
 
 
-def push_body(
-    core_ref,
-    arrived_ref,
-    base_ref,
-    weight_ref,
-    before_ref,
-    after_ref,
-    mate_before_ref,
-    mate_after_ref,
-    _,
-    out_ref,
-    hits_ref,
-):
-    weights = [weight_ref[n : n + 1, :] for n in range(len(ORDER))]
-    row = lax.broadcasted_iota(jnp.int32, (ROWS, COLS), 0)
-    above = edge_terms(
-        before_ref[LEV, WIDE - 1 :, :], mate_before_ref[LEV, WIDE - 1 :, :], weights[:3]
-    )
-    below = edge_terms(after_ref[LEV, :1, :], mate_after_ref[LEV, :1, :], weights[5:])
-    base = base_ref[...] + jnp.where(row == 0, above, 0.0) + jnp.where(row == ROWS - 1, below, 0.0)
+def push_body(core_ref, arrived_ref, base_ref, out_ref, hits_ref):
     blocks = RANKS // CORES
     arrived = arrived_ref[...].astype(F32).reshape(blocks, CORES, ATMOS_SLOTS, COLS)
     for core in range(CORES):
@@ -607,14 +615,33 @@
         pushed = lax.dot_general(
             hits, values, (((0,), (0,)), ((), ())), preferred_element_type=F32
         )
-        out_ref[core] = pushed + jnp.where(core_ref[0] == core, base, 0.0)
-
-
-def pick_body(mine_ref, mate_ref, hits_ref, out_ref):
+        out_ref[core] = pushed + jnp.where(core_ref[0] == core, base_ref[...], 0.0)
+
+
+def pick_body(
+    core_ref,
+    mine_ref,
+    mate_ref,
+    weight_ref,
+    mate_weight_ref,
+    before_ref,
+    after_ref,
+    mate_before_ref,
+    mate_after_ref,
+    hits_ref,
+    out_ref,
+):
     blocks = RANKS // CORES
+    row = lax.broadcasted_iota(jnp.int32, (ROWS, COLS), 0)
+    own_rows = [before_ref[LEV, WIDE - 1 :, :], after_ref[LEV, :1, :]]
+    mate_rows = [mate_before_ref[LEV, WIDE - 1 :, :], mate_after_ref[LEV, :1, :]]
+    own = both_edges(own_rows[0], mate_rows[0], own_rows[1], mate_rows[1], weight_ref)
+    mate = both_edges(mate_rows[0], own_rows[0], mate_rows[1], own_rows[1], mate_weight_ref)
     for core in range(CORES):
-        top = (mine_ref[core] + mate_ref[core]).astype(BF16)
-        picked = jnp.dot(hits_ref[core], top, preferred_element_type=F32)
+        above, below = (jnp.where(core_ref[0] == core, o, m) for o, m in zip(own, mate))
+        top = mine_ref[core] + mate_ref[core]
+        top += jnp.where(row == 0, above, 0.0) + jnp.where(row == ROWS - 1, below, 0.0)
+        picked = jnp.dot(hits_ref[core], top.astype(BF16), preferred_element_type=F32)
         out_ref[:, core] = picked.astype(BF16).reshape(blocks, ATMOS_SLOTS, COLS)
 
 
@@ -663,7 +690,9 @@
     )(arrived, base, share)
 
 
-def remap_body(pos_ref, arrived_ref, w_ref, out_ref, held, values, own, sems):
+def remap_body(pos_hbm_ref, arrived_ref, w_ref, out_ref, held, pos_ref, values, own, sems):
+    pos_copy = pltpu.make_async_copy(pos_hbm_ref, pos_ref, sems.at[ROWS // REMAP_ROWS])
+    pos_copy.start()
     copy = weight_copies(w_ref, held, sems, REMAP_ROWS)
     for c in range(ROWS // REMAP_ROWS):
         copy(c).start()
@@ -671,6 +700,7 @@
     by_column = arrived_ref[...].astype(F32).reshape(slots, COLS).T.astype(BF16)
     at = lax.broadcasted_iota(jnp.int32, (slots, ROWS), 0)
     groups = ROWS // COLS
+    pos_copy.wait()
     for k in range(K):
         hits = jnp.where(at == pos_ref[K + k : K + k + 1, :], 1.0, 0.0).astype(BF16)
         found = jnp.dot(by_column, hits, preferred_element_type=F32).astype(BF16)
@@ -701,13 +731,14 @@
     return pl.pallas_call(
         remap_body,
         out_shape=jax.ShapeDtypeStruct((ROWS, COLS), F32),
-        in_specs=[VMEM, VMEM, HBM],
+        in_specs=[ANY, VMEM, HBM],
         out_specs=VMEM,
         scratch_shapes=WEIGHTS_HELD
         + [
+            pltpu.VMEM((2 * K, ROWS), jnp.int32),
             pltpu.VMEM((ROWS // COLS, K * COLS, COLS), BF16),
             pltpu.VMEM((ROWS // COLS, COLS, COLS), F32),
-            pltpu.SemaphoreType.DMA((ROWS // REMAP_ROWS,)),
+            pltpu.SemaphoreType.DMA((ROWS // REMAP_ROWS + 1,)),
         ],
         compiler_params=pltpu.CompilerParams(vmem_limit_bytes=32 << 20),
     )(pos, arrived, weights)
@@ -733,7 +764,7 @@
     plane = jax.ShapeDtypeStruct((ROWS, COLS), F32)
     swap = [(0, 1), (1, 0)]
 
-    cross = cross_kernel(lax.axis_index("comp").reshape(1), own)
+    cross, last, first = cross_kernel(lax.axis_index("comp").reshape(1), own)
     other = lax.ppermute(cross, "comp", [(0, 1), (1, 0)])
 
     def atmosphere_early():
@@ -746,48 +777,42 @@
             interpolation_matrix_blocks,
             depth_fraction_matrix,
         )
-        nothing = jnp.zeros((LEV, WIDE, COLS), F32)
-        return packed, pos, nothing, nothing
+        return packed, pos, unused((LEV, COLS), F32), unused((1, LEV, COLS), F32)
 
     def ocean_early():
-        before, after = from_neighbours(*edge_rows(own))
+        before, after = from_neighbours(last, first)
         packed = unused((RANKS, ATMOS_SLOTS, COLS), BF16)
-        return packed, jnp.zeros((2 * K, ROWS), jnp.int32), before, after
-
-    packed, pos, *ocean_rows = lax.cond(is_atmosphere_side, atmosphere_early, ocean_early)
+        return packed, unused((2 * K, ROWS), jnp.int32), before, after[None]
+
+    packed, pos, before, after = lax.cond(is_atmosphere_side, atmosphere_early, ocean_early)
+    ocean_rows = (before, after[0])
+    edge_shape = jax.ShapeDtypeStruct((len(ORDER), COLS), F32)
 
     def atmosphere():
         by_chip = (RANKS // CORES, CORES * ATMOS_SLOTS, COLS)
-        payload, *edges = lax.optimization_barrier((packed, *edge_rows(own, other[:1])))
-        rows = from_neighbours(*edges)
-        arrived = to_peers(payload.reshape(by_chip), "gx")
+        rows = from_neighbours(*edge_rows(own, other[:1]))
+        arrived = to_peers(packed.reshape(by_chip), "gx")
         sides = from_mate(shadow_call(sides_body, plane, [VMEM])(own))
         moved = shadow_call(local_body, block, [VMEM], us=3)(own)
-        base, weights = shadow_call(
-            top_base_body, (plane, jax.ShapeDtypeStruct((len(ORDER), COLS), F32)), [VMEM] * 3, us=2
-        )(other, from_mate(other), adjacent_cell_table)
+        base, weights = shadow_call(top_base_body, (plane, edge_shape), [VMEM] * 3, us=2)(
+            other, from_mate(other), adjacent_cell_table
+        )
         *rows, moved, base = lax.optimization_barrier((*rows, moved, base))
         rows = [*rows, *map(from_mate, rows)]
+        core = lax.axis_index("gy").reshape(1)
         mine, hits = call(
             push_body,
             (
                 jax.ShapeDtypeStruct((CORES, ROWS, COLS), F32),
                 jax.ShapeDtypeStruct((CORES, RANKS // CORES * ATMOS_SLOTS, ROWS), BF16),
             ),
-            [SMEM] + [VMEM] * 7 + [ANY],
-        )(
-            lax.axis_index("gy").reshape(1),
-            arrived.reshape(RANKS, ATMOS_SLOTS, COLS),
-            base,
-            weights,
-            *rows,
-            moved,
-        )
+            [SMEM, VMEM, VMEM],
+        )(core, arrived.reshape(RANKS, ATMOS_SLOTS, COLS), base)
         picked = call(
             pick_body,
             jax.ShapeDtypeStruct((RANKS // CORES, CORES, ATMOS_SLOTS, COLS), BF16),
-            [VMEM] * 3,
-        )(mine, from_mate(mine), hits)
+            [SMEM] + [VMEM] * 9,
+        )(core, mine, from_mate(mine), weights, from_mate(weights), *rows, hits)
         returned = to_peers(picked.reshape(by_chip), "gx")
         wide = pltpu.VMEM((LEV, EXTENDED, COLS), F32)
         final = shadow_call(

time: 66.4 us -> 64.5 us (0.971)
  the two profiles are of different devices: /device:TPU:65 before, /device:TPU:1 now
where the time goes in v6:
time: 64.5 us; the launch traced here: 63.5 us
  Pallas kernels  31.9 us (49%)
  starting transfers between devices  25.6 us (40%)
  waiting for transfers between devices  3.27 us (5%)
  between operations  0.86 us (1%)
  local copies, waits for them, and re-layouts  0.79 us (1%)
  other arithmetic  0.69 us (1%)
    all_to_all x2, starting transfers between devices, to_peers(): lax.all_to_all(payload, axes, split_axis=0, concat_axis=0, tiled=True)  11.9 us
    pallas_call x1, Pallas kernels, remap(): pl.pallas_call(remap_body, out_shape=jax.ShapeDtypeStruct((ROWS, COLS), F...  8.34 us
    pallas_call x1, Pallas kernels, atmos_flux(): pl.pallas_call(atmos_flux_body, out_shape=(jax.ShapeDtypeStruct((RANKS, A...  8.22 us
    pallas_call x1, Pallas kernels, atmosphere(): shadow_call(substeps_body, block, [VMEM] * 6 + [ANY], scratch_shapes=[wide])  6.93 us
    ppermute x2, starting transfers between devices, from_neighbours(): return (lax.ppermute(last, 'gx', up), lax.ppermute(first, 'gx', down))  5.81 us
    ppermute x1, starting transfers between devices, local(): other = lax.ppermute(cross, 'comp', [(0, 1), (1, 0)])  4.51 us
    ppermute x6, starting transfers between devices, from_mate(): return lax.ppermute(field, 'gy', [(0, 1), (1, 0)])  3.33 us
    pallas_call x1, Pallas kernels, atmosphere(): moved = shadow_call(local_body, block, [VMEM], us=3)(own)  3.01 us
  transfers between devices with their start and end apart: 11, of which 3 were waited for; matrix products, arithmetic and copies ran while one was open for 2% of the time, Pallas kernels for 33%

profile of v6, /device:TPU:1, one launch (start us, length us, event | category | flops | bytes accessed | tf_op | source)
XLA Modules:
  0.0 63.5 jit_solution(7651535788854924987)
XLA Ops:
  0.6 1.0 %shard_map.95 = (bf16[2,256,128]{2,1,0:T(8,128)(2,1)S(1)}, f32[8,128]{1,0:T(8,128)S(1)}, f32[8,128]{1,0:T(8,128)S(1)}) custom-call(s32[1]{0:T(128)} %bitcast.16.side_ref, f32[8,256,128]{2,1,0:T(8,128)} %bitcast.21), custom_call_target="tpu_custom_call" | custom-call | tf_op jit(solution)/shard_map/pallas_call | solution.py:135
  1.7 4.5 %collective-permute-start.13 = (bf16[2,256,128]{2,1,0:T(8,128)(2,1)S(1)}, bf16[2,256,128]{2,1,0:T(8,128)(2,1)}, u32[]{:S(2)}, u32[]{:S(2)}) collective-permute-start(bf16[2,256,128]{2,1,0:T(8,128)(2,1)S(1)} %get-tuple-element.104), channel_id=1, source_target_pairs={{0,64},{64,0},{1,65},{65,1},{2,66},{66,2},{3,67},{67,3},{4,68},{68... | collective-permute-start | bytes 393224 | tf_op jit(solution)/shard_map/ppermute | solution.py:768
  6.2 8.2 %conditional.2 = (bf16[64,24,128]{2,1,0:T(8,128)(2,1)}, s32[4,256]{1,0:T(4,128)}, f32[8,128]{1,0:T(8,128)}, f32[8,128]{1,0:T(8,128)}) conditional(s32[]{:T(128)} %convert_element_type.10, (f32[8,128]{1,0:T(8,128)S(1)}, f32[8,128]{1,0:T(8,128)S(1)}) %tuple.30, (s32[256,2]{0,1:T(2,128)}, s32[256,2]{0,1:T(2,128)}, f32[8,256,128]{2,1,0:T(8,128)}, ...), branch_computations={%region_0.0_spmd, %region_1.0_spmd} | conditional | bytes 32880 | solution.py:787
  6.2 8.2 %branch_1_fun.10 = (bf16[64,24,128]{2,1,0:T(8,128)(2,1)}, s32[4,256]{1,0:T(4,128)}) custom-call(s32[2,256]{1,0:T(2,128)} %bitcast.27, s32[2,256]{1,0:T(2,128)} %bitcast.29, f32[8,256,128]{2,1,0:T(8,128)} %get-tuple-element.61.own_ref, f32[256,128]{1,0:T(8,128)} %get-tuple-element.62.prior_ref, f32[8,256,128]{2,1,0:T(8,128)} %get-tuple-element.63.factor_ref, ...), custom_call_target="tpu_custom_call" | custom-call | tf_op jit(solution)/shard_map/cond/branch_1_fun/pallas_call | solution.py:349
  14.4 48.9 %conditional.3 = (f32[1,8,256,128]{3,2,1,0:T(8,128)}, f32[1,256,128]{2,1,0:T(8,128)}) conditional(s32[]{:T(128)} %convert_element_type.10, (s32[256,2]{0,1:T(2,128)}, s32[256,2]{0,1:T(2,128)}, bf16[2,256,128]{2,1,0:T(8,128)(2,1)}, f32[256,128]{1,0:T(8,128)}, f32[8,256,128]{2,1,0:T(8,128)}, /*index=5*/bf16[256,2,128,128]{3,2,1,0:T(8,128)(2,1)}, ...), branch_computations={%region_2.0_spmd, %region_3.0_spmd} | conditional | flops 20482 | bytes 28014636 | solution.py:846
  14.4 1.0 %collective-permute-start.7 = (bf16[2,256,128]{2,1,0:T(8,128)(2,1)}, bf16[2,256,128]{2,1,0:T(8,128)(2,1)S(1)}, u32[]{:S(2)}, u32[]{:S(2)}) collective-permute-start(bf16[2,256,128]{2,1,0:T(8,128)(2,1)} %get-tuple-element.82.other_ref), channel_id=1, source_target_pairs={{0,1},{1,0},{2,3},{3,2},{4,5},{5,4},{6,7},{7,6},{8,9},{9,8},{10,11... | collective-permute-start | bytes 393224 | tf_op jit(solution)/shard_map/cond/branch_1_fun/ppermute | solution.py:592
  15.5 7.5 %all-to-all-start.1 = ((bf16[32,48,128]{2,1,0:T(8,128)(2,1)}), bf16[32,48,128]{2,1,0:T(8,128)(2,1)S(1)}, u32[]{:S(2)}, u32[]{:S(2)}) async-start(bf16[32,48,128]{2,1,0:T(8,128)(2,1)} %bitcast.26), calls=%async_computation.1 | async-start | bytes 786432 | tf_op jit(solution)/shard_map/cond/branch_1_fun/all_to_all | solution.py:748
  23.0 0.8 %fusion = (f32[8,8,128]{2,1,0:T(8,128)S(1)}, f32[8,8,128]{2,1,0:T(8,128)S(1)}) fusion(f32[8,256,128]{2,1,0:T(8,128)} %get-tuple-element.81.u_ref.own_ref), kind=kLoop, calls=%fused_computation.4 | loop fusion | bytes 131072 | tf_op jit(solution)/shard_map/cond/branch_1_fun/slice | solution.py:580
  23.8 0.7 %slice_convert_fusion = (f32[1,8,128]{2,1,0:T(8,128)S(1)}, f32[1,8,128]{2,1,0:T(8,128)S(1)}) fusion(bf16[2,256,128]{2,1,0:T(8,128)(2,1)} %get-tuple-element.82.other_ref), kind=kLoop, calls=%fused_computation.2 | loop fusion | flops 2048 | bytes 12288 | tf_op jit(solution)/shard_map/cond/branch_1_fun/convert_element_type | solution.py:580
  24.5 1.2 %collective-permute-start.5 = (f32[9,8,128]{2,1,0:T(8,128)S(1)}, f32[9,8,128]{2,1,0:T(8,128)S(1)}, u32[]{:S(2)}, u32[]{:S(2)}) collective-permute-start(f32[9,8,128]{2,1,0:T(8,128)S(1)} %pad_maximum_fusion), channel_id=1, source_target_pairs={{0,2},{2,4},{4,6},{6,8},{8,10},{10,12},{12,14},{14,16},{16,18},{18... | collective-permute-start | bytes 110600 | tf_op jit(solution)/shard_map/cond/branch_1_fun/ppermute | solution.py:588
  25.7 4.6 %collective-permute-start.6 = (f32[9,8,128]{2,1,0:T(8,128)S(1)}, f32[9,8,128]{2,1,0:T(8,128)S(1)}, u32[]{:S(2)}, u32[]{:S(2)}) collective-permute-start(f32[9,8,128]{2,1,0:T(8,128)S(1)} %pad_maximum_fusion.1), channel_id=1, source_target_pairs={{2,0},{4,2},{6,4},{8,6},{10,8},{12,10},{14,12},{16,14},{18,16},{20... | collective-permute-start | bytes 110600 | tf_op jit(solution)/shard_map/cond/branch_1_fun/ppermute | solution.py:588
  30.3 3.0 %branch_1_fun.13.local_ref = f32[8,256,128]{2,1,0:T(8,128)S(1)} custom-call(f32[8,256,128]{2,1,0:T(8,128)} %get-tuple-element.81.u_ref.own_ref), custom_call_target="tpu_custom_call" | custom-call | bytes 11070000 | tf_op jit(solution)/shard_map/cond/branch_1_fun/pallas_call | solution.py:796
  33.3 2.2 %branch_1_fun.14 = (f32[256,128]{1,0:T(8,128)S(1)}, f32[8,128]{1,0:T(8,128)S(1)}) custom-call(bf16[2,256,128]{2,1,0:T(8,128)(2,1)} %get-tuple-element.82.other_ref, bf16[2,256,128]{2,1,0:T(8,128)(2,1)S(1)} %collective-permute-done.7.mate_ref, s32[6,256,128]{2,1,0:T(8,128)} %get-tuple-element.83.table_ref), custom_call_target="tpu_custom_call" | custom-call | bytes 7380000 | tf_op jit(solution)/shard_map/cond/branch_1_fun/pallas_call | solution.py:797
  35.6 0.7 %branch_1_fun.16 = (f32[2,256,128]{2,1,0:T(8,128)S(1)}, bf16[2,768,256]{2,1,0:T(8,128)(2,1)S(1)}) custom-call(s32[1]{0:T(128)} %bitcast.9.core_ref, bf16[64,24,128]{2,1,0:T(8,128)(2,1)S(1)} %bitcast.19, f32[256,128]{1,0:T(8,128)S(1)} %get-tuple-element.89.base_ref), custom_call_target="tpu_custom_call" | custom-call | tf_op jit(solution)/shard_map/cond/branch_1_fun/pallas_call | solution.py:803
  36.2 0.9 %collective-permute-start.11 = (f32[2,256,128]{2,1,0:T(8,128)S(1)}, f32[2,256,128]{2,1,0:T(8,128)S(1)}, u32[]{:S(2)}, u32[]{:S(2)}) collective-permute-start(f32[2,256,128]{2,1,0:T(8,128)S(1)} %get-tuple-element.90.mine_ref), channel_id=1, source_target_pairs={{0,1},{1,0},{2,3},{3,2},{4,5},{5,4},{6,7},{7,6},{8,9},{9,8},{10,11... | collective-permute-start | bytes 786440 | tf_op jit(solution)/shard_map/cond/branch_1_fun/ppermute | solution.py:592
  37.3 0.4 collective-permute-start.10
  37.8 1.1 %collective-permute-done.12.mate_weight_ref = f32[8,128]{1,0:T(8,128)S(1)} collective-permute-done((f32[8,128]{1,0:T(8,128)S(1)}, f32[8,128]{1,0:T(8,128)S(1)}, u32[]{:S(2)}, u32[]{:S(2)}) %collective-permute-start.12) | collective-permute-done | bytes 4128 | tf_op jit(solution)/shard_map/cond/branch_1_fun/ppermute | solution.py:592
  38.9 1.2 %branch_1_fun.17._ = bf16[32,2,24,128]{3,2,1,0:T(8,128)(2,1)} custom-call(s32[1]{0:T(128)} %bitcast.9.core_ref, f32[2,256,128]{2,1,0:T(8,128)S(1)} %get-tuple-element.90.mine_ref, f32[2,256,128]{2,1,0:T(8,128)S(1)} %collective-permute-done.11.mate_ref, f32[8,128]{1,0:T(8,128)S(1)} %get-tuple-element.91.weight_ref, ...), custom_call_target="tpu_custom_call" | custom-call | tf_op jit(solution)/shard_map/cond/branch_1_fun/pallas_call | solution.py:811
  40.1 4.4 %all-to-all-start.2 = ((bf16[32,48,128]{2,1,0:T(8,128)(2,1)}), bf16[32,48,128]{2,1,0:T(8,128)(2,1)S(1)}, u32[]{:S(2)}, u32[]{:S(2)}) async-start(bf16[32,48,128]{2,1,0:T(8,128)(2,1)} %bitcast.13), calls=%async_computation.2 | async-start | bytes 786432 | tf_op jit(solution)/shard_map/cond/branch_1_fun/all_to_all | solution.py:748
  44.8 0.7 %collective-permute-start.8 = (f32[256,128]{1,0:T(8,128)S(1)}, f32[256,128]{1,0:T(8,128)S(1)}, u32[]{:S(2)}, u32[]{:S(2)}) collective-permute-start(f32[256,128]{1,0:T(8,128)S(1)} %branch_1_fun.15), channel_id=1, source_target_pairs={{0,1},{1,0},{2,3},{3,2},{4,5},{5,4},{6,7},{7,6},{8,9},{9,8},{10,11... | collective-permute-start | bytes 393224 | tf_op jit(solution)/shard_map/cond/branch_1_fun/ppermute | solution.py:592
  45.6 1.0 %collective-permute-done.8.sides_ref = f32[256,128]{1,0:T(8,128)S(1)} collective-permute-done((f32[256,128]{1,0:T(8,128)S(1)}, f32[256,128]{1,0:T(8,128)S(1)}, u32[]{:S(2)}, u32[]{:S(2)}) %collective-permute-start.8) | collective-permute-done | bytes 131104 | tf_op jit(solution)/shard_map/cond/branch_1_fun/ppermute | solution.py:592
  46.6 6.9 %branch_1_fun.18 = f32[8,256,128]{2,1,0:T(8,128)} custom-call(f32[8,256,128]{2,1,0:T(8,128)S(1)} %branch_1_fun.13.local_ref, f32[256,128]{1,0:T(8,128)S(1)} %collective-permute-done.8.sides_ref, f32[9,8,128]{2,1,0:T(8,128)S(1)} %collective-permute-done.5.before_ref, f32[9,8,128]{2,1,0:T(8,128)S(1)} %collective-permute-done.6.after_ref, ...), custom_call_target="tpu_custom_call" | custom-call | tf_op jit(solution)/shard_map/cond/branch_1_fun/pallas_call | solution.py:818
  53.5 1.2 %all-to-all-done.2 = bf16[32,48,128]{2,1,0:T(8,128)(2,1)S(1)} async-done(((bf16[32,48,128]{2,1,0:T(8,128)(2,1)}), bf16[32,48,128]{2,1,0:T(8,128)(2,1)S(1)}, u32[]{:S(2)}, u32[]{:S(2)}) %all-to-all-start.2) | async-done | bytes 393248 | tf_op jit(solution)/shard_map/cond/branch_1_fun/all_to_all | solution.py:748
  54.7 8.3 %branch_1_fun.19 = f32[256,128]{1,0:T(8,128)} custom-call(s32[4,256]{1,0:T(4,128)S(1)} %copy-done.2, bf16[64,24,128]{2,1,0:T(8,128)(2,1)S(1)} %bitcast.20, bf16[256,2,128,128]{3,2,1,0:T(8,128)(2,1)} %get-tuple-element.94.w_ref), custom_call_target="tpu_custom_call" | custom-call | tf_op jit(solution)/shard_map/cond/branch_1_fun/pallas_call | solution.py:731
  (19 shorter events, 0.6 us)
Async XLA Ops:
  1.7 12.8 %collective-permute-start.13 = (bf16[2,256,128]{2,1,0:T(8,128)(2,1)S(1)}, bf16[2,256,128]{2,1,0:T(8,128)(2,1)}, u32[]{:S(2)}, u32[]{:S(2)}) collective-permute-start(bf16[2,256,128]{2,1,0:T(8,128)(2,1)S(1)} %get-tuple-element.104), channel_id=1, source_target_pairs={{0,64},{64,0},{1,65},{65,1},{2,66},{66,2},{3,67},{67,3},{4,68},{68... | collective-permute-start | bytes 393224 | tf_op jit(solution)/shard_map/ppermute | solution.py:768
  14.4 18.9 %collective-permute-start.7 = (bf16[2,256,128]{2,1,0:T(8,128)(2,1)}, bf16[2,256,128]{2,1,0:T(8,128)(2,1)S(1)}, u32[]{:S(2)}, u32[]{:S(2)}) collective-permute-start(bf16[2,256,128]{2,1,0:T(8,128)(2,1)} %get-tuple-element.82.other_ref), channel_id=1, source_target_pairs={{0,1},{1,0},{2,3},{3,2},{4,5},{5,4},{6,7},{7,6},{8,9},{9,8},{10,11... | collective-permute-start | bytes 393224 | tf_op jit(solution)/shard_map/cond/branch_1_fun/ppermute | solution.py:592
  15.5 20.1 %all-to-all-start.1 = ((bf16[32,48,128]{2,1,0:T(8,128)(2,1)}), bf16[32,48,128]{2,1,0:T(8,128)(2,1)S(1)}, u32[]{:S(2)}, u32[]{:S(2)}) async-start(bf16[32,48,128]{2,1,0:T(8,128)(2,1)} %bitcast.26), calls=%async_computation.1 | async-start | bytes 786432 | tf_op jit(solution)/shard_map/cond/branch_1_fun/all_to_all | solution.py:748
  24.5 11.1 %collective-permute-start.5 = (f32[9,8,128]{2,1,0:T(8,128)S(1)}, f32[9,8,128]{2,1,0:T(8,128)S(1)}, u32[]{:S(2)}, u32[]{:S(2)}) collective-permute-start(f32[9,8,128]{2,1,0:T(8,128)S(1)} %pad_maximum_fusion), channel_id=1, source_target_pairs={{0,2},{2,4},{4,6},{6,8},{8,10},{10,12},{12,14},{14,16},{16,18},{18... | collective-permute-start | bytes 110600 | tf_op jit(solution)/shard_map/cond/branch_1_fun/ppermute | solution.py:588
  25.7 9.8 %collective-permute-start.6 = (f32[9,8,128]{2,1,0:T(8,128)S(1)}, f32[9,8,128]{2,1,0:T(8,128)S(1)}, u32[]{:S(2)}, u32[]{:S(2)}) collective-permute-start(f32[9,8,128]{2,1,0:T(8,128)S(1)} %pad_maximum_fusion.1), channel_id=1, source_target_pairs={{2,0},{4,2},{6,4},{8,6},{10,8},{12,10},{14,12},{16,14},{18,16},{20... | collective-permute-start | bytes 110600 | tf_op jit(solution)/shard_map/cond/branch_1_fun/ppermute | solution.py:588
  33.3 11.2 %copy-start.1 = (f32[8,256,128]{2,1,0:T(8,128)S(1)}, f32[8,256,128]{2,1,0:T(8,128)}, u32[]{:S(2)}) copy-start(f32[8,256,128]{2,1,0:T(8,128)} %get-tuple-element.81.u_ref.own_ref) | copy-start | bytes 3145732 | tf_op jit(solution)/shard_map/cond
  36.2 2.6 %collective-permute-start.11 = (f32[2,256,128]{2,1,0:T(8,128)S(1)}, f32[2,256,128]{2,1,0:T(8,128)S(1)}, u32[]{:S(2)}, u32[]{:S(2)}) collective-permute-start(f32[2,256,128]{2,1,0:T(8,128)S(1)} %get-tuple-element.90.mine_ref), channel_id=1, source_target_pairs={{0,1},{1,0},{2,3},{3,2},{4,5},{5,4},{6,7},{7,6},{8,9},{9,8},{10,11... | collective-permute-start | bytes 786440 | tf_op jit(solution)/shard_map/cond/branch_1_fun/ppermute | solution.py:592
  37.2 1.7 %collective-permute-start.9 = (f32[9,8,128]{2,1,0:T(8,128)S(1)}, f32[9,8,128]{2,1,0:T(8,128)S(1)}, u32[]{:S(2)}, u32[]{:S(2)}) collective-permute-start(f32[9,8,128]{2,1,0:T(8,128)S(1)} %collective-permute-done.5.before_ref), channel_id=1, source_target_pairs={{0,1},{1,0},{2,3},{3,2},{4,5},{5,4},{6,7},{7,6},{8,9},{9,8},{10,11... | collective-permute-start | bytes 110600 | tf_op jit(solution)/shard_map/cond/branch_1_fun/ppermute | solution.py:592
  37.3 1.6 %collective-permute-start.10 = (f32[9,8,128]{2,1,0:T(8,128)S(1)}, f32[9,8,128]{2,1,0:T(8,128)S(1)}, u32[]{:S(2)}, u32[]{:S(2)}) collective-permute-start(f32[9,8,128]{2,1,0:T(8,128)S(1)} %collective-permute-done.6.after_ref), channel_id=1, source_target_pairs={{0,1},{1,0},{2,3},{3,2},{4,5},{5,4},{6,7},{7,6},{8,9},{9,8},{10,11... | collective-permute-start | bytes 110600 | tf_op jit(solution)/shard_map/cond/branch_1_fun/ppermute | solution.py:592
  37.7 1.2 %collective-permute-start.12 = (f32[8,128]{1,0:T(8,128)S(1)}, f32[8,128]{1,0:T(8,128)S(1)}, u32[]{:S(2)}, u32[]{:S(2)}) collective-permute-start(f32[8,128]{1,0:T(8,128)S(1)} %get-tuple-element.91.weight_ref), channel_id=1, source_target_pairs={{0,1},{1,0},{2,3},{3,2},{4,5},{5,4},{6,7},{7,6},{8,9},{9,8},{10,11... | collective-permute-start | bytes 12296 | tf_op jit(solution)/shard_map/cond/branch_1_fun/ppermute | solution.py:592
  40.1 14.6 %copy-start.2 = (s32[4,256]{1,0:T(4,128)S(1)}, s32[4,256]{1,0:T(4,128)}, u32[]{:S(2)}) copy-start(s32[4,256]{1,0:T(4,128)} %get-tuple-element.93.pos_hbm_ref) | copy-start | bytes 12292 | tf_op jit(solution)/shard_map/cond
  40.1 14.6 %all-to-all-start.2 = ((bf16[32,48,128]{2,1,0:T(8,128)(2,1)}), bf16[32,48,128]{2,1,0:T(8,128)(2,1)S(1)}, u32[]{:S(2)}, u32[]{:S(2)}) async-start(bf16[32,48,128]{2,1,0:T(8,128)(2,1)} %bitcast.13), calls=%async_computation.2 | async-start | bytes 786432 | tf_op jit(solution)/shard_map/cond/branch_1_fun/all_to_all | solution.py:748
  44.8 1.7 %collective-permute-start.8 = (f32[256,128]{1,0:T(8,128)S(1)}, f32[256,128]{1,0:T(8,128)S(1)}, u32[]{:S(2)}, u32[]{:S(2)}) collective-permute-start(f32[256,128]{1,0:T(8,128)S(1)} %branch_1_fun.15), channel_id=1, source_target_pairs={{0,1},{1,0},{2,3},{3,2},{4,5},{5,4},{6,7},{7,6},{8,9},{9,8},{10,11... | collective-permute-start | bytes 393224 | tf_op jit(solution)/shard_map/cond/branch_1_fun/ppermute | solution.py:592

commit v7 on v6

--- a/solution.py
+++ b/solution.py
@@ -669,11 +669,14 @@
         summed = jnp.dot(hits, both, preferred_element_type=F32)
         forcing += [summed[:, :COLS], summed[:, COLS:]]
     first_ref[...] = forcing[0]
-    for l in range(LEV):
-        level = base_ref[l]
-        for f in range(NF):
-            level += share_ref[l, f] * forcing[f]
-        out_ref[l] = level
+    for begin in range(0, ROWS, 32):
+        part = slice(begin, begin + 32)
+        near = [v[part] for v in forcing]
+        for l in range(LEV):
+            level = base_ref[l, part, :]
+            for f in range(NF):
+                level += share_ref[l, f] * near[f]
+            out_ref[l, part, :] = level
 
 
 def ocean_sums(arrived, base, share):
@@ -790,12 +793,13 @@
 
     def atmosphere():
         by_chip = (RANKS // CORES, CORES * ATMOS_SLOTS, COLS)
-        rows = from_neighbours(*edge_rows(own, other[:1]))
+        *edges, later = lax.optimization_barrier((*edge_rows(own, other[:1]), other))
+        rows = from_neighbours(*edges)
         arrived = to_peers(packed.reshape(by_chip), "gx")
         sides = from_mate(shadow_call(sides_body, plane, [VMEM])(own))
         moved = shadow_call(local_body, block, [VMEM], us=3)(own)
         base, weights = shadow_call(top_base_body, (plane, edge_shape), [VMEM] * 3, us=2)(
-            other, from_mate(other), adjacent_cell_table
+            other, from_mate(later), adjacent_cell_table
         )
         *rows, moved, base = lax.optimization_barrier((*rows, moved, base))
         rows = [*rows, *map(from_mate, rows)]

time: 64.5 us -> 64.5 us (level)
  no operation moved by 1% of the time
where the time goes in v7:
time: 64.5 us; the launch traced here: 63.6 us
  Pallas kernels  32 us (50%)
  starting transfers between devices  25.6 us (40%)
  waiting for transfers between devices  3.26 us (5%)
  between operations  0.86 us (1%)
  local copies, waits for them, and re-layouts  0.79 us (1%)
  other arithmetic  0.7 us (1%)
    all_to_all x2, starting transfers between devices, to_peers(): lax.all_to_all(payload, axes, split_axis=0, concat_axis=0, tiled=True)  11.9 us
    pallas_call x1, Pallas kernels, remap(): pl.pallas_call(remap_body, out_shape=jax.ShapeDtypeStruct((ROWS, COLS), F...  8.38 us
    pallas_call x1, Pallas kernels, atmos_flux(): pl.pallas_call(atmos_flux_body, out_shape=(jax.ShapeDtypeStruct((RANKS, A...  8.22 us
    pallas_call x1, Pallas kernels, atmosphere(): shadow_call(substeps_body, block, [VMEM] * 6 + [ANY], scratch_shapes=[wide])  6.93 us
    ppermute x2, starting transfers between devices, from_neighbours(): return (lax.ppermute(last, 'gx', up), lax.ppermute(first, 'gx', down))  5.82 us
    ppermute x1, starting transfers between devices, local(): other = lax.ppermute(cross, 'comp', [(0, 1), (1, 0)])  4.51 us
    ppermute x6, starting transfers between devices, from_mate(): return lax.ppermute(field, 'gy', [(0, 1), (1, 0)])  3.36 us
    pallas_call x1, Pallas kernels, atmosphere(): moved = shadow_call(local_body, block, [VMEM], us=3)(own)  3.01 us
  transfers between devices with their start and end apart: 11, of which 3 were waited for; matrix products, arithmetic and copies ran while one was open for 2% of the time, Pallas kernels for 33%

profile of v7, /device:TPU:1, one launch (start us, length us, event | category | flops | bytes accessed | tf_op | source)
XLA Modules:
  0.0 63.6 jit_solution(7193040283495680691)
XLA Ops:
  0.6 1.0 %shard_map.95 = (bf16[2,256,128]{2,1,0:T(8,128)(2,1)S(1)}, f32[8,128]{1,0:T(8,128)S(1)}, f32[8,128]{1,0:T(8,128)S(1)}) custom-call(s32[1]{0:T(128)} %bitcast.16.side_ref, f32[8,256,128]{2,1,0:T(8,128)} %bitcast.21), custom_call_target="tpu_custom_call" | custom-call | tf_op jit(solution)/shard_map/pallas_call | solution.py:135
  1.7 4.5 %collective-permute-start.13 = (bf16[2,256,128]{2,1,0:T(8,128)(2,1)S(1)}, bf16[2,256,128]{2,1,0:T(8,128)(2,1)}, u32[]{:S(2)}, u32[]{:S(2)}) collective-permute-start(bf16[2,256,128]{2,1,0:T(8,128)(2,1)S(1)} %get-tuple-element.107), channel_id=1, source_target_pairs={{0,64},{64,0},{1,65},{65,1},{2,66},{66,2},{3,67},{67,3},{4,68},{68... | collective-permute-start | bytes 393224 | tf_op jit(solution)/shard_map/ppermute | solution.py:771
  6.2 8.2 %conditional.2 = (bf16[64,24,128]{2,1,0:T(8,128)(2,1)}, s32[4,256]{1,0:T(4,128)}, f32[8,128]{1,0:T(8,128)}, f32[8,128]{1,0:T(8,128)}) conditional(s32[]{:T(128)} %convert_element_type.10, (f32[8,128]{1,0:T(8,128)S(1)}, f32[8,128]{1,0:T(8,128)S(1)}) %tuple.31, (s32[256,2]{0,1:T(2,128)}, s32[256,2]{0,1:T(2,128)}, f32[8,256,128]{2,1,0:T(8,128)}, ...), branch_computations={%region_0.0_spmd, %region_1.0_spmd} | conditional | bytes 32880 | solution.py:790
  6.2 8.2 %branch_1_fun.10 = (bf16[64,24,128]{2,1,0:T(8,128)(2,1)}, s32[4,256]{1,0:T(4,128)}) custom-call(s32[2,256]{1,0:T(2,128)} %bitcast.27, s32[2,256]{1,0:T(2,128)} %bitcast.29, f32[8,256,128]{2,1,0:T(8,128)} %get-tuple-element.61.own_ref, f32[256,128]{1,0:T(8,128)} %get-tuple-element.62.prior_ref, f32[8,256,128]{2,1,0:T(8,128)} %get-tuple-element.63.factor_ref, ...), custom_call_target="tpu_custom_call" | custom-call | tf_op jit(solution)/shard_map/cond/branch_1_fun/pallas_call | solution.py:349
  14.4 49.0 %conditional.3 = (f32[1,8,256,128]{3,2,1,0:T(8,128)}, f32[1,256,128]{2,1,0:T(8,128)}) conditional(s32[]{:T(128)} %convert_element_type.10, (s32[256,2]{0,1:T(2,128)}, s32[256,2]{0,1:T(2,128)}, bf16[2,256,128]{2,1,0:T(8,128)(2,1)}, f32[256,128]{1,0:T(8,128)}, f32[8,256,128]{2,1,0:T(8,128)}, /*index=5*/bf16[256,2,128,128]{3,2,1,0:T(8,128)(2,1)}, ...), branch_computations={%region_2.0_spmd, %region_3.0_spmd} | conditional | flops 20482 | bytes 28014636 | solution.py:850
  14.4 7.5 %all-to-all-start.1 = ((bf16[32,48,128]{2,1,0:T(8,128)(2,1)}), bf16[32,48,128]{2,1,0:T(8,128)(2,1)S(1)}, u32[]{:S(2)}, u32[]{:S(2)}) async-start(bf16[32,48,128]{2,1,0:T(8,128)(2,1)} %bitcast.26), calls=%async_computation.1 | async-start | bytes 786432 | tf_op jit(solution)/shard_map/cond/branch_1_fun/all_to_all | solution.py:751
  22.0 0.8 %fusion = (f32[8,8,128]{2,1,0:T(8,128)S(1)}, f32[8,8,128]{2,1,0:T(8,128)S(1)}) fusion(f32[8,256,128]{2,1,0:T(8,128)} %get-tuple-element.81.u_ref.own_ref), kind=kLoop, calls=%fused_computation.4 | loop fusion | bytes 131072 | tf_op jit(solution)/shard_map/cond/branch_1_fun/slice | solution.py:580
  22.7 0.7 %slice_convert_fusion = (f32[1,8,128]{2,1,0:T(8,128)S(1)}, f32[1,8,128]{2,1,0:T(8,128)S(1)}) fusion(bf16[2,256,128]{2,1,0:T(8,128)(2,1)} %get-tuple-element.85.other_ref), kind=kLoop, calls=%fused_computation.2 | loop fusion | flops 2048 | bytes 12288 | tf_op jit(solution)/shard_map/cond/branch_1_fun/convert_element_type | solution.py:580
  23.4 1.3 %collective-permute-start.7 = (bf16[2,256,128]{2,1,0:T(8,128)(2,1)}, bf16[2,256,128]{2,1,0:T(8,128)(2,1)S(1)}, u32[]{:S(2)}, u32[]{:S(2)}) collective-permute-start(bf16[2,256,128]{2,1,0:T(8,128)(2,1)} %get-tuple-element.85.other_ref), channel_id=1, source_target_pairs={{0,1},{1,0},{2,3},{3,2},{4,5},{5,4},{6,7},{7,6},{8,9},{9,8},{10,11... | collective-permute-start | bytes 393224 | tf_op jit(solution)/shard_map/cond/branch_1_fun/ppermute | solution.py:592
  24.8 1.5 %collective-permute-start.5 = (f32[9,8,128]{2,1,0:T(8,128)S(1)}, f32[9,8,128]{2,1,0:T(8,128)S(1)}, u32[]{:S(2)}, u32[]{:S(2)}) collective-permute-start(f32[9,8,128]{2,1,0:T(8,128)S(1)} %get-tuple-element.83), channel_id=1, source_target_pairs={{0,2},{2,4},{4,6},{6,8},{8,10},{10,12},{12,14},{14,16},{16,18},{18... | collective-permute-start | bytes 110600 | tf_op jit(solution)/shard_map/cond/branch_1_fun/ppermute | solution.py:588
  26.3 4.3 %collective-permute-start.6 = (f32[9,8,128]{2,1,0:T(8,128)S(1)}, f32[9,8,128]{2,1,0:T(8,128)S(1)}, u32[]{:S(2)}, u32[]{:S(2)}) collective-permute-start(f32[9,8,128]{2,1,0:T(8,128)S(1)} %get-tuple-element.84), channel_id=1, source_target_pairs={{2,0},{4,2},{6,4},{8,6},{10,8},{12,10},{14,12},{16,14},{18,16},{20... | collective-permute-start | bytes 110600 | tf_op jit(solution)/shard_map/cond/branch_1_fun/ppermute | solution.py:588
  30.6 3.0 %branch_1_fun.13.local_ref = f32[8,256,128]{2,1,0:T(8,128)S(1)} custom-call(f32[8,256,128]{2,1,0:T(8,128)} %get-tuple-element.81.u_ref.own_ref), custom_call_target="tpu_custom_call" | custom-call | bytes 11070000 | tf_op jit(solution)/shard_map/cond/branch_1_fun/pallas_call | solution.py:800
  33.6 2.2 %branch_1_fun.14 = (f32[256,128]{1,0:T(8,128)S(1)}, f32[8,128]{1,0:T(8,128)S(1)}) custom-call(bf16[2,256,128]{2,1,0:T(8,128)(2,1)} %get-tuple-element.85.other_ref, bf16[2,256,128]{2,1,0:T(8,128)(2,1)S(1)} %collective-permute-done.7.mate_ref, s32[6,256,128]{2,1,0:T(8,128)} %get-tuple-element.86.table_ref), custom_call_target="tpu_custom_call" | custom-call | bytes 7380000 | tf_op jit(solution)/shard_map/cond/branch_1_fun/pallas_call | solution.py:801
  35.9 0.7 %branch_1_fun.16 = (f32[2,256,128]{2,1,0:T(8,128)S(1)}, bf16[2,768,256]{2,1,0:T(8,128)(2,1)S(1)}) custom-call(s32[1]{0:T(128)} %bitcast.9.core_ref, bf16[64,24,128]{2,1,0:T(8,128)(2,1)S(1)} %bitcast.19, f32[256,128]{1,0:T(8,128)S(1)} %get-tuple-element.92.base_ref), custom_call_target="tpu_custom_call" | custom-call | tf_op jit(solution)/shard_map/cond/branch_1_fun/pallas_call | solution.py:807
  36.6 0.7 %collective-permute-start.11 = (f32[2,256,128]{2,1,0:T(8,128)S(1)}, f32[2,256,128]{2,1,0:T(8,128)S(1)}, u32[]{:S(2)}, u32[]{:S(2)}) collective-permute-start(f32[2,256,128]{2,1,0:T(8,128)S(1)} %get-tuple-element.93.mine_ref), channel_id=1, source_target_pairs={{0,1},{1,0},{2,3},{3,2},{4,5},{5,4},{6,7},{7,6},{8,9},{9,8},{10,11... | collective-permute-start | bytes 786440 | tf_op jit(solution)/shard_map/cond/branch_1_fun/ppermute | solution.py:592
  37.3 0.4 collective-permute-start.10
  37.9 1.1 %collective-permute-done.12.mate_weight_ref = f32[8,128]{1,0:T(8,128)S(1)} collective-permute-done((f32[8,128]{1,0:T(8,128)S(1)}, f32[8,128]{1,0:T(8,128)S(1)}, u32[]{:S(2)}, u32[]{:S(2)}) %collective-permute-start.12) | collective-permute-done | bytes 4128 | tf_op jit(solution)/shard_map/cond/branch_1_fun/ppermute | solution.py:592
  38.9 1.2 %branch_1_fun.17._ = bf16[32,2,24,128]{3,2,1,0:T(8,128)(2,1)} custom-call(s32[1]{0:T(128)} %bitcast.9.core_ref, f32[2,256,128]{2,1,0:T(8,128)S(1)} %get-tuple-element.93.mine_ref, f32[2,256,128]{2,1,0:T(8,128)S(1)} %collective-permute-done.11.mate_ref, f32[8,128]{1,0:T(8,128)S(1)} %get-tuple-element.94.weight_ref, ...), custom_call_target="tpu_custom_call" | custom-call | tf_op jit(solution)/shard_map/cond/branch_1_fun/pallas_call | solution.py:815
  40.1 4.4 %all-to-all-start.2 = ((bf16[32,48,128]{2,1,0:T(8,128)(2,1)}), bf16[32,48,128]{2,1,0:T(8,128)(2,1)S(1)}, u32[]{:S(2)}, u32[]{:S(2)}) async-start(bf16[32,48,128]{2,1,0:T(8,128)(2,1)} %bitcast.13), calls=%async_computation.2 | async-start | bytes 786432 | tf_op jit(solution)/shard_map/cond/branch_1_fun/all_to_all | solution.py:751
  44.9 0.8 %collective-permute-start.8 = (f32[256,128]{1,0:T(8,128)S(1)}, f32[256,128]{1,0:T(8,128)S(1)}, u32[]{:S(2)}, u32[]{:S(2)}) collective-permute-start(f32[256,128]{1,0:T(8,128)S(1)} %branch_1_fun.15), channel_id=1, source_target_pairs={{0,1},{1,0},{2,3},{3,2},{4,5},{5,4},{6,7},{7,6},{8,9},{9,8},{10,11... | collective-permute-start | bytes 393224 | tf_op jit(solution)/shard_map/cond/branch_1_fun/ppermute | solution.py:592
  45.7 1.0 %collective-permute-done.8.sides_ref = f32[256,128]{1,0:T(8,128)S(1)} collective-permute-done((f32[256,128]{1,0:T(8,128)S(1)}, f32[256,128]{1,0:T(8,128)S(1)}, u32[]{:S(2)}, u32[]{:S(2)}) %collective-permute-start.8) | collective-permute-done | bytes 131104 | tf_op jit(solution)/shard_map/cond/branch_1_fun/ppermute | solution.py:592
  46.6 6.9 %branch_1_fun.18 = f32[8,256,128]{2,1,0:T(8,128)} custom-call(f32[8,256,128]{2,1,0:T(8,128)S(1)} %branch_1_fun.13.local_ref, f32[256,128]{1,0:T(8,128)S(1)} %collective-permute-done.8.sides_ref, f32[9,8,128]{2,1,0:T(8,128)S(1)} %collective-permute-done.5.before_ref, f32[9,8,128]{2,1,0:T(8,128)S(1)} %collective-permute-done.6.after_ref, ...), custom_call_target="tpu_custom_call" | custom-call | tf_op jit(solution)/shard_map/cond/branch_1_fun/pallas_call | solution.py:822
  53.6 1.2 %all-to-all-done.2 = bf16[32,48,128]{2,1,0:T(8,128)(2,1)S(1)} async-done(((bf16[32,48,128]{2,1,0:T(8,128)(2,1)}), bf16[32,48,128]{2,1,0:T(8,128)(2,1)S(1)}, u32[]{:S(2)}, u32[]{:S(2)}) %all-to-all-start.2) | async-done | bytes 393248 | tf_op jit(solution)/shard_map/cond/branch_1_fun/all_to_all | solution.py:751
  54.8 8.4 %branch_1_fun.19 = f32[256,128]{1,0:T(8,128)} custom-call(s32[4,256]{1,0:T(4,128)S(1)} %copy-done.2, bf16[64,24,128]{2,1,0:T(8,128)(2,1)S(1)} %bitcast.20, bf16[256,2,128,128]{3,2,1,0:T(8,128)(2,1)} %get-tuple-element.97.w_ref), custom_call_target="tpu_custom_call" | custom-call | tf_op jit(solution)/shard_map/cond/branch_1_fun/pallas_call | solution.py:734
  (18 shorter events, 0.6 us)
Async XLA Ops:
  1.7 12.8 %collective-permute-start.13 = (bf16[2,256,128]{2,1,0:T(8,128)(2,1)S(1)}, bf16[2,256,128]{2,1,0:T(8,128)(2,1)}, u32[]{:S(2)}, u32[]{:S(2)}) collective-permute-start(bf16[2,256,128]{2,1,0:T(8,128)(2,1)S(1)} %get-tuple-element.107), channel_id=1, source_target_pairs={{0,64},{64,0},{1,65},{65,1},{2,66},{66,2},{3,67},{67,3},{4,68},{68... | collective-permute-start | bytes 393224 | tf_op jit(solution)/shard_map/ppermute | solution.py:771
  14.4 21.4 %all-to-all-start.1 = ((bf16[32,48,128]{2,1,0:T(8,128)(2,1)}), bf16[32,48,128]{2,1,0:T(8,128)(2,1)S(1)}, u32[]{:S(2)}, u32[]{:S(2)}) async-start(bf16[32,48,128]{2,1,0:T(8,128)(2,1)} %bitcast.26), calls=%async_computation.1 | async-start | bytes 786432 | tf_op jit(solution)/shard_map/cond/branch_1_fun/all_to_all | solution.py:751
  23.4 10.2 %collective-permute-start.7 = (bf16[2,256,128]{2,1,0:T(8,128)(2,1)}, bf16[2,256,128]{2,1,0:T(8,128)(2,1)S(1)}, u32[]{:S(2)}, u32[]{:S(2)}) collective-permute-start(bf16[2,256,128]{2,1,0:T(8,128)(2,1)} %get-tuple-element.85.other_ref), channel_id=1, source_target_pairs={{0,1},{1,0},{2,3},{3,2},{4,5},{5,4},{6,7},{7,6},{8,9},{9,8},{10,11... | collective-permute-start | bytes 393224 | tf_op jit(solution)/shard_map/cond/branch_1_fun/ppermute | solution.py:592
  24.8 11.1 %collective-permute-start.5 = (f32[9,8,128]{2,1,0:T(8,128)S(1)}, f32[9,8,128]{2,1,0:T(8,128)S(1)}, u32[]{:S(2)}, u32[]{:S(2)}) collective-permute-start(f32[9,8,128]{2,1,0:T(8,128)S(1)} %get-tuple-element.83), channel_id=1, source_target_pairs={{0,2},{2,4},{4,6},{6,8},{8,10},{10,12},{12,14},{14,16},{16,18},{18... | collective-permute-start | bytes 110600 | tf_op jit(solution)/shard_map/cond/branch_1_fun/ppermute | solution.py:588
  26.3 9.6 %collective-permute-start.6 = (f32[9,8,128]{2,1,0:T(8,128)S(1)}, f32[9,8,128]{2,1,0:T(8,128)S(1)}, u32[]{:S(2)}, u32[]{:S(2)}) collective-permute-start(f32[9,8,128]{2,1,0:T(8,128)S(1)} %get-tuple-element.84), channel_id=1, source_target_pairs={{2,0},{4,2},{6,4},{8,6},{10,8},{12,10},{14,12},{16,14},{18,16},{20... | collective-permute-start | bytes 110600 | tf_op jit(solution)/shard_map/cond/branch_1_fun/ppermute | solution.py:588
  33.6 11.0 %copy-start.1 = (f32[8,256,128]{2,1,0:T(8,128)S(1)}, f32[8,256,128]{2,1,0:T(8,128)}, u32[]{:S(2)}) copy-start(f32[8,256,128]{2,1,0:T(8,128)} %get-tuple-element.81.u_ref.own_ref) | copy-start | bytes 3145732 | tf_op jit(solution)/shard_map/cond
  36.6 2.4 %collective-permute-start.11 = (f32[2,256,128]{2,1,0:T(8,128)S(1)}, f32[2,256,128]{2,1,0:T(8,128)S(1)}, u32[]{:S(2)}, u32[]{:S(2)}) collective-permute-start(f32[2,256,128]{2,1,0:T(8,128)S(1)} %get-tuple-element.93.mine_ref), channel_id=1, source_target_pairs={{0,1},{1,0},{2,3},{3,2},{4,5},{5,4},{6,7},{7,6},{8,9},{9,8},{10,11... | collective-permute-start | bytes 786440 | tf_op jit(solution)/shard_map/cond/branch_1_fun/ppermute | solution.py:592
  37.3 1.7 %collective-permute-start.9 = (f32[9,8,128]{2,1,0:T(8,128)S(1)}, f32[9,8,128]{2,1,0:T(8,128)S(1)}, u32[]{:S(2)}, u32[]{:S(2)}) collective-permute-start(f32[9,8,128]{2,1,0:T(8,128)S(1)} %collective-permute-done.5.before_ref), channel_id=1, source_target_pairs={{0,1},{1,0},{2,3},{3,2},{4,5},{5,4},{6,7},{7,6},{8,9},{9,8},{10,11... | collective-permute-start | bytes 110600 | tf_op jit(solution)/shard_map/cond/branch_1_fun/ppermute | solution.py:592
  37.3 1.6 %collective-permute-start.10 = (f32[9,8,128]{2,1,0:T(8,128)S(1)}, f32[9,8,128]{2,1,0:T(8,128)S(1)}, u32[]{:S(2)}, u32[]{:S(2)}) collective-permute-start(f32[9,8,128]{2,1,0:T(8,128)S(1)} %collective-permute-done.6.after_ref), channel_id=1, source_target_pairs={{0,1},{1,0},{2,3},{3,2},{4,5},{5,4},{6,7},{7,6},{8,9},{9,8},{10,11... | collective-permute-start | bytes 110600 | tf_op jit(solution)/shard_map/cond/branch_1_fun/ppermute | solution.py:592
  37.8 1.2 %collective-permute-start.12 = (f32[8,128]{1,0:T(8,128)S(1)}, f32[8,128]{1,0:T(8,128)S(1)}, u32[]{:S(2)}, u32[]{:S(2)}) collective-permute-start(f32[8,128]{1,0:T(8,128)S(1)} %get-tuple-element.94.weight_ref), channel_id=1, source_target_pairs={{0,1},{1,0},{2,3},{3,2},{4,5},{5,4},{6,7},{7,6},{8,9},{9,8},{10,11... | collective-permute-start | bytes 12296 | tf_op jit(solution)/shard_map/cond/branch_1_fun/ppermute | solution.py:592
  40.1 14.6 %copy-start.2 = (s32[4,256]{1,0:T(4,128)S(1)}, s32[4,256]{1,0:T(4,128)}, u32[]{:S(2)}) copy-start(s32[4,256]{1,0:T(4,128)} %get-tuple-element.96.pos_hbm_ref) | copy-start | bytes 12292 | tf_op jit(solution)/shard_map/cond
  40.1 14.6 %all-to-all-start.2 = ((bf16[32,48,128]{2,1,0:T(8,128)(2,1)}), bf16[32,48,128]{2,1,0:T(8,128)(2,1)S(1)}, u32[]{:S(2)}, u32[]{:S(2)}) async-start(bf16[32,48,128]{2,1,0:T(8,128)(2,1)} %bitcast.13), calls=%async_computation.2 | async-start | bytes 786432 | tf_op jit(solution)/shard_map/cond/branch_1_fun/all_to_all | solution.py:751
  44.9 1.7 %collective-permute-start.8 = (f32[256,128]{1,0:T(8,128)S(1)}, f32[256,128]{1,0:T(8,128)S(1)}, u32[]{:S(2)}, u32[]{:S(2)}) collective-permute-start(f32[256,128]{1,0:T(8,128)S(1)} %branch_1_fun.15), channel_id=1, source_target_pairs={{0,1},{1,0},{2,3},{3,2},{4,5},{5,4},{6,7},{7,6},{8,9},{9,8},{10,11... | collective-permute-start | bytes 393224 | tf_op jit(solution)/shard_map/cond/branch_1_fun/ppermute | solution.py:592

commit v8 on v6

--- a/solution.py
+++ b/solution.py
@@ -793,11 +793,11 @@
         rows = from_neighbours(*edge_rows(own, other[:1]))
         arrived = to_peers(packed.reshape(by_chip), "gx")
         sides = from_mate(shadow_call(sides_body, plane, [VMEM])(own))
-        moved = shadow_call(local_body, block, [VMEM], us=3)(own)
+        moved = shadow_call(local_body, block, [VMEM])(own)
         base, weights = shadow_call(top_base_body, (plane, edge_shape), [VMEM] * 3, us=2)(
             other, from_mate(other), adjacent_cell_table
         )
-        *rows, moved, base = lax.optimization_barrier((*rows, moved, base))
+        *rows, base = lax.optimization_barrier((*rows, base))
         rows = [*rows, *map(from_mate, rows)]
         core = lax.axis_index("gy").reshape(1)
         mine, hits = call(

time: 64.5 us -> 64.4 us (level)
  Pallas kernels: 31.9 us -> 30.6 us
  starting transfers between devices: 25.6 us -> 26.5 us
    ppermute x2, waiting for transfers between devices: 0.01 us -> 1.95 us  [from_neighbours(): return (lax.ppermute(last, 'gx', up), lax.ppermute(first, 'gx', down))]
    pallas_call x1, Pallas kernels: 3.01 us -> 1.78 us  [atmosphere(): moved = shadow_call(local_body, block, [VMEM])(own)]
    all_to_all x2, starting transfers between devices: 11.9 us -> 13.1 us  [to_peers(): lax.all_to_all(payload, axes, split_axis=0, concat_axis=0, tiled=True)]
    ppermute x6, waiting for transfers between devices: 2.07 us -> 1.09 us  [from_mate(): return lax.ppermute(field, 'gy', [(0, 1), (1, 0)])]
  transfers between devices with their start and end apart: 11 -> 11, of which waited for: 3 -> 3; matrix products, arithmetic and copies ran while one was open for 2% -> 2% of each run, Pallas kernels for 33% -> 31%
where the time goes in v8:
time: 64.4 us; the launch traced here: 63.5 us
  Pallas kernels  30.6 us (48%)
  starting transfers between devices  26.5 us (41%)
  waiting for transfers between devices  3.65 us (6%)
  between operations  0.84 us (1%)
  local copies, waits for them, and re-layouts  0.79 us (1%)
  other arithmetic  0.69 us (1%)
    all_to_all x2, starting transfers between devices, to_peers(): lax.all_to_all(payload, axes, split_axis=0, concat_axis=0, tiled=True)  13.1 us
    pallas_call x1, Pallas kernels, remap(): pl.pallas_call(remap_body, out_shape=jax.ShapeDtypeStruct((ROWS, COLS), F...  8.37 us
    pallas_call x1, Pallas kernels, atmos_flux(): pl.pallas_call(atmos_flux_body, out_shape=(jax.ShapeDtypeStruct((RANKS, A...  8.22 us
    pallas_call x1, Pallas kernels, atmosphere(): shadow_call(substeps_body, block, [VMEM] * 6 + [ANY], scratch_shapes=[wide])  6.91 us
    ppermute x2, starting transfers between devices, from_neighbours(): return (lax.ppermute(last, 'gx', up), lax.ppermute(first, 'gx', down))  5.81 us
    ppermute x1, starting transfers between devices, local(): other = lax.ppermute(cross, 'comp', [(0, 1), (1, 0)])  4.51 us
    ppermute x6, starting transfers between devices, from_mate(): return lax.ppermute(field, 'gy', [(0, 1), (1, 0)])  3.15 us
    pallas_call x1, Pallas kernels, atmosphere(): shadow_call(top_base_body, (plane, edge_shape), [VMEM] * 3, us=2)  2.14 us
  transfers between devices with their start and end apart: 11, of which 3 were waited for; matrix products, arithmetic and copies ran while one was open for 2% of the time, Pallas kernels for 31%

profile of v8, /device:TPU:1, one launch (start us, length us, event | category | flops | bytes accessed | tf_op | source)
XLA Modules:
  0.0 63.5 jit_solution(4212373545163557035)
XLA Ops:
  0.6 1.0 %shard_map.95 = (bf16[2,256,128]{2,1,0:T(8,128)(2,1)S(1)}, f32[8,128]{1,0:T(8,128)S(1)}, f32[8,128]{1,0:T(8,128)S(1)}) custom-call(s32[1]{0:T(128)} %bitcast.16.side_ref, f32[8,256,128]{2,1,0:T(8,128)} %bitcast.21), custom_call_target="tpu_custom_call" | custom-call | tf_op jit(solution)/shard_map/pallas_call | solution.py:135
  1.7 4.5 %collective-permute-start.13 = (bf16[2,256,128]{2,1,0:T(8,128)(2,1)S(1)}, bf16[2,256,128]{2,1,0:T(8,128)(2,1)}, u32[]{:S(2)}, u32[]{:S(2)}) collective-permute-start(bf16[2,256,128]{2,1,0:T(8,128)(2,1)S(1)} %get-tuple-element.103), channel_id=1, source_target_pairs={{0,64},{64,0},{1,65},{65,1},{2,66},{66,2},{3,67},{67,3},{4,68},{68... | collective-permute-start | bytes 393224 | tf_op jit(solution)/shard_map/ppermute | solution.py:768
  6.2 8.2 %conditional.2 = (bf16[64,24,128]{2,1,0:T(8,128)(2,1)}, s32[4,256]{1,0:T(4,128)}, f32[8,128]{1,0:T(8,128)}, f32[8,128]{1,0:T(8,128)}) conditional(s32[]{:T(128)} %convert_element_type.10, (f32[8,128]{1,0:T(8,128)S(1)}, f32[8,128]{1,0:T(8,128)S(1)}) %tuple.30, (s32[256,2]{0,1:T(2,128)}, s32[256,2]{0,1:T(2,128)}, f32[8,256,128]{2,1,0:T(8,128)}, ...), branch_computations={%region_0.0_spmd, %region_1.0_spmd} | conditional | bytes 32880 | solution.py:787
  6.2 8.2 %branch_1_fun.10 = (bf16[64,24,128]{2,1,0:T(8,128)(2,1)}, s32[4,256]{1,0:T(4,128)}) custom-call(s32[2,256]{1,0:T(2,128)} %bitcast.27, s32[2,256]{1,0:T(2,128)} %bitcast.29, f32[8,256,128]{2,1,0:T(8,128)} %get-tuple-element.61.own_ref, f32[256,128]{1,0:T(8,128)} %get-tuple-element.62.prior_ref, f32[8,256,128]{2,1,0:T(8,128)} %get-tuple-element.63.factor_ref, ...), custom_call_target="tpu_custom_call" | custom-call | tf_op jit(solution)/shard_map/cond/branch_1_fun/pallas_call | solution.py:349
  14.4 48.9 %conditional.3 = (f32[1,8,256,128]{3,2,1,0:T(8,128)}, f32[1,256,128]{2,1,0:T(8,128)}) conditional(s32[]{:T(128)} %convert_element_type.10, (s32[256,2]{0,1:T(2,128)}, s32[256,2]{0,1:T(2,128)}, bf16[2,256,128]{2,1,0:T(8,128)(2,1)}, f32[256,128]{1,0:T(8,128)}, f32[8,256,128]{2,1,0:T(8,128)}, /*index=5*/bf16[256,2,128,128]{3,2,1,0:T(8,128)(2,1)}, ...), branch_computations={%region_2.0_spmd, %region_3.0_spmd} | conditional | flops 20482 | bytes 16944636 | solution.py:846
  14.4 1.0 %collective-permute-start.8 = (bf16[2,256,128]{2,1,0:T(8,128)(2,1)}, bf16[2,256,128]{2,1,0:T(8,128)(2,1)S(1)}, u32[]{:S(2)}, u32[]{:S(2)}) collective-permute-start(bf16[2,256,128]{2,1,0:T(8,128)(2,1)} %get-tuple-element.82.other_ref), channel_id=1, source_target_pairs={{0,1},{1,0},{2,3},{3,2},{4,5},{5,4},{6,7},{7,6},{8,9},{9,8},{10,11... | collective-permute-start | bytes 393224 | tf_op jit(solution)/shard_map/cond/branch_1_fun/ppermute | solution.py:592
  15.5 7.6 %all-to-all-start.1 = ((bf16[32,48,128]{2,1,0:T(8,128)(2,1)}), bf16[32,48,128]{2,1,0:T(8,128)(2,1)S(1)}, u32[]{:S(2)}, u32[]{:S(2)}) async-start(bf16[32,48,128]{2,1,0:T(8,128)(2,1)} %bitcast.26), calls=%async_computation.1 | async-start | bytes 786432 | tf_op jit(solution)/shard_map/cond/branch_1_fun/all_to_all | solution.py:748
  23.1 0.8 %fusion = (f32[8,8,128]{2,1,0:T(8,128)S(1)}, f32[8,8,128]{2,1,0:T(8,128)S(1)}) fusion(f32[8,256,128]{2,1,0:T(8,128)} %get-tuple-element.81.u_ref.own_ref), kind=kLoop, calls=%fused_computation.4 | loop fusion | bytes 131072 | tf_op jit(solution)/shard_map/cond/branch_1_fun/slice | solution.py:580
  23.9 0.7 %slice_convert_fusion = (f32[1,8,128]{2,1,0:T(8,128)S(1)}, f32[1,8,128]{2,1,0:T(8,128)S(1)}) fusion(bf16[2,256,128]{2,1,0:T(8,128)(2,1)} %get-tuple-element.82.other_ref), kind=kLoop, calls=%fused_computation.2 | loop fusion | flops 2048 | bytes 12288 | tf_op jit(solution)/shard_map/cond/branch_1_fun/convert_element_type | solution.py:580
  24.6 1.2 %collective-permute-start.6 = (f32[9,8,128]{2,1,0:T(8,128)S(1)}, f32[9,8,128]{2,1,0:T(8,128)S(1)}, u32[]{:S(2)}, u32[]{:S(2)}) collective-permute-start(f32[9,8,128]{2,1,0:T(8,128)S(1)} %pad_maximum_fusion), channel_id=1, source_target_pairs={{0,2},{2,4},{4,6},{6,8},{8,10},{10,12},{12,14},{14,16},{16,18},{18... | collective-permute-start | bytes 110600 | tf_op jit(solution)/shard_map/cond/branch_1_fun/ppermute | solution.py:588
  25.8 4.6 %collective-permute-start.7 = (f32[9,8,128]{2,1,0:T(8,128)S(1)}, f32[9,8,128]{2,1,0:T(8,128)S(1)}, u32[]{:S(2)}, u32[]{:S(2)}) collective-permute-start(f32[9,8,128]{2,1,0:T(8,128)S(1)} %pad_maximum_fusion.1), channel_id=1, source_target_pairs={{2,0},{4,2},{6,4},{8,6},{10,8},{12,10},{14,12},{16,14},{18,16},{20... | collective-permute-start | bytes 110600 | tf_op jit(solution)/shard_map/cond/branch_1_fun/ppermute | solution.py:588
  30.4 2.1 %branch_1_fun.15 = (f32[256,128]{1,0:T(8,128)S(1)}, f32[8,128]{1,0:T(8,128)S(1)}) custom-call(bf16[2,256,128]{2,1,0:T(8,128)(2,1)} %get-tuple-element.82.other_ref, bf16[2,256,128]{2,1,0:T(8,128)(2,1)S(1)} %collective-permute-done.8.mate_ref, s32[6,256,128]{2,1,0:T(8,128)} %get-tuple-element.83.table_ref), custom_call_target="tpu_custom_call" | custom-call | bytes 7380000 | tf_op jit(solution)/shard_map/cond/branch_1_fun/pallas_call | solution.py:797
  32.5 1.9 %collective-permute-done.6.before_ref = f32[9,8,128]{2,1,0:T(8,128)S(1)} collective-permute-done((f32[9,8,128]{2,1,0:T(8,128)S(1)}, f32[9,8,128]{2,1,0:T(8,128)S(1)}, u32[]{:S(2)}, u32[]{:S(2)}) %collective-permute-start.6) | collective-permute-done | bytes 36896 | tf_op jit(solution)/shard_map/cond/branch_1_fun/ppermute | solution.py:588
  34.5 0.7 %branch_1_fun.16 = (f32[2,256,128]{2,1,0:T(8,128)S(1)}, bf16[2,768,256]{2,1,0:T(8,128)(2,1)S(1)}) custom-call(s32[1]{0:T(128)} %bitcast.9.core_ref, bf16[64,24,128]{2,1,0:T(8,128)(2,1)S(1)} %bitcast.19, f32[256,128]{1,0:T(8,128)S(1)} %get-tuple-element.88.base_ref), custom_call_target="tpu_custom_call" | custom-call | tf_op jit(solution)/shard_map/cond/branch_1_fun/pallas_call | solution.py:803
  35.2 1.0 %collective-permute-start.11 = (f32[2,256,128]{2,1,0:T(8,128)S(1)}, f32[2,256,128]{2,1,0:T(8,128)S(1)}, u32[]{:S(2)}, u32[]{:S(2)}) collective-permute-start(f32[2,256,128]{2,1,0:T(8,128)S(1)} %get-tuple-element.89.mine_ref), channel_id=1, source_target_pairs={{0,1},{1,0},{2,3},{3,2},{4,5},{5,4},{6,7},{7,6},{8,9},{9,8},{10,11... | collective-permute-start | bytes 786440 | tf_op jit(solution)/shard_map/cond/branch_1_fun/ppermute | solution.py:592
  36.3 0.4 collective-permute-start.10
  36.8 1.1 %collective-permute-done.12.mate_weight_ref = f32[8,128]{1,0:T(8,128)S(1)} collective-permute-done((f32[8,128]{1,0:T(8,128)S(1)}, f32[8,128]{1,0:T(8,128)S(1)}, u32[]{:S(2)}, u32[]{:S(2)}) %collective-permute-start.12) | collective-permute-done | bytes 4128 | tf_op jit(solution)/shard_map/cond/branch_1_fun/ppermute | solution.py:592
  37.9 1.2 %branch_1_fun.17._ = bf16[32,2,24,128]{3,2,1,0:T(8,128)(2,1)} custom-call(s32[1]{0:T(128)} %bitcast.9.core_ref, f32[2,256,128]{2,1,0:T(8,128)S(1)} %get-tuple-element.89.mine_ref, f32[2,256,128]{2,1,0:T(8,128)S(1)} %collective-permute-done.11.mate_ref, f32[8,128]{1,0:T(8,128)S(1)} %get-tuple-element.90.weight_ref, ...), custom_call_target="tpu_custom_call" | custom-call | tf_op jit(solution)/shard_map/cond/branch_1_fun/pallas_call | solution.py:811
  39.0 5.4 %all-to-all-start.2 = ((bf16[32,48,128]{2,1,0:T(8,128)(2,1)}), bf16[32,48,128]{2,1,0:T(8,128)(2,1)S(1)}, u32[]{:S(2)}, u32[]{:S(2)}) async-start(bf16[32,48,128]{2,1,0:T(8,128)(2,1)} %bitcast.13), calls=%async_computation.2 | async-start | bytes 786432 | tf_op jit(solution)/shard_map/cond/branch_1_fun/all_to_all | solution.py:748
  44.9 0.5 collective-permute-start.5
  45.4 1.8 %branch_1_fun.13.local_ref = f32[8,256,128]{2,1,0:T(8,128)S(1)} custom-call(f32[8,256,128]{2,1,0:T(8,128)S(1)} %copy-done.1), custom_call_target="tpu_custom_call" | custom-call | tf_op jit(solution)/shard_map/cond/branch_1_fun/pallas_call | solution.py:796
  47.2 6.9 %branch_1_fun.18 = f32[8,256,128]{2,1,0:T(8,128)} custom-call(f32[8,256,128]{2,1,0:T(8,128)S(1)} %branch_1_fun.13.local_ref, f32[256,128]{1,0:T(8,128)S(1)} %collective-permute-done.5.sides_ref, f32[9,8,128]{2,1,0:T(8,128)S(1)} %collective-permute-done.6.before_ref, f32[9,8,128]{2,1,0:T(8,128)S(1)} %collective-permute-done.7.after_ref, ...), custom_call_target="tpu_custom_call" | custom-call | tf_op jit(solution)/shard_map/cond/branch_1_fun/pallas_call | solution.py:818
  54.1 0.6 all-to-all-done.2
  54.7 8.4 %branch_1_fun.19 = f32[256,128]{1,0:T(8,128)} custom-call(s32[4,256]{1,0:T(4,128)S(1)} %copy-done.2, bf16[64,24,128]{2,1,0:T(8,128)(2,1)S(1)} %bitcast.20, bf16[256,2,128,128]{3,2,1,0:T(8,128)(2,1)} %get-tuple-element.93.w_ref), custom_call_target="tpu_custom_call" | custom-call | tf_op jit(solution)/shard_map/cond/branch_1_fun/pallas_call | solution.py:731
  (19 shorter events, 0.6 us)
Async XLA Ops:
  1.7 12.8 %collective-permute-start.13 = (bf16[2,256,128]{2,1,0:T(8,128)(2,1)S(1)}, bf16[2,256,128]{2,1,0:T(8,128)(2,1)}, u32[]{:S(2)}, u32[]{:S(2)}) collective-permute-start(bf16[2,256,128]{2,1,0:T(8,128)(2,1)S(1)} %get-tuple-element.103), channel_id=1, source_target_pairs={{0,64},{64,0},{1,65},{65,1},{2,66},{66,2},{3,67},{67,3},{4,68},{68... | collective-permute-start | bytes 393224 | tf_op jit(solution)/shard_map/ppermute | solution.py:768
  14.4 16.0 %collective-permute-start.8 = (bf16[2,256,128]{2,1,0:T(8,128)(2,1)}, bf16[2,256,128]{2,1,0:T(8,128)(2,1)S(1)}, u32[]{:S(2)}, u32[]{:S(2)}) collective-permute-start(bf16[2,256,128]{2,1,0:T(8,128)(2,1)} %get-tuple-element.82.other_ref), channel_id=1, source_target_pairs={{0,1},{1,0},{2,3},{3,2},{4,5},{5,4},{6,7},{7,6},{8,9},{9,8},{10,11... | collective-permute-start | bytes 393224 | tf_op jit(solution)/shard_map/cond/branch_1_fun/ppermute | solution.py:592
  15.5 29.0 %copy-start.1 = (f32[8,256,128]{2,1,0:T(8,128)S(1)}, f32[8,256,128]{2,1,0:T(8,128)}, u32[]{:S(2)}) copy-start(f32[8,256,128]{2,1,0:T(8,128)} %get-tuple-element.81.u_ref.own_ref) | copy-start | bytes 3145732 | tf_op jit(solution)/shard_map/cond
  15.5 19.0 %all-to-all-start.1 = ((bf16[32,48,128]{2,1,0:T(8,128)(2,1)}), bf16[32,48,128]{2,1,0:T(8,128)(2,1)S(1)}, u32[]{:S(2)}, u32[]{:S(2)}) async-start(bf16[32,48,128]{2,1,0:T(8,128)(2,1)} %bitcast.26), calls=%async_computation.1 | async-start | bytes 786432 | tf_op jit(solution)/shard_map/cond/branch_1_fun/all_to_all | solution.py:748
  24.6 9.9 %collective-permute-start.6 = (f32[9,8,128]{2,1,0:T(8,128)S(1)}, f32[9,8,128]{2,1,0:T(8,128)S(1)}, u32[]{:S(2)}, u32[]{:S(2)}) collective-permute-start(f32[9,8,128]{2,1,0:T(8,128)S(1)} %pad_maximum_fusion), channel_id=1, source_target_pairs={{0,2},{2,4},{4,6},{6,8},{8,10},{10,12},{12,14},{14,16},{16,18},{18... | collective-permute-start | bytes 110600 | tf_op jit(solution)/shard_map/cond/branch_1_fun/ppermute | solution.py:588
  25.8 8.7 %collective-permute-start.7 = (f32[9,8,128]{2,1,0:T(8,128)S(1)}, f32[9,8,128]{2,1,0:T(8,128)S(1)}, u32[]{:S(2)}, u32[]{:S(2)}) collective-permute-start(f32[9,8,128]{2,1,0:T(8,128)S(1)} %pad_maximum_fusion.1), channel_id=1, source_target_pairs={{2,0},{4,2},{6,4},{8,6},{10,8},{12,10},{14,12},{16,14},{18,16},{20... | collective-permute-start | bytes 110600 | tf_op jit(solution)/shard_map/cond/branch_1_fun/ppermute | solution.py:588
  35.2 2.7 %collective-permute-start.11 = (f32[2,256,128]{2,1,0:T(8,128)S(1)}, f32[2,256,128]{2,1,0:T(8,128)S(1)}, u32[]{:S(2)}, u32[]{:S(2)}) collective-permute-start(f32[2,256,128]{2,1,0:T(8,128)S(1)} %get-tuple-element.89.mine_ref), channel_id=1, source_target_pairs={{0,1},{1,0},{2,3},{3,2},{4,5},{5,4},{6,7},{7,6},{8,9},{9,8},{10,11... | collective-permute-start | bytes 786440 | tf_op jit(solution)/shard_map/cond/branch_1_fun/ppermute | solution.py:592
  36.2 1.7 %collective-permute-start.9 = (f32[9,8,128]{2,1,0:T(8,128)S(1)}, f32[9,8,128]{2,1,0:T(8,128)S(1)}, u32[]{:S(2)}, u32[]{:S(2)}) collective-permute-start(f32[9,8,128]{2,1,0:T(8,128)S(1)} %collective-permute-done.6.before_ref), channel_id=1, source_target_pairs={{0,1},{1,0},{2,3},{3,2},{4,5},{5,4},{6,7},{7,6},{8,9},{9,8},{10,11... | collective-permute-start | bytes 110600 | tf_op jit(solution)/shard_map/cond/branch_1_fun/ppermute | solution.py:592
  36.3 1.6 %collective-permute-start.10 = (f32[9,8,128]{2,1,0:T(8,128)S(1)}, f32[9,8,128]{2,1,0:T(8,128)S(1)}, u32[]{:S(2)}, u32[]{:S(2)}) collective-permute-start(f32[9,8,128]{2,1,0:T(8,128)S(1)} %collective-permute-done.7.after_ref), channel_id=1, source_target_pairs={{0,1},{1,0},{2,3},{3,2},{4,5},{5,4},{6,7},{7,6},{8,9},{9,8},{10,11... | collective-permute-start | bytes 110600 | tf_op jit(solution)/shard_map/cond/branch_1_fun/ppermute | solution.py:592
  36.7 1.2 %collective-permute-start.12 = (f32[8,128]{1,0:T(8,128)S(1)}, f32[8,128]{1,0:T(8,128)S(1)}, u32[]{:S(2)}, u32[]{:S(2)}) collective-permute-start(f32[8,128]{1,0:T(8,128)S(1)} %get-tuple-element.90.weight_ref), channel_id=1, source_target_pairs={{0,1},{1,0},{2,3},{3,2},{4,5},{5,4},{6,7},{7,6},{8,9},{9,8},{10,11... | collective-permute-start | bytes 12296 | tf_op jit(solution)/shard_map/cond/branch_1_fun/ppermute | solution.py:592
  39.0 15.7 %all-to-all-start.2 = ((bf16[32,48,128]{2,1,0:T(8,128)(2,1)}), bf16[32,48,128]{2,1,0:T(8,128)(2,1)S(1)}, u32[]{:S(2)}, u32[]{:S(2)}) async-start(bf16[32,48,128]{2,1,0:T(8,128)(2,1)} %bitcast.13), calls=%async_computation.2 | async-start | bytes 786432 | tf_op jit(solution)/shard_map/cond/branch_1_fun/all_to_all | solution.py:748
  44.8 9.9 %copy-start.2 = (s32[4,256]{1,0:T(4,128)S(1)}, s32[4,256]{1,0:T(4,128)}, u32[]{:S(2)}) copy-start(s32[4,256]{1,0:T(4,128)} %get-tuple-element.92.pos_hbm_ref) | copy-start | bytes 12292 | tf_op jit(solution)/shard_map/cond
  44.9 2.3 %collective-permute-start.5 = (f32[256,128]{1,0:T(8,128)S(1)}, f32[256,128]{1,0:T(8,128)S(1)}, u32[]{:S(2)}, u32[]{:S(2)}) collective-permute-start(f32[256,128]{1,0:T(8,128)S(1)} %branch_1_fun.14), channel_id=1, source_target_pairs={{0,1},{1,0},{2,3},{3,2},{4,5},{5,4},{6,7},{7,6},{8,9},{9,8},{10,11... | collective-permute-start | bytes 393224 | tf_op jit(solution)/shard_map/cond/branch_1_fun/ppermute | solution.py:592
